TPU v7x, 256 devices: a whole 4x4x8 slice. The times are simulated.
256 devices in a mesh: section: 8 (over x, z_hi), expert: 8 (over y, core), mp: 4 (over z_lo).
Axes of the slice: x: 4, y: 4, z: 8 (z_hi: 2, z_lo: 4; z = z_hi * 4 + z_lo), core: 2. Of those that a mesh axis runs over, the one named last changes fastest.
Arguments:
- tokens_in: bfloat16 [8, 1024, 4096], P('section', 'expert', 'mp'), may hold values from -6 to 6
- route_ids: int32 [8, 1024, 2], P('section', 'expert'), may hold values from 0 to 7, all different within a row; in each aligned block of 128 rows (0 to 127, 128 to 255, ..., all dimensions but the last counted through in order) at most 64 rows name the same one
- route_weights: float32 [8, 1024, 2], P('section', 'expert'), may hold values from 0.25 to 1
- stash: bfloat16 [8, 2, 1024, 4096], P('section', None, 'expert', 'mp'), may hold values from -6 to 6
- returned_batch_index: int32 [8, 8], P('section', 'expert'), may hold values from 0 to 1
- back_ids: int32 [8, 1024, 2], P('section', 'expert'), may hold values from 0 to 7, all different within a row; in each aligned block of 128 rows (0 to 127, 128 to 255, ..., all dimensions but the last counted through in order) at most 64 rows name the same one
- back_weights: float32 [8, 1024, 2], P('section', 'expert'), may hold values from 0.25 to 1
- upstream: bfloat16 [8, 1024, 4096], P('section', 'expert', 'mp'), may hold values from -1.5 to 1.5
- window_expert: int32 [8], P('section'), may hold values from 0 to 7
- w_gate: bfloat16 [8, 7168, 4096], P('section', ('expert', 'mp')), may hold values from -0.09375 to 0.09375
- w_up: bfloat16 [8, 7168, 4096], P('section', ('expert', 'mp')), may hold values from -0.09375 to 0.09375
- w_down: bfloat16 [8, 7168, 4096], P('section', ('expert', 'mp')), may hold values from -0.0625 to 0.0625
Outputs:
- expert_out: bfloat16 [8, 1024, 4096], P('section', 'expert', 'mp')
- input_grad: bfloat16 [8, 1024, 4096], P('section', 'expert', 'mp')
- grad_gate: bfloat16 [8, 7168, 4096], P('section', ('expert', 'mp'))
- grad_up: bfloat16 [8, 7168, 4096], P('section', ('expert', 'mp'))
- grad_down: bfloat16 [8, 7168, 4096], P('section', ('expert', 'mp'))
Inputs may be any that keep to these rules, and one draw needn't show every extreme that they name: `route_ids`: each token names two different experts; among the 128 tokens of one group no expert is named by more than 64 tokens, a bound that some block reaches. `back_ids`: as route_ids.
All inputs are finite; a program needn't handle non-finite values.
Results may differ from a plain program's by a relative error of at most 0.0058.
Values may be sent and summed in bfloat16 or wider, within the bound.
No kernel may reach another device: no remote copies, remote signals or barrier semaphores. Data moves between devices by JAX's collectives and lax.ppermute only.
A program may use at most 128 MiB of HBM per device.

v0:
```python
import jax
import jax.numpy as jnp
from jax import lax
from jax.experimental import pallas as pl
from jax.experimental.pallas import tpu as pltpu
from jax.sharding import PartitionSpec as P

CAP = 64


def together(*arrays):
    return lax.optimization_barrier(arrays)


def along_y(array, step):
    n = lax.axis_size("expert")
    return lax.ppermute(array, "expert", [(i, (i + 2 * step) % n) for i in range(n)])


def other_core(array):
    n = lax.axis_size("expert")
    return lax.ppermute(array, "expert", [(i, i ^ 1) for i in range(n)])


def along_mp(array, flip):
    n = lax.axis_size("mp")
    return lax.ppermute(array, "mp", [(i, i ^ flip) for i in range(n)])


def mirrored(array):
    n = lax.axis_size("section")
    return lax.ppermute(array, "section", [(i, n - 1 - i) for i in range(n)])


def routing(pair_ids, pair_weights, expert):
    matches = pair_ids == expert
    routed = jnp.any(matches, axis=1)
    counted = routed.astype(jnp.int32)
    slot_of = jnp.cumsum(counted) - counted
    gate_share = jnp.sum(jnp.where(matches, pair_weights, 0.0), axis=1)
    return (gate_share, jnp.where(routed, slot_of, CAP))


def picker_of(slot_or_cap):
    places = jnp.arange(CAP, dtype=jnp.int32)[:, None]
    return slot_or_cap[None, :] == places


def pack(picker, values):
    return jnp.dot(
        picker.astype(jnp.bfloat16), values, preferred_element_type=jnp.float32
    ).astype(jnp.bfloat16)


def unpack(picker, rows):
    return lax.dot_general(
        picker.astype(jnp.bfloat16),
        rows,
        (((0,), (0,)), ((), ())),
        preferred_element_type=jnp.float32,
    ).astype(jnp.bfloat16)


def swapped(flag, first, second):
    return (jnp.where(flag, second, first), jnp.where(flag, first, second))


def beside(flag, here, there):
    first, second = swapped(flag, here, there)
    return jnp.concatenate([first, second], axis=1)


def widen(block, others, place):
    one, two, three = others
    odd, high = (place & 1) == 1, (place & 2) == 2
    return beside(high, beside(odd, block, one), beside(odd, two, three))


def ask_mp(block):
    return tuple(along_mp(block, flip) for flip in (1, 2, 3))


def both_ways(to_ahead, to_behind):
    return (along_y(to_ahead, 1), along_y(to_behind, -1))


def stacked(*arrays):
    return jnp.concatenate(arrays, axis=0)


def fetch(sources, target, sems, first):
    copies = []
    into = 0
    for index, (ref, start, rows) in enumerate(sources):
        copies.append(
            pltpu.make_async_copy(
                ref.at[pl.ds(start, rows)],
                target.at[pl.ds(into, rows)],
                sems.at[first + index],
            )
        )
        into += rows
    for copy in copies:
        copy.start()
    return copies


def whole(*refs):
    return tuple((ref, 0, ref.shape[0]) for ref in refs)


def arrive(copies):
    for copy in copies:
        copy.wait()


def times_rows(weight, rows):
    return lax.dot_general(
        weight, rows, (((1,), (1,)), ((), ())), preferred_element_type=jnp.float32
    )


def spread_kernel_part(pairs, own_ref, far_refs):
    width = own_ref.shape[1]
    step = min(width, 1024)
    for left in range(0, width, step):
        columns = slice(left, left + step)
        term = 0.0
        for hidden, weight in pairs:
            term = term + lax.dot_general(
                hidden,
                weight[:, columns],
                (((0,), (0,)), ((), ())),
                preferred_element_type=jnp.float32,
            )
        own_ref[:, columns] = term[:CAP]
        for index, ref in enumerate(far_refs):
            ref[:, columns] = term[CAP * (index + 1) : CAP * (index + 2)].astype(jnp.bfloat16)


def fwd_kernel(*refs):
    wide, behind, ahead, low, high = refs[:5]
    gate_own, up_own, down_own, gate_x, up_x, down_x = refs[5:11]
    own_ref, behind_ref, ahead_ref, far_ref = refs[11:15]
    rows, gate, up, down, sems = refs[15:]
    half = CAP // 2
    rows_in = fetch(whole(wide, behind, ahead) + ((low, 0, half), (high, 0, half)), rows, sems, 0)
    gate_in = fetch(whole(gate_own, gate_x), gate, sems, 5)
    up_in = fetch(whole(up_own, up_x), up, sems, 7)
    down_in = fetch(whole(down_own, down_x), down, sems, 9)
    arrive(rows_in)
    arrive(gate_in)
    pre = times_rows(gate[...], rows[...])
    arrive(up_in)
    hidden = (pre * jax.nn.sigmoid(pre) * times_rows(up[...], rows[...])).astype(jnp.bfloat16)
    arrive(down_in)
    spread_kernel_part(((hidden, down),), own_ref, (behind_ref, ahead_ref, far_ref))


def later_rows(refs):
    wide, behind, ahead, low, high = refs
    half = CAP // 2
    return whole(wide) + (
        (behind, half, CAP),
        (ahead, half, CAP),
        (low, 0, half),
        (high, 0, half),
    )


def grad_kernel(*refs):
    down_own, down_x, hidden_ref, rows_out, rows, down, sems = refs[5:]
    rows_in = fetch(later_rows(refs[:5]), rows, sems, 0)
    down_in = fetch(whole(down_own, down_x), down, sems, 5)
    arrive(rows_in)
    keep = pltpu.make_async_copy(rows, rows_out, sems.at[7])
    keep.start()
    arrive(down_in)
    hidden_ref[...] = times_rows(down[...], rows[...])
    keep.wait()


def back_kernel(*refs):
    hidden_grad_ref, gate_own, up_own, gate_x, up_x = refs[5:10]
    own_ref, behind_ref, ahead_ref, far_ref, keep_ref, send_ref, rows_out = refs[10:17]
    rows, gate, up, sems = refs[17:]
    units = gate_own.shape[0]
    rows_in = fetch(later_rows(refs[:5]), rows, sems, 0)
    gate_in = fetch(whole(gate_own, gate_x), gate, sems, 5)
    up_in = fetch(whole(up_own, up_x), up, sems, 7)
    arrive(rows_in)
    rows_back = pltpu.make_async_copy(rows, rows_out, sems.at[9])
    rows_back.start()
    arrive(gate_in)
    pre_gate = times_rows(gate[...], rows[...])
    arrive(up_in)
    pre_up = times_rows(up[...], rows[...])
    sigmoid_pre = jax.nn.sigmoid(pre_gate)
    activated = pre_gate * sigmoid_pre
    hidden_grad = hidden_grad_ref[...]
    hidden = (activated * pre_up).astype(jnp.bfloat16)
    gate_grad = (
        hidden_grad * pre_up * sigmoid_pre * (1.0 + pre_gate * (1.0 - sigmoid_pre))
    ).astype(jnp.bfloat16)
    up_grad = (hidden_grad * activated).astype(jnp.bfloat16)
    for index, array in enumerate((hidden, gate_grad, up_grad)):
        keep_ref[units * index : units * (index + 1)] = array[:units]
        send_ref[units * index : units * (index + 1)] = array[units:]
    spread_kernel_part(
        ((gate_grad, gate), (up_grad, up)), own_ref, (behind_ref, ahead_ref, far_ref)
    )
    rows_back.wait()


def weight_kernel(hidden_ref, hidden_x_ref, grad_ref, grad_x_ref, back_ref, back_x_ref, *outs):
    units = outs[0].shape[0]
    for index, out in enumerate(outs):
        part = slice(units * index, units * (index + 1))
        rows, rows_x = (grad_ref, grad_x_ref) if index == 0 else (back_ref, back_x_ref)
        total = jnp.dot(hidden_ref[part], rows[...], preferred_element_type=jnp.float32)
        total = total + jnp.dot(
            hidden_x_ref[part], rows_x[...], preferred_element_type=jnp.float32
        )
        out[...] = total.astype(jnp.bfloat16)


HBM = pl.BlockSpec(memory_space=pltpu.HBM)
VMEM = pl.BlockSpec(memory_space=pltpu.VMEM)
LIMIT = 56 * 2**20
PARAMS = pltpu.CompilerParams(vmem_limit_bytes=LIMIT)
SMALL = pl.CostEstimate(flops=1, bytes_accessed=1, transcendentals=0)


def block_shapes(width):
    narrow = jax.ShapeDtypeStruct((CAP, width), jnp.bfloat16)
    return (jax.ShapeDtypeStruct((CAP, width), jnp.float32), narrow, narrow, narrow)


def rows_shape(width):
    return jax.ShapeDtypeStruct((4 * CAP, width), jnp.bfloat16)


def scratch(units, width, weights, sems):
    return (
        [pltpu.VMEM((4 * CAP, width), jnp.bfloat16)]
        + [pltpu.VMEM((2 * units, width), jnp.bfloat16)] * weights
        + [pltpu.SemaphoreType.DMA((sems,))]
    )


def run_fwd(pieces, weights):
    units, width = weights[0].shape
    return pl.pallas_call(
        fwd_kernel,
        out_shape=block_shapes(width),
        in_specs=[HBM] * 11,
        out_specs=(VMEM,) * 4,
        scratch_shapes=scratch(units, width, 3, 11),
        compiler_params=PARAMS,
        cost_estimate=SMALL,
    )(*pieces, *weights)


def run_grad(pieces, weights):
    units, width = weights[0].shape
    return pl.pallas_call(
        grad_kernel,
        out_shape=(
            jax.ShapeDtypeStruct((2 * units, 4 * CAP), jnp.float32),
            rows_shape(width),
        ),
        in_specs=[HBM] * 7,
        out_specs=(VMEM, HBM),
        scratch_shapes=scratch(units, width, 1, 8),
        compiler_params=PARAMS,
        cost_estimate=SMALL,
    )(*pieces, *weights)


def run_back(pieces, hidden_grad, weights):
    units, width = weights[0].shape
    hidden = jax.ShapeDtypeStruct((3 * units, 4 * CAP), jnp.bfloat16)
    return pl.pallas_call(
        back_kernel,
        out_shape=block_shapes(width) + (hidden, hidden, rows_shape(width)),
        in_specs=[HBM] * 5 + [VMEM] + [HBM] * 4,
        out_specs=(VMEM,) * 6 + (HBM,),
        scratch_shapes=scratch(units, width, 2, 10),
        compiler_params=PARAMS,
        cost_estimate=SMALL,
    )(*pieces, hidden_grad, *weights)


def run_weights(hidden, hidden_x, grad_rows, grad_rows_x, back_rows, back_rows_x):
    units, width = hidden.shape[0] // 3, grad_rows.shape[1]
    step = min(width, 512)
    held = pl.BlockSpec(hidden.shape, lambda i: (0, 0))
    rows = pl.BlockSpec((grad_rows.shape[0], step), lambda i: (0, i))
    return pl.pallas_call(
        weight_kernel,
        grid=(width // step,),
        out_shape=(jax.ShapeDtypeStruct((units, width), jnp.bfloat16),) * 3,
        in_specs=[held] * 2 + [rows] * 4,
        out_specs=(pl.BlockSpec((units, step), lambda i: (0, i)),) * 3,
        compiler_params=PARAMS,
        cost_estimate=SMALL,
    )(hidden, hidden_x, grad_rows, grad_rows_x, back_rows, back_rows_x)


def add_parts(own, parts):
    total = own
    for part in parts:
        total = total + part.astype(jnp.float32)
    return total


def near_with_far(behind, ahead, from_behind, from_ahead):
    half = from_behind.shape[0]

    def plus(block, start, extra):
        padded = jnp.pad(extra, ((start, block.shape[0] - half - start), (0, 0)))
        return (block.astype(jnp.float32) + padded.astype(jnp.float32)).astype(jnp.bfloat16)

    return both_ways(plus(ahead, 0, from_behind), plus(behind, half, from_ahead))


def split_mp(total, place):
    width = total.shape[1] // 4

    def columns(array, index):
        return lax.dynamic_slice_in_dim(array, index * width, width, axis=1)

    low = total.astype(jnp.bfloat16)
    return (columns(total, place),) + tuple(columns(low, place ^ flip) for flip in (1, 2, 3))


def send_mp(blocks):
    return tuple(along_mp(block, flip) for flip, block in zip((1, 2, 3), blocks))


def per_device(
    tokens_in,
    route_ids,
    route_weights,
    stash,
    returned_batch_index,
    back_ids,
    back_weights,
    upstream,
    window_expert,
    w_gate,
    w_up,
    w_down,
):
    expert = window_expert[0]
    place = lax.axis_index("mp")
    half = CAP // 2
    gate_w, up_w, down_w = (w_gate[0], w_up[0], w_down[0])

    fwd_gate, fwd_slot = routing(route_ids[0], route_weights[0], expert)
    fwd_pick = picker_of(fwd_slot)
    back_gate, back_slot = routing(back_ids[0], back_weights[0], expert)
    back_pick = picker_of(back_slot)
    grad_tokens = (back_gate[:, None] * upstream[0].astype(jnp.float32)).astype(jnp.bfloat16)
    bufs = stacked(pack(fwd_pick, tokens_in[0]), pack(back_pick, grad_tokens))
    held_rows = lax.dynamic_index_in_dim(
        stash[0], returned_batch_index[0, 0], axis=0, keepdims=False
    )
    bufs, back_slot, gate_w, up_w, down_w, held_rows = together(
        bufs, back_slot, gate_w, up_w, down_w, held_rows
    )
    one, two, three, held_slot, gate_x, up_w, down_w, held_rows = together(
        *ask_mp(bufs), mirrored(back_slot), other_core(gate_w), up_w, down_w, held_rows
    )

    wide = widen(bufs, (one, two, three), place)
    fwd_wide, grad_wide = wide[:CAP], wide[CAP:]
    fwd_behind, fwd_ahead, back_buf, up_x, down_x, grad_wide = together(
        *both_ways(fwd_wide, fwd_wide),
        mirrored(pack(picker_of(held_slot), held_rows)),
        other_core(up_w),
        other_core(down_w),
        grad_wide,
    )

    cw, ccw, one, two, three = together(
        *both_ways(stacked(fwd_behind[:half], grad_wide), stacked(fwd_ahead[half:], grad_wide)),
        *ask_mp(back_buf),
    )

    fwd_terms = run_fwd(
        (fwd_wide, fwd_behind, fwd_ahead, cw, ccw), (gate_w, up_w, down_w, gate_x, up_x, down_x)
    )
    grad_pieces = (grad_wide, cw, ccw)
    back_wide = widen(back_buf, (one, two, three), place)
    cw, ccw, *fwd_terms = together(
        *both_ways(stacked(cw[half:CAP], back_wide), stacked(ccw[CAP:], back_wide)), *fwd_terms
    )
    fwd_own, fwd_to_behind, fwd_to_ahead, fwd_to_far = fwd_terms

    hidden_grad, grad_rows = run_grad((*grad_pieces, cw, ccw), (down_w, down_x))
    back_pieces = (back_wide, cw, ccw)
    cw, ccw, hidden_grad, grad_rows = together(
        *both_ways(
            stacked(cw[half:CAP], fwd_to_far[:half]), stacked(ccw[CAP:], fwd_to_far[half:])
        ),
        hidden_grad,
        grad_rows,
    )

    back_terms = run_back((*back_pieces, cw, ccw), hidden_grad, (gate_w, up_w, gate_x, up_x))
    p0, p1, grad_rows_x, *back_terms = together(
        *near_with_far(fwd_to_behind, fwd_to_ahead, cw[half:], ccw[half:]),
        other_core(grad_rows),
        *back_terms,
    )
    back_own, back_to_behind, back_to_ahead, back_to_far = back_terms[:4]
    hidden_keep, hidden_send, back_rows = back_terms[4:]

    fwd_total = add_parts(fwd_own, (p0, p1))
    f0, f1, hidden_x, back_rows_x, *fwd_blocks = together(
        *both_ways(back_to_far[:half], back_to_far[half:]),
        other_core(hidden_send),
        other_core(back_rows),
        *split_mp(fwd_total, place),
    )

    p0, p1, one, two, three, *grads = together(
        *near_with_far(back_to_behind, back_to_ahead, f0, f1),
        *send_mp(fwd_blocks[1:]),
        *run_weights(hidden_keep, hidden_x, grad_rows, grad_rows_x, back_rows, back_rows_x),
    )
    grad_down, grad_gate, grad_up = grads

    back_here, *back_sent = split_mp(add_parts(back_own, (p0, p1)), place)
    back_sent = send_mp(back_sent)
    fwd_sum = add_parts(fwd_blocks[0], (one, two, three))
    fwd_row_gate = jnp.sum(jnp.where(fwd_pick, fwd_gate[None, :], 0.0), axis=1)
    expert_out = unpack(fwd_pick, (fwd_sum * fwd_row_gate[:, None]).astype(jnp.bfloat16))
    input_grad = unpack(back_pick, add_parts(back_here, back_sent).astype(jnp.bfloat16))
    return (
        expert_out[None],
        input_grad[None],
        grad_gate[None],
        grad_up[None],
        grad_down[None],
    )


def solution(mesh):
    placed = (
        P("section", "expert", "mp"),
        P("section", "expert", None),
        P("section", "expert", None),
        P("section", None, "expert", "mp"),
        P("section", "expert"),
        P("section", "expert", None),
        P("section", "expert", None),
        P("section", "expert", "mp"),
        P("section"),
        P("section", ("expert", "mp"), None),
        P("section", ("expert", "mp"), None),
        P("section", ("expert", "mp"), None),
    )
    return jax.shard_map(
        per_device,
        mesh=mesh,
        in_specs=placed,
        out_specs=(
            P("section", "expert", "mp"),
            P("section", "expert", "mp"),
            P("section", ("expert", "mp"), None),
            P("section", ("expert", "mp"), None),
            P("section", ("expert", "mp"), None),
        ),
        check_vma=False,
    )
```

profile of v0, /device:TPU:32, one launch (start us, length us, event | category | flops | bytes accessed | tf_op | source)
XLA Modules:
  0.0 172.7 jit_solution(4697346563841539821)
XLA Ops:
  2.1 0.7 fusion.17
  4.4 1.1 convolution_convert_fusion.4
  5.5 1.2 convolution_convert_fusion.3
  6.9 2.0 %collective-permute-start.2 = (bf16[128,1024]{1,0:T(8,128)(2,1)S(1)}, bf16[128,1024]{1,0:T(8,128)(2,1)S(1)}, u32[]{:S(2)}, u32[]{:S(2)}) collective-permute-start(bf16[128,1024]{1,0:T(8,128)(2,1)S(1)} %pad_maximum_fusion.11), channel_id=1, source_target_pairs={{0,3},{1,2},{2,1},{3,0},{4,7},{5,6},{6,5},{7,4},{8,11},{9,10},{10,... | collective-permute-start | bytes 786440 | tf_op jit(solution)/shard_map/ppermute | solution.py:27
  8.9 2.3 %collective-permute-start.1 = (bf16[128,1024]{1,0:T(8,128)(2,1)S(1)}, bf16[128,1024]{1,0:T(8,128)(2,1)S(1)}, u32[]{:S(2)}, u32[]{:S(2)}) collective-permute-start(bf16[128,1024]{1,0:T(8,128)(2,1)S(1)} %pad_maximum_fusion.11), channel_id=1, source_target_pairs={{0,2},{1,3},{2,0},{3,1},{4,6},{5,7},{6,4},{7,5},{8,10},{9,11},{10,... | collective-permute-start | bytes 786440 | tf_op jit(solution)/shard_map/ppermute | solution.py:27
  11.7 7.2 %collective-permute-start.3 = (s32[128]{0:T(128)S(1)}, s32[128]{0:T(128)S(1)}, u32[]{:S(2)}, u32[]{:S(2)}) collective-permute-start(s32[128]{0:T(128)S(1)} %fusion.15), channel_id=1, source_target_pairs={{0,224},{32,192},{64,160},{96,128},{128,96},{160,64},{192,32},{224... | collective-permute-start | bytes 1544 | tf_op jit(solution)/shard_map/ppermute | solution.py:32
  18.9 11.6 %collective-permute-done.3 = s32[128]{0:T(128)S(1)} collective-permute-done((s32[128]{0:T(128)S(1)}, s32[128]{0:T(128)S(1)}, u32[]{:S(2)}, u32[]{:S(2)}) %collective-permute-start.3) | collective-permute-done | bytes 544 | tf_op jit(solution)/shard_map/ppermute | solution.py:32
  30.6 1.3 collective-permute-done.1
  33.2 1.0 broadcast_select_fusion.5
  34.6 3.1 %collective-permute-start.6 = (bf16[64,4096]{1,0:T(8,128)(2,1)S(1)}, bf16[64,4096]{1,0:T(8,128)(2,1)S(1)}, u32[]{:S(2)}, u32[]{:S(2)}) collective-permute-start(bf16[64,4096]{1,0:T(8,128)(2,1)S(1)} %get-tuple-element.164.refs_0_), channel_id=1, source_target_pairs={{0,24},{4,28},{8,0},{12,4},{16,8},{20,12},{24,16},{28,20},{1,25},{... | collective-permute-start | bytes 1572872 | tf_op jit(solution)/shard_map/ppermute | solution.py:17
  37.9 7.7 %collective-permute-start.7 = (bf16[64,1024]{1,0:T(8,128)(2,1)S(1)}, bf16[64,1024]{1,0:T(8,128)(2,1)S(1)}, u32[]{:S(2)}, u32[]{:S(2)}) collective-permute-start(bf16[64,1024]{1,0:T(8,128)(2,1)S(1)} %convolution_convert_fusion.2), channel_id=1, source_target_pairs={{0,224},{32,192},{64,160},{96,128},{128,96},{160,64},{192,32},{224... | collective-permute-start | bytes 393224 | tf_op jit(solution)/shard_map/ppermute | solution.py:32
  45.5 3.4 %collective-permute-done.7 = bf16[64,1024]{1,0:T(8,128)(2,1)S(1)} collective-permute-done((bf16[64,1024]{1,0:T(8,128)(2,1)S(1)}, bf16[64,1024]{1,0:T(8,128)(2,1)S(1)}, u32[]{:S(2)}, u32[]{:S(2)}) %collective-permute-start.7) | collective-permute-done | bytes 131104 | tf_op jit(solution)/shard_map/ppermute | solution.py:32
  49.0 3.1 %collective-permute-done.5.refs_1_ = bf16[64,4096]{1,0:T(8,128)(2,1)S(1)} collective-permute-done((bf16[64,4096]{1,0:T(8,128)(2,1)S(1)}, bf16[64,4096]{1,0:T(8,128)(2,1)S(1)}, u32[]{:S(2)}, u32[]{:S(2)}) %collective-permute-start.5) | collective-permute-done | bytes 524320 | tf_op jit(solution)/shard_map/ppermute | solution.py:17
  52.9 0.8 collective-permute-start.11
  53.7 1.2 collective-permute-start.10
  55.3 6.7 %collective-permute-start.13 = (bf16[64,1024]{1,0:T(8,128)(2,1)S(1)}, bf16[64,1024]{1,0:T(8,128)(2,1)S(1)}, u32[]{:S(2)}, u32[]{:S(2)}) collective-permute-start(bf16[64,1024]{1,0:T(8,128)(2,1)S(1)} %collective-permute-done.7), channel_id=1, source_target_pairs={{0,2},{1,3},{2,0},{3,1},{4,6},{5,7},{6,4},{7,5},{8,10},{9,11},{10,... | collective-permute-start | bytes 393224 | tf_op jit(solution)/shard_map/ppermute | solution.py:27
  62.1 6.5 %collective-permute-done.13 = bf16[64,1024]{1,0:T(8,128)(2,1)S(1)} collective-permute-done((bf16[64,1024]{1,0:T(8,128)(2,1)S(1)}, bf16[64,1024]{1,0:T(8,128)(2,1)S(1)}, u32[]{:S(2)}, u32[]{:S(2)}) %collective-permute-start.13) | collective-permute-done | bytes 131104 | tf_op jit(solution)/shard_map/ppermute | solution.py:27
  68.5 1.0 collective-permute-done.12
  69.5 1.2 collective-permute-done.11.refs_4_.refs_2_
  70.8 1.7 collective-permute-done.10.refs_3_.refs_1_
  73.9 1.5 collective-permute-start.15
  75.4 9.7 %shard_map.155 = (f32[64,4096]{1,0:T(8,128)}, bf16[64,4096]{1,0:T(8,128)(2,1)}, bf16[64,4096]{1,0:T(8,128)(2,1)}, bf16[64,4096]{1,0:T(8,128)(2,1)}) custom-call(bf16[64,4096]{1,0:T(8,128)(2,1)} %copy-done.8, bf16[64,4096]{1,0:T(8,128)(2,1)} %copy-done.11, bf16[64,4096]{1,0:T(8,128)(2,1)} %copy-done.10, bf16[96,4096]{1,0:T(8,128)(2,1)} %copy-done.5, ...), custom_call_target="tpu_custom_call" | custom-call | flops 1 | bytes 1 | tf_op jit(solution)/shard_map/pallas_call | solution.py:253
  85.0 4.9 %collective-permute-done.16.refs_4_.refs_2_ = bf16[96,4096]{1,0:T(8,128)(2,1)S(1)} collective-permute-done((bf16[96,4096]{1,0:T(8,128)(2,1)S(1)}, bf16[96,4096]{1,0:T(8,128)(2,1)S(1)}, u32[]{:S(2)}, u32[]{:S(2)}) %collective-permute-start.16) | collective-permute-done | bytes 786464 | tf_op jit(solution)/shard_map/ppermute | solution.py:17
  90.0 3.0 %collective-permute-done.15.refs_3_.refs_1_ = bf16[96,4096]{1,0:T(8,128)(2,1)S(1)} collective-permute-done((bf16[96,4096]{1,0:T(8,128)(2,1)S(1)}, bf16[96,4096]{1,0:T(8,128)(2,1)S(1)}, u32[]{:S(2)}, u32[]{:S(2)}) %collective-permute-start.15) | collective-permute-done | bytes 786464 | tf_op jit(solution)/shard_map/ppermute | solution.py:17
  93.1 1.3 fusion.22
  94.6 3.3 %collective-permute-start.18 = (bf16[64,4096]{1,0:T(8,128)(2,1)S(1)}, bf16[64,4096]{1,0:T(8,128)(2,1)S(1)}, u32[]{:S(2)}, u32[]{:S(2)}) collective-permute-start(bf16[64,4096]{1,0:T(8,128)(2,1)S(1)} %pad_maximum_fusion.10), channel_id=1, source_target_pairs={{0,24},{4,28},{8,0},{12,4},{16,8},{20,12},{24,16},{28,20},{1,25},{... | collective-permute-start | bytes 1572872 | tf_op jit(solution)/shard_map/ppermute | solution.py:17
  97.9 5.2 %shard_map.156 = (f32[448,256]{1,0:T(8,128)}, bf16[256,4096]{1,0:T(8,128)(2,1)}) custom-call(bf16[64,4096]{1,0:T(8,128)(2,1)} %copy-done.3, bf16[96,4096]{1,0:T(8,128)(2,1)} %copy-done.5, bf16[96,4096]{1,0:T(8,128)(2,1)} %copy-done.4, bf16[96,4096]{1,0:T(8,128)(2,1)} %copy-done.7, bf16[96,4096]{1,0:T(8,128)(2,1)} %copy-done.6, bf16[224,4096]{1,0:T(8,128)(2,1)} %bitcast.35, ...), custom_call_target="tpu_custom_call" | custom-call | flops 1 | bytes 1 | tf_op jit(solution)/shard_map/pallas_call | solution.py:266
  103.1 4.0 %collective-permute-done.17.refs_3_ = bf16[64,4096]{1,0:T(8,128)(2,1)S(1)} collective-permute-done((bf16[64,4096]{1,0:T(8,128)(2,1)S(1)}, bf16[64,4096]{1,0:T(8,128)(2,1)S(1)}, u32[]{:S(2)}, u32[]{:S(2)}) %collective-permute-start.17) | collective-permute-done | bytes 524320 | tf_op jit(solution)/shard_map/ppermute | solution.py:17
  107.5 0.9 add_convert_fusion.2
  108.3 3.2 %collective-permute-start.20 = (bf16[64,4096]{1,0:T(8,128)(2,1)}, bf16[64,4096]{1,0:T(8,128)(2,1)S(1)}, u32[]{:S(2)}, u32[]{:S(2)}) collective-permute-start(bf16[64,4096]{1,0:T(8,128)(2,1)} %add_convert_fusion.2), channel_id=1, source_target_pairs={{0,24},{4,28},{8,0},{12,4},{16,8},{20,12},{24,16},{28,20},{1,25},{... | collective-permute-start | bytes 1572872 | tf_op jit(solution)/shard_map/ppermute | solution.py:17
  111.6 0.9 pad_maximum_fusion.8.refs_0_
  112.4 12.5 %shard_map.157 = (f32[64,4096]{1,0:T(8,128)}, bf16[64,4096]{1,0:T(8,128)(2,1)}, bf16[64,4096]{1,0:T(8,128)(2,1)}, bf16[64,4096]{1,0:T(8,128)(2,1)}, bf16[672,256...) custom-call(bf16[64,4096]{1,0:T(8,128)(2,1)} %pad_maximum_fusion.8.refs_0_, ...), custom_call_target="tpu_custom_call" | custom-call | flops 1 | bytes 1 | tf_op jit(solution)/shard_map/pallas_call | solution.py:283
  125.3 1.1 fusion.21
  126.4 1.9 %collective-permute-start.23 = (bf16[32,4096]{1,0:T(8,128)(2,1)S(1)}, bf16[32,4096]{1,0:T(8,128)(2,1)S(1)}, u32[]{:S(2)}, u32[]{:S(2)}) collective-permute-start(bf16[32,4096]{1,0:T(8,128)(2,1)S(1)} %get-tuple-element.173), channel_id=1, source_target_pairs={{0,24},{4,28},{8,0},{12,4},{16,8},{20,12},{24,16},{28,20},{1,25},{... | collective-permute-start | bytes 786440 | tf_op jit(solution)/shard_map/ppermute | solution.py:17
  128.8 6.3 %collective-permute-done.23 = bf16[32,4096]{1,0:T(8,128)(2,1)S(1)} collective-permute-done((bf16[32,4096]{1,0:T(8,128)(2,1)S(1)}, bf16[32,4096]{1,0:T(8,128)(2,1)S(1)}, u32[]{:S(2)}, u32[]{:S(2)}) %collective-permute-start.23) | collective-permute-done | bytes 262176 | tf_op jit(solution)/shard_map/ppermute | solution.py:17
  135.1 2.8 %collective-permute-done.22 = bf16[32,4096]{1,0:T(8,128)(2,1)S(1)} collective-permute-done((bf16[32,4096]{1,0:T(8,128)(2,1)S(1)}, bf16[32,4096]{1,0:T(8,128)(2,1)S(1)}, u32[]{:S(2)}, u32[]{:S(2)}) %collective-permute-start.22) | collective-permute-done | bytes 262176 | tf_op jit(solution)/shard_map/ppermute | solution.py:17
  138.2 3.3 %collective-permute-start.27 = (bf16[64,4096]{1,0:T(8,128)(2,1)S(1)}, bf16[64,4096]{1,0:T(8,128)(2,1)S(1)}, u32[]{:S(2)}, u32[]{:S(2)}) collective-permute-start(bf16[64,4096]{1,0:T(8,128)(2,1)S(1)} %add_convert_fusion), channel_id=1, source_target_pairs={{0,24},{4,28},{8,0},{12,4},{16,8},{20,12},{24,16},{28,20},{1,25},{... | collective-permute-start | bytes 1572872 | tf_op jit(solution)/shard_map/ppermute | solution.py:17
  141.5 4.8 %collective-permute-start.28 = (bf16[64,1024]{1,0:T(8,128)(2,1)S(1)}, bf16[64,1024]{1,0:T(8,128)(2,1)S(1)}, u32[]{:S(2)}, u32[]{:S(2)}) collective-permute-start(bf16[64,1024]{1,0:T(8,128)(2,1)S(1)} %get-tuple-element.140), channel_id=1, source_target_pairs={{0,1},{1,0},{2,3},{3,2},{4,5},{5,4},{6,7},{7,6},{8,9},{9,8},{10,11... | collective-permute-start | bytes 393224 | tf_op jit(solution)/shard_map/ppermute | solution.py:27
  146.3 1.5 collective-permute-start.29
  148.5 9.4 %shard_map.158 = (bf16[224,4096]{1,0:T(8,128)(2,1)}, bf16[224,4096]{1,0:T(8,128)(2,1)}, bf16[224,4096]{1,0:T(8,128)(2,1)}) custom-call(bf16[672,256]{1,0:T(8,128)(2,1)} %get-tuple-element.143.hidden_ref, bf16[672,256]{1,0:T(8,128)(2,1)} %copy-done.20, bf16[256,4096]{1,0:T(8,128)(2,1)} %get-tuple-element.120.grad_ref, ...), custom_call_target="tpu_custom_call" | custom-call | flops 1 | bytes 1 | tf_op jit(solution)/shard_map/pallas_call | solution.py:299
  157.9 1.1 collective-permute-done.30
  159.2 1.4 collective-permute-start.31
  160.6 2.0 %collective-permute-start.33 = (bf16[64,1024]{1,0:T(8,128)(2,1)S(1)}, bf16[64,1024]{1,0:T(8,128)(2,1)S(1)}, u32[]{:S(2)}, u32[]{:S(2)}) collective-permute-start(bf16[64,1024]{1,0:T(8,128)(2,1)S(1)} %get-tuple-element.168), channel_id=1, source_target_pairs={{0,3},{1,2},{2,1},{3,0},{4,7},{5,6},{6,5},{7,4},{8,11},{9,10},{10,... | collective-permute-start | bytes 393224 | tf_op jit(solution)/shard_map/ppermute | solution.py:27
  162.7 1.0 collective-permute-start.32
  163.7 1.0 fusion
  164.7 0.9 collective-permute-done.31
  165.6 5.4 %collective-permute-done.33 = bf16[64,1024]{1,0:T(8,128)(2,1)S(1)} collective-permute-done((bf16[64,1024]{1,0:T(8,128)(2,1)S(1)}, bf16[64,1024]{1,0:T(8,128)(2,1)S(1)}, u32[]{:S(2)}, u32[]{:S(2)}) %collective-permute-start.33) | collective-permute-done | bytes 131104 | tf_op jit(solution)/shard_map/ppermute | solution.py:27
  171.7 1.0 fusion.1
  (124 shorter events, 9.7 us)
Async XLA Ops:
  0.6 6.1 %copy-start = (bf16[1,2,128,1024]{3,2,1,0:T(8,128)(2,1)S(1)}, bf16[1,2,128,1024]{3,2,1,0:T(8,128)(2,1)}, u32[]{:S(2)}) copy-start(bf16[1,2,128,1024]{3,2,1,0:T(8,128)(2,1)} %param.15) | copy-start | bytes 1572868
  0.6 31.4 %copy-start.1 = (bf16[1,224,4096]{2,1,0:T(8,128)(2,1)S(1)}, bf16[1,224,4096]{2,1,0:T(8,128)(2,1)}, u32[]{:S(2)}) copy-start(bf16[1,224,4096]{2,1,0:T(8,128)(2,1)} %param.23) | copy-start | bytes 5505028
  6.8 25.1 %collective-permute-start.4 = (bf16[224,4096]{1,0:T(8,128)(2,1)}, bf16[224,4096]{1,0:T(8,128)(2,1)S(1)}, u32[]{:S(2)}, u32[]{:S(2)}) collective-permute-start(bf16[224,4096]{1,0:T(8,128)(2,1)} %bitcast.37), channel_id=1, source_target_pairs={{0,4},{4,0},{8,12},{12,8},{16,20},{20,16},{24,28},{28,24},{1,5},{5... | collective-permute-start | bytes 5505032 | tf_op jit(solution)/shard_map/ppermute | solution.py:22
  6.9 23.7 %collective-permute-start.2 = (bf16[128,1024]{1,0:T(8,128)(2,1)S(1)}, bf16[128,1024]{1,0:T(8,128)(2,1)S(1)}, u32[]{:S(2)}, u32[]{:S(2)}) collective-permute-start(bf16[128,1024]{1,0:T(8,128)(2,1)S(1)} %pad_maximum_fusion.11), channel_id=1, source_target_pairs={{0,3},{1,2},{2,1},{3,0},{4,7},{5,6},{6,5},{7,4},{8,11},{9,10},{10,... | collective-permute-start | bytes 786440 | tf_op jit(solution)/shard_map/ppermute | solution.py:27
  8.9 23.0 %collective-permute-start.1 = (bf16[128,1024]{1,0:T(8,128)(2,1)S(1)}, bf16[128,1024]{1,0:T(8,128)(2,1)S(1)}, u32[]{:S(2)}, u32[]{:S(2)}) collective-permute-start(bf16[128,1024]{1,0:T(8,128)(2,1)S(1)} %pad_maximum_fusion.11), channel_id=1, source_target_pairs={{0,2},{1,3},{2,0},{3,1},{4,6},{5,7},{6,4},{7,5},{8,10},{9,11},{10,... | collective-permute-start | bytes 786440 | tf_op jit(solution)/shard_map/ppermute | solution.py:27
  11.2 20.7 %collective-permute-start = (bf16[128,1024]{1,0:T(8,128)(2,1)S(1)}, bf16[128,1024]{1,0:T(8,128)(2,1)S(1)}, u32[]{:S(2)}, u32[]{:S(2)}) collective-permute-start(bf16[128,1024]{1,0:T(8,128)(2,1)S(1)} %pad_maximum_fusion.11), channel_id=1, source_target_pairs={{0,1},{1,0},{2,3},{3,2},{4,5},{5,4},{6,7},{7,6},{8,9},{9,8},{10,11... | collective-permute-start | bytes 786440 | tf_op jit(solution)/shard_map/ppermute | solution.py:27
  11.7 18.9 %collective-permute-start.3 = (s32[128]{0:T(128)S(1)}, s32[128]{0:T(128)S(1)}, u32[]{:S(2)}, u32[]{:S(2)}) collective-permute-start(s32[128]{0:T(128)S(1)} %fusion.15), channel_id=1, source_target_pairs={{0,224},{32,192},{64,160},{96,128},{128,96},{160,64},{192,32},{224... | collective-permute-start | bytes 1544 | tf_op jit(solution)/shard_map/ppermute | solution.py:32
  31.9 20.1 %collective-permute-start.8 = (bf16[224,4096]{1,0:T(8,128)(2,1)}, bf16[224,4096]{1,0:T(8,128)(2,1)}, u32[]{:S(2)}, u32[]{:S(2)}) collective-permute-start(bf16[224,4096]{1,0:T(8,128)(2,1)} %bitcast.40), channel_id=1, source_target_pairs={{0,4},{4,0},{8,12},{12,8},{16,20},{20,16},{24,28},{28,24},{1,5},{5... | collective-permute-start | bytes 5505032 | tf_op jit(solution)/shard_map/ppermute | solution.py:22
  32.1 20.0 %collective-permute-start.9 = (bf16[224,4096]{1,0:T(8,128)(2,1)S(1)}, bf16[224,4096]{1,0:T(8,128)(2,1)}, u32[]{:S(2)}, u32[]{:S(2)}) collective-permute-start(bf16[224,4096]{1,0:T(8,128)(2,1)S(1)} %bitcast.36), channel_id=1, source_target_pairs={{0,4},{4,0},{8,12},{12,8},{16,20},{20,16},{24,28},{28,24},{1,5},{5... | collective-permute-start | bytes 5505032 | tf_op jit(solution)/shard_map/ppermute | solution.py:22
  34.6 17.8 %copy-start.3 = (bf16[64,4096]{1,0:T(8,128)(2,1)}, bf16[64,4096]{1,0:T(8,128)(2,1)S(1)}, u32[]{:S(2)}) copy-start(bf16[64,4096]{1,0:T(8,128)(2,1)S(1)} %get-tuple-element.96.refs_0_) | copy-start | bytes 1572868
  34.6 17.8 %copy-start.8 = (bf16[64,4096]{1,0:T(8,128)(2,1)}, bf16[64,4096]{1,0:T(8,128)(2,1)S(1)}, u32[]{:S(2)}) copy-start(bf16[64,4096]{1,0:T(8,128)(2,1)S(1)} %get-tuple-element.164.refs_0_) | copy-start | bytes 1572868
  34.6 14.4 %collective-permute-start.6 = (bf16[64,4096]{1,0:T(8,128)(2,1)S(1)}, bf16[64,4096]{1,0:T(8,128)(2,1)S(1)}, u32[]{:S(2)}, u32[]{:S(2)}) collective-permute-start(bf16[64,4096]{1,0:T(8,128)(2,1)S(1)} %get-tuple-element.164.refs_0_), channel_id=1, source_target_pairs={{0,24},{4,28},{8,0},{12,4},{16,8},{20,12},{24,16},{28,20},{1,25},{... | collective-permute-start | bytes 1572872 | tf_op jit(solution)/shard_map/ppermute | solution.py:17
  37.7 14.4 %collective-permute-start.5 = (bf16[64,4096]{1,0:T(8,128)(2,1)S(1)}, bf16[64,4096]{1,0:T(8,128)(2,1)S(1)}, u32[]{:S(2)}, u32[]{:S(2)}) collective-permute-start(bf16[64,4096]{1,0:T(8,128)(2,1)S(1)} %get-tuple-element.164.refs_0_), channel_id=1, source_target_pairs={{0,8},{4,12},{8,16},{12,20},{16,24},{20,28},{24,0},{28,4},{1,9},{5... | collective-permute-start | bytes 1572872 | tf_op jit(solution)/shard_map/ppermute | solution.py:17
  37.9 11.1 %collective-permute-start.7 = (bf16[64,1024]{1,0:T(8,128)(2,1)S(1)}, bf16[64,1024]{1,0:T(8,128)(2,1)S(1)}, u32[]{:S(2)}, u32[]{:S(2)}) collective-permute-start(bf16[64,1024]{1,0:T(8,128)(2,1)S(1)} %convolution_convert_fusion.2), channel_id=1, source_target_pairs={{0,224},{32,192},{64,160},{96,128},{128,96},{160,64},{192,32},{224... | collective-permute-start | bytes 393224 | tf_op jit(solution)/shard_map/ppermute | solution.py:32
  52.9 17.9 %collective-permute-start.11 = (bf16[96,4096]{1,0:T(8,128)(2,1)S(1)}, bf16[96,4096]{1,0:T(8,128)(2,1)S(1)}, u32[]{:S(2)}, u32[]{:S(2)}) collective-permute-start(bf16[96,4096]{1,0:T(8,128)(2,1)S(1)} %get-tuple-element.181), channel_id=1, source_target_pairs={{0,24},{4,28},{8,0},{12,4},{16,8},{20,12},{24,16},{28,20},{1,25},{... | collective-permute-start | bytes 2359304 | tf_op jit(solution)/shard_map/ppermute | solution.py:17
  53.7 18.8 %collective-permute-start.10 = (bf16[96,4096]{1,0:T(8,128)(2,1)S(1)}, bf16[96,4096]{1,0:T(8,128)(2,1)S(1)}, u32[]{:S(2)}, u32[]{:S(2)}) collective-permute-start(bf16[96,4096]{1,0:T(8,128)(2,1)S(1)} %get-tuple-element.182), channel_id=1, source_target_pairs={{0,8},{4,12},{8,16},{12,20},{16,24},{20,28},{24,0},{28,4},{1,9},{5... | collective-permute-start | bytes 2359304 | tf_op jit(solution)/shard_map/ppermute | solution.py:17
  54.9 7.2 %collective-permute-start.14 = (bf16[64,1024]{1,0:T(8,128)(2,1)S(1)}, bf16[64,1024]{1,0:T(8,128)(2,1)S(1)}, u32[]{:S(2)}, u32[]{:S(2)}) collective-permute-start(bf16[64,1024]{1,0:T(8,128)(2,1)S(1)} %collective-permute-done.7), channel_id=1, source_target_pairs={{0,3},{1,2},{2,1},{3,0},{4,7},{5,6},{6,5},{7,4},{8,11},{9,10},{10,... | collective-permute-start | bytes 393224 | tf_op jit(solution)/shard_map/ppermute | solution.py:27
  55.3 13.2 %collective-permute-start.13 = (bf16[64,1024]{1,0:T(8,128)(2,1)S(1)}, bf16[64,1024]{1,0:T(8,128)(2,1)S(1)}, u32[]{:S(2)}, u32[]{:S(2)}) collective-permute-start(bf16[64,1024]{1,0:T(8,128)(2,1)S(1)} %collective-permute-done.7), channel_id=1, source_target_pairs={{0,2},{1,3},{2,0},{3,1},{4,6},{5,7},{6,4},{7,5},{8,10},{9,11},{10,... | collective-permute-start | bytes 393224 | tf_op jit(solution)/shard_map/ppermute | solution.py:27
  62.1 7.5 %collective-permute-start.12 = (bf16[64,1024]{1,0:T(8,128)(2,1)S(1)}, bf16[64,1024]{1,0:T(8,128)(2,1)S(1)}, u32[]{:S(2)}, u32[]{:S(2)}) collective-permute-start(bf16[64,1024]{1,0:T(8,128)(2,1)S(1)} %collective-permute-done.7), channel_id=1, source_target_pairs={{0,1},{1,0},{2,3},{3,2},{4,5},{5,4},{6,7},{7,6},{8,9},{9,8},{10,11... | collective-permute-start | bytes 393224 | tf_op jit(solution)/shard_map/ppermute | solution.py:27
  73.3 16.6 %collective-permute-start.16 = (bf16[96,4096]{1,0:T(8,128)(2,1)S(1)}, bf16[96,4096]{1,0:T(8,128)(2,1)S(1)}, u32[]{:S(2)}, u32[]{:S(2)}) collective-permute-start(bf16[96,4096]{1,0:T(8,128)(2,1)S(1)} %get-tuple-element.177), channel_id=1, source_target_pairs={{0,24},{4,28},{8,0},{12,4},{16,8},{20,12},{24,16},{28,20},{1,25},{... | collective-permute-start | bytes 2359304 | tf_op jit(solution)/shard_map/ppermute | solution.py:17
  73.9 19.1 %collective-permute-start.15 = (bf16[96,4096]{1,0:T(8,128)(2,1)S(1)}, bf16[96,4096]{1,0:T(8,128)(2,1)S(1)}, u32[]{:S(2)}, u32[]{:S(2)}) collective-permute-start(bf16[96,4096]{1,0:T(8,128)(2,1)S(1)} %get-tuple-element.178), channel_id=1, source_target_pairs={{0,8},{4,12},{8,16},{12,20},{16,24},{20,28},{24,0},{28,4},{1,9},{5... | collective-permute-start | bytes 2359304 | tf_op jit(solution)/shard_map/ppermute | solution.py:17
  90.0 4.6 %copy-start.6 = (bf16[96,4096]{1,0:T(8,128)(2,1)}, bf16[96,4096]{1,0:T(8,128)(2,1)S(1)}, u32[]{:S(2)}) copy-start(bf16[96,4096]{1,0:T(8,128)(2,1)S(1)} %collective-permute-done.16.refs_4_.refs_2_) | copy-start | bytes 2359300
  94.4 12.7 %collective-permute-start.17 = (bf16[64,4096]{1,0:T(8,128)(2,1)S(1)}, bf16[64,4096]{1,0:T(8,128)(2,1)S(1)}, u32[]{:S(2)}, u32[]{:S(2)}) collective-permute-start(bf16[64,4096]{1,0:T(8,128)(2,1)S(1)} %pad_maximum_fusion.9), channel_id=1, source_target_pairs={{0,8},{4,12},{8,16},{12,20},{16,24},{20,28},{24,0},{28,4},{1,9},{5... | collective-permute-start | bytes 1572872 | tf_op jit(solution)/shard_map/ppermute | solution.py:17
  94.6 12.7 %copy-start.19 = (bf16[64,4096]{1,0:T(8,128)(2,1)S(1)}, bf16[64,4096]{1,0:T(8,128)(2,1)}, u32[]{:S(2)}) copy-start(bf16[64,4096]{1,0:T(8,128)(2,1)} %get-tuple-element.111) | copy-start | bytes 1572868
  94.6 12.5 %collective-permute-start.18 = (bf16[64,4096]{1,0:T(8,128)(2,1)S(1)}, bf16[64,4096]{1,0:T(8,128)(2,1)S(1)}, u32[]{:S(2)}, u32[]{:S(2)}) collective-permute-start(bf16[64,4096]{1,0:T(8,128)(2,1)S(1)} %pad_maximum_fusion.10), channel_id=1, source_target_pairs={{0,24},{4,28},{8,0},{12,4},{16,8},{20,12},{24,16},{28,20},{1,25},{... | collective-permute-start | bytes 1572872 | tf_op jit(solution)/shard_map/ppermute | solution.py:17
  107.2 17.7 %collective-permute-start.21 = (bf16[256,4096]{1,0:T(8,128)(2,1)}, bf16[256,4096]{1,0:T(8,128)(2,1)}, u32[]{:S(2)}, u32[]{:S(2)}) collective-permute-start(bf16[256,4096]{1,0:T(8,128)(2,1)} %get-tuple-element.120.grad_ref), channel_id=1, source_target_pairs={{0,4},{4,0},{8,12},{12,8},{16,20},{20,16},{24,28},{28,24},{1,5},{5... | collective-permute-start | bytes 6291464 | tf_op jit(solution)/shard_map/ppermute | solution.py:22
  107.4 17.5 %collective-permute-start.19 = (bf16[64,4096]{1,0:T(8,128)(2,1)S(1)}, bf16[64,4096]{1,0:T(8,128)(2,1)S(1)}, u32[]{:S(2)}, u32[]{:S(2)}) collective-permute-start(bf16[64,4096]{1,0:T(8,128)(2,1)S(1)} %add_convert_fusion.3), channel_id=1, source_target_pairs={{0,8},{4,12},{8,16},{12,20},{16,24},{20,28},{24,0},{28,4},{1,9},{5... | collective-permute-start | bytes 1572872 | tf_op jit(solution)/shard_map/ppermute | solution.py:17
  108.3 16.6 %collective-permute-start.20 = (bf16[64,4096]{1,0:T(8,128)(2,1)}, bf16[64,4096]{1,0:T(8,128)(2,1)S(1)}, u32[]{:S(2)}, u32[]{:S(2)}) collective-permute-start(bf16[64,4096]{1,0:T(8,128)(2,1)} %add_convert_fusion.2), channel_id=1, source_target_pairs={{0,24},{4,28},{8,0},{12,4},{16,8},{20,12},{24,16},{28,20},{1,25},{... | collective-permute-start | bytes 1572872 | tf_op jit(solution)/shard_map/ppermute | solution.py:17
  112.4 16.1 %copy-start.14 = (f32[64,4096]{1,0:T(8,128)S(1)}, f32[64,4096]{1,0:T(8,128)}, u32[]{:S(2)}) copy-start(f32[64,4096]{1,0:T(8,128)} %get-tuple-element.132) | copy-start | bytes 3145732
  124.9 13.0 %collective-permute-start.25 = (bf16[256,4096]{1,0:T(8,128)(2,1)}, bf16[256,4096]{1,0:T(8,128)(2,1)S(1)}, u32[]{:S(2)}, u32[]{:S(2)}) collective-permute-start(bf16[256,4096]{1,0:T(8,128)(2,1)} %get-tuple-element.131.back_ref), channel_id=1, source_target_pairs={{0,4},{4,0},{8,12},{12,8},{16,20},{20,16},{24,28},{28,24},{1,5},{5... | collective-permute-start | bytes 6291464 | tf_op jit(solution)/shard_map/ppermute | solution.py:22
  126.4 8.7 %collective-permute-start.23 = (bf16[32,4096]{1,0:T(8,128)(2,1)S(1)}, bf16[32,4096]{1,0:T(8,128)(2,1)S(1)}, u32[]{:S(2)}, u32[]{:S(2)}) collective-permute-start(bf16[32,4096]{1,0:T(8,128)(2,1)S(1)} %get-tuple-element.173), channel_id=1, source_target_pairs={{0,24},{4,28},{8,0},{12,4},{16,8},{20,12},{24,16},{28,20},{1,25},{... | collective-permute-start | bytes 786440 | tf_op jit(solution)/shard_map/ppermute | solution.py:17
  128.3 9.7 %copy-start.17 = (bf16[64,4096]{1,0:T(8,128)(2,1)S(1)}, bf16[64,4096]{1,0:T(8,128)(2,1)}, u32[]{:S(2)}) copy-start(bf16[64,4096]{1,0:T(8,128)(2,1)} %get-tuple-element.136) | copy-start | bytes 1572868
  128.3 9.6 %collective-permute-start.22 = (bf16[32,4096]{1,0:T(8,128)(2,1)S(1)}, bf16[32,4096]{1,0:T(8,128)(2,1)S(1)}, u32[]{:S(2)}, u32[]{:S(2)}) collective-permute-start(bf16[32,4096]{1,0:T(8,128)(2,1)S(1)} %get-tuple-element.174), channel_id=1, source_target_pairs={{0,8},{4,12},{8,16},{12,20},{16,24},{20,28},{24,0},{28,4},{1,9},{5... | collective-permute-start | bytes 786440 | tf_op jit(solution)/shard_map/ppermute | solution.py:17
  128.5 9.5 %collective-permute-start.24 = (bf16[672,256]{1,0:T(8,128)(2,1)}, bf16[672,256]{1,0:T(8,128)(2,1)S(1)}, u32[]{:S(2)}, u32[]{:S(2)}) collective-permute-start(bf16[672,256]{1,0:T(8,128)(2,1)} %get-tuple-element.130), channel_id=1, source_target_pairs={{0,4},{4,0},{8,12},{12,8},{16,20},{20,16},{24,28},{28,24},{1,5},{5... | collective-permute-start | bytes 1032200 | tf_op jit(solution)/shard_map/ppermute | solution.py:22
  128.7 9.5 %copy-start.16 = (bf16[64,4096]{1,0:T(8,128)(2,1)S(1)}, bf16[64,4096]{1,0:T(8,128)(2,1)}, u32[]{:S(2)}) copy-start(bf16[64,4096]{1,0:T(8,128)(2,1)} %get-tuple-element.138) | copy-start | bytes 1572868
  128.8 19.6 %copy-start.22 = (s32[1,128,2]{1,2,0:T(2,128)S(1)}, s32[1,128,2]{1,2,0:T(2,128)}, u32[]{:S(2)}) copy-start(s32[1,128,2]{1,2,0:T(2,128)} %param.13) | copy-start | bytes 3076
  128.8 19.6 %copy-start.23 = (f32[1,128,2]{1,2,0:T(2,128)S(1)}, f32[1,128,2]{1,2,0:T(2,128)}, u32[]{:S(2)}) copy-start(f32[1,128,2]{1,2,0:T(2,128)} %param.14) | copy-start | bytes 3076
  138.0 10.5 %copy-start.20 = (bf16[672,256]{1,0:T(8,128)(2,1)}, bf16[672,256]{1,0:T(8,128)(2,1)S(1)}, u32[]{:S(2)}) copy-start(bf16[672,256]{1,0:T(8,128)(2,1)S(1)} %collective-permute-done.24.hidden_x_ref) | copy-start | bytes 1032196
  138.0 10.5 %copy-start.9 = (bf16[256,4096]{1,0:T(8,128)(2,1)}, bf16[256,4096]{1,0:T(8,128)(2,1)S(1)}, u32[]{:S(2)}) copy-start(bf16[256,4096]{1,0:T(8,128)(2,1)S(1)} %collective-permute-done.25.back_x_ref) | copy-start | bytes 6291460
  138.1 20.9 %collective-permute-start.26 = (bf16[64,4096]{1,0:T(8,128)(2,1)S(1)}, bf16[64,4096]{1,0:T(8,128)(2,1)S(1)}, u32[]{:S(2)}, u32[]{:S(2)}) collective-permute-start(bf16[64,4096]{1,0:T(8,128)(2,1)S(1)} %add_convert_fusion.1), channel_id=1, source_target_pairs={{0,8},{4,12},{8,16},{12,20},{16,24},{20,28},{24,0},{28,4},{1,9},{5... | collective-permute-start | bytes 1572872 | tf_op jit(solution)/shard_map/ppermute | solution.py:17
  138.2 20.8 %collective-permute-start.27 = (bf16[64,4096]{1,0:T(8,128)(2,1)S(1)}, bf16[64,4096]{1,0:T(8,128)(2,1)S(1)}, u32[]{:S(2)}, u32[]{:S(2)}) collective-permute-start(bf16[64,4096]{1,0:T(8,128)(2,1)S(1)} %add_convert_fusion), channel_id=1, source_target_pairs={{0,24},{4,28},{8,0},{12,4},{16,8},{20,12},{24,16},{28,20},{1,25},{... | collective-permute-start | bytes 1572872 | tf_op jit(solution)/shard_map/ppermute | solution.py:17
  141.5 16.4 %collective-permute-start.28 = (bf16[64,1024]{1,0:T(8,128)(2,1)S(1)}, bf16[64,1024]{1,0:T(8,128)(2,1)S(1)}, u32[]{:S(2)}, u32[]{:S(2)}) collective-permute-start(bf16[64,1024]{1,0:T(8,128)(2,1)S(1)} %get-tuple-element.140), channel_id=1, source_target_pairs={{0,1},{1,0},{2,3},{3,2},{4,5},{5,4},{6,7},{7,6},{8,9},{9,8},{10,11... | collective-permute-start | bytes 393224 | tf_op jit(solution)/shard_map/ppermute | solution.py:27
  146.3 11.6 %collective-permute-start.29 = (bf16[64,1024]{1,0:T(8,128)(2,1)S(1)}, bf16[64,1024]{1,0:T(8,128)(2,1)S(1)}, u32[]{:S(2)}, u32[]{:S(2)}) collective-permute-start(bf16[64,1024]{1,0:T(8,128)(2,1)S(1)} %get-tuple-element.141), channel_id=1, source_target_pairs={{0,2},{1,3},{2,0},{3,1},{4,6},{5,7},{6,4},{7,5},{8,10},{9,11},{10,... | collective-permute-start | bytes 393224 | tf_op jit(solution)/shard_map/ppermute | solution.py:27
  147.8 11.2 %collective-permute-start.30 = (bf16[64,1024]{1,0:T(8,128)(2,1)S(1)}, bf16[64,1024]{1,0:T(8,128)(2,1)S(1)}, u32[]{:S(2)}, u32[]{:S(2)}) collective-permute-start(bf16[64,1024]{1,0:T(8,128)(2,1)S(1)} %get-tuple-element.142), channel_id=1, source_target_pairs={{0,3},{1,2},{2,1},{3,0},{4,7},{5,6},{6,5},{7,4},{8,11},{9,10},{10,... | collective-permute-start | bytes 393224 | tf_op jit(solution)/shard_map/ppermute | solution.py:27
  148.5 10.5 %copy-start.15 = (f32[64,4096]{1,0:T(8,128)S(1)}, f32[64,4096]{1,0:T(8,128)}, u32[]{:S(2)}) copy-start(f32[64,4096]{1,0:T(8,128)} %get-tuple-element.153) | copy-start | bytes 3145732
  159.2 6.4 %collective-permute-start.31 = (bf16[64,1024]{1,0:T(8,128)(2,1)S(1)}, bf16[64,1024]{1,0:T(8,128)(2,1)S(1)}, u32[]{:S(2)}, u32[]{:S(2)}) collective-permute-start(bf16[64,1024]{1,0:T(8,128)(2,1)S(1)} %get-tuple-element.167), channel_id=1, source_target_pairs={{0,1},{1,0},{2,3},{3,2},{4,5},{5,4},{6,7},{7,6},{8,9},{9,8},{10,11... | collective-permute-start | bytes 393224 | tf_op jit(solution)/shard_map/ppermute | solution.py:27
  160.6 10.5 %collective-permute-start.33 = (bf16[64,1024]{1,0:T(8,128)(2,1)S(1)}, bf16[64,1024]{1,0:T(8,128)(2,1)S(1)}, u32[]{:S(2)}, u32[]{:S(2)}) collective-permute-start(bf16[64,1024]{1,0:T(8,128)(2,1)S(1)} %get-tuple-element.168), channel_id=1, source_target_pairs={{0,3},{1,2},{2,1},{3,0},{4,7},{5,6},{6,5},{7,4},{8,11},{9,10},{10,... | collective-permute-start | bytes 393224 | tf_op jit(solution)/shard_map/ppermute | solution.py:27
  162.7 9.1 %collective-permute-start.32 = (bf16[64,1024]{1,0:T(8,128)(2,1)S(1)}, bf16[64,1024]{1,0:T(8,128)(2,1)S(1)}, u32[]{:S(2)}, u32[]{:S(2)}) collective-permute-start(bf16[64,1024]{1,0:T(8,128)(2,1)S(1)} %get-tuple-element.169), channel_id=1, source_target_pairs={{0,2},{1,3},{2,0},{3,1},{4,6},{5,7},{6,4},{7,5},{8,10},{9,11},{10,... | collective-permute-start | bytes 393224 | tf_op jit(solution)/shard_map/ppermute | solution.py:27
  (10 other events, 17.5 us)
where the time goes:
time: 175 us; the launch traced here: 173 us
  waiting for transfers between devices  59.2 us (34%)
  starting transfers between devices  58.7 us (34%)
  Pallas kernels  36.7 us (21%)
  other arithmetic  6.28 us (4%)
  local copies, waits for them, and re-layouts  4.64 us (3%)
  matrix products  4.47 us (3%)
  between operations  2.71 us (2%)
    ppermute x14, waiting for transfers between devices, along_y(): lax.ppermute(array, 'expert', [(i, (i + 2 * step) % n) for i in range(n)])  27.2 us
    ppermute x12, starting transfers between devices, along_mp(): return lax.ppermute(array, 'mp', [(i, i ^ flip) for i in range(n)])  23.3 us
    ppermute x14, starting transfers between devices, along_y(): lax.ppermute(array, 'expert', [(i, (i + 2 * step) % n) for i in range(n)])  19.3 us
    ppermute x12, waiting for transfers between devices, along_mp(): return lax.ppermute(array, 'mp', [(i, i ^ flip) for i in range(n)])  16.9 us
    ppermute x2, waiting for transfers between devices, mirrored(): return lax.ppermute(array, 'section', [(i, n - 1 - i) for i in range(n)])  15.1 us
    ppermute x2, starting transfers between devices, mirrored(): return lax.ppermute(array, 'section', [(i, n - 1 - i) for i in range(n)])  14.9 us
    pallas_call x1, Pallas kernels, run_back(): pl.pallas_call(back_kernel, out_shape=block_shapes(width) + (hidden, hidd...  12.5 us
    pallas_call x1, Pallas kernels, run_fwd(): pl.pallas_call(fwd_kernel, out_shape=block_shapes(width), in_specs=[HBM]...  9.66 us
  transfers between devices with their start and end apart: 34, of which 17 were waited for; matrix products, arithmetic and copies ran while one was open for 3% of the time, Pallas kernels for 21%

commit v1 on v0

--- a/solution.py
+++ b/solution.py
@@ -28,8 +28,9 @@
 
 
 def mirrored(array):
-    n = lax.axis_size("section")
-    return lax.ppermute(array, "section", [(i, n - 1 - i) for i in range(n)])
+    sections, places = (lax.axis_size("section"), lax.axis_size("mp"))
+    last = sections * places - 1
+    return lax.ppermute(array, ("section", "mp"), [(i, last - i) for i in range(last + 1)])
 
 
 def routing(pair_ids, pair_weights, expert):
@@ -182,8 +183,8 @@
 
 def back_kernel(*refs):
     hidden_grad_ref, gate_own, up_own, gate_x, up_x = refs[5:10]
-    own_ref, behind_ref, ahead_ref, far_ref, keep_ref, send_ref, rows_out = refs[10:17]
-    rows, gate, up, sems = refs[17:]
+    own_ref, behind_ref, ahead_ref, far_ref, first_ref, keep_ref, send_ref, rows_out = refs[10:18]
+    rows, gate, up, sems = refs[18:]
     units = gate_own.shape[0]
     rows_in = fetch(later_rows(refs[:5]), rows, sems, 0)
     gate_in = fetch(whole(gate_own, gate_x), gate, sems, 5)
@@ -203,31 +204,32 @@
         hidden_grad * pre_up * sigmoid_pre * (1.0 + pre_gate * (1.0 - sigmoid_pre))
     ).astype(jnp.bfloat16)
     up_grad = (hidden_grad * activated).astype(jnp.bfloat16)
-    for index, array in enumerate((hidden, gate_grad, up_grad)):
-        keep_ref[units * index : units * (index + 1)] = array[:units]
-        send_ref[units * index : units * (index + 1)] = array[units:]
+    first_ref[...] = hidden[:units]
+    keep_ref[:units] = gate_grad[:units]
+    keep_ref[units:] = up_grad[:units]
+    send_ref[:units] = hidden[units:]
+    send_ref[units : 2 * units] = gate_grad[units:]
+    send_ref[2 * units :] = up_grad[units:]
     spread_kernel_part(
         ((gate_grad, gate), (up_grad, up)), own_ref, (behind_ref, ahead_ref, far_ref)
     )
     rows_back.wait()
 
 
-def weight_kernel(hidden_ref, hidden_x_ref, grad_ref, grad_x_ref, back_ref, back_x_ref, *outs):
+def weight_kernel(hidden_ref, hidden_x_ref, rows_ref, rows_x_ref, *outs):
     units = outs[0].shape[0]
     for index, out in enumerate(outs):
         part = slice(units * index, units * (index + 1))
-        rows, rows_x = (grad_ref, grad_x_ref) if index == 0 else (back_ref, back_x_ref)
-        total = jnp.dot(hidden_ref[part], rows[...], preferred_element_type=jnp.float32)
+        total = jnp.dot(hidden_ref[part], rows_ref[...], preferred_element_type=jnp.float32)
         total = total + jnp.dot(
-            hidden_x_ref[part], rows_x[...], preferred_element_type=jnp.float32
+            hidden_x_ref[part], rows_x_ref[...], preferred_element_type=jnp.float32
         )
         out[...] = total.astype(jnp.bfloat16)
 
 
 HBM = pl.BlockSpec(memory_space=pltpu.HBM)
 VMEM = pl.BlockSpec(memory_space=pltpu.VMEM)
-LIMIT = 56 * 2**20
-PARAMS = pltpu.CompilerParams(vmem_limit_bytes=LIMIT)
+PARAMS = pltpu.CompilerParams(vmem_limit_bytes=30 * 2**20)
 SMALL = pl.CostEstimate(flops=1, bytes_accessed=1, transcendentals=0)
 
 
@@ -279,32 +281,36 @@
 
 def run_back(pieces, hidden_grad, weights):
     units, width = weights[0].shape
-    hidden = jax.ShapeDtypeStruct((3 * units, 4 * CAP), jnp.bfloat16)
+
+    def hidden(count):
+        return jax.ShapeDtypeStruct((count * units, 4 * CAP), jnp.bfloat16)
+
     return pl.pallas_call(
         back_kernel,
-        out_shape=block_shapes(width) + (hidden, hidden, rows_shape(width)),
+        out_shape=block_shapes(width) + (hidden(1), hidden(2), hidden(3), rows_shape(width)),
         in_specs=[HBM] * 5 + [VMEM] + [HBM] * 4,
-        out_specs=(VMEM,) * 6 + (HBM,),
+        out_specs=(VMEM,) * 7 + (HBM,),
         scratch_shapes=scratch(units, width, 2, 10),
-        compiler_params=PARAMS,
+        compiler_params=pltpu.CompilerParams(vmem_limit_bytes=56 * 2**20),
         cost_estimate=SMALL,
     )(*pieces, hidden_grad, *weights)
 
 
-def run_weights(hidden, hidden_x, grad_rows, grad_rows_x, back_rows, back_rows_x):
-    units, width = hidden.shape[0] // 3, grad_rows.shape[1]
+def run_weights(units, hidden, hidden_x, rows, rows_x):
+    width = rows.shape[1]
     step = min(width, 512)
+    outs = hidden.shape[0] // units
     held = pl.BlockSpec(hidden.shape, lambda i: (0, 0))
-    rows = pl.BlockSpec((grad_rows.shape[0], step), lambda i: (0, i))
+    columns = pl.BlockSpec((rows.shape[0], step), lambda i: (0, i))
     return pl.pallas_call(
         weight_kernel,
         grid=(width // step,),
-        out_shape=(jax.ShapeDtypeStruct((units, width), jnp.bfloat16),) * 3,
-        in_specs=[held] * 2 + [rows] * 4,
-        out_specs=(pl.BlockSpec((units, step), lambda i: (0, i)),) * 3,
+        out_shape=(jax.ShapeDtypeStruct((units, width), jnp.bfloat16),) * outs,
+        in_specs=[held] * 2 + [columns] * 2,
+        out_specs=(pl.BlockSpec((units, step), lambda i: (0, i)),) * outs,
         compiler_params=PARAMS,
         cost_estimate=SMALL,
-    )(hidden, hidden_x, grad_rows, grad_rows_x, back_rows, back_rows_x)
+    )(hidden, hidden_x, rows, rows_x)
 
 
 def add_parts(own, parts):
@@ -359,42 +365,43 @@
 
     fwd_gate, fwd_slot = routing(route_ids[0], route_weights[0], expert)
     fwd_pick = picker_of(fwd_slot)
+    fwd_buf = pack(fwd_pick, tokens_in[0])
+    held_rows = lax.dynamic_index_in_dim(
+        stash[0], returned_batch_index[0, 0], axis=0, keepdims=False
+    )
+    fwd_buf, back_ids, back_weights = together(fwd_buf, back_ids, back_weights)
     back_gate, back_slot = routing(back_ids[0], back_weights[0], expert)
     back_pick = picker_of(back_slot)
     grad_tokens = (back_gate[:, None] * upstream[0].astype(jnp.float32)).astype(jnp.bfloat16)
-    bufs = stacked(pack(fwd_pick, tokens_in[0]), pack(back_pick, grad_tokens))
-    held_rows = lax.dynamic_index_in_dim(
-        stash[0], returned_batch_index[0, 0], axis=0, keepdims=False
-    )
-    bufs, back_slot, gate_w, up_w, down_w, held_rows = together(
-        bufs, back_slot, gate_w, up_w, down_w, held_rows
-    )
-    one, two, three, held_slot, gate_x, up_w, down_w, held_rows = together(
-        *ask_mp(bufs), mirrored(back_slot), other_core(gate_w), up_w, down_w, held_rows
-    )
-
-    wide = widen(bufs, (one, two, three), place)
-    fwd_wide, grad_wide = wide[:CAP], wide[CAP:]
-    fwd_behind, fwd_ahead, back_buf, up_x, down_x, grad_wide = together(
-        *both_ways(fwd_wide, fwd_wide),
-        mirrored(pack(picker_of(held_slot), held_rows)),
-        other_core(up_w),
-        other_core(down_w),
-        grad_wide,
-    )
-
-    cw, ccw, one, two, three = together(
+    one, two, three, held_rows, gate_x, grad_buf = together(
+        *ask_mp(fwd_buf), mirrored(held_rows), other_core(gate_w), pack(back_pick, grad_tokens)
+    )
+
+    fwd_wide = widen(fwd_buf, (one, two, three), place)
+    fwd_behind, fwd_ahead, one, two, three, held_rows = together(
+        *both_ways(fwd_wide, fwd_wide), *ask_mp(grad_buf), held_rows
+    )
+
+    grad_wide = widen(grad_buf, (one, two, three), place)
+    back_buf = pack(back_pick, held_rows)
+    cw, ccw, one, two, three, up_w, down_w = together(
         *both_ways(stacked(fwd_behind[:half], grad_wide), stacked(fwd_ahead[half:], grad_wide)),
         *ask_mp(back_buf),
-    )
-
+        up_w,
+        down_w,
+    )
+
+    up_x, down_x = (other_core(up_w), other_core(down_w))
     fwd_terms = run_fwd(
         (fwd_wide, fwd_behind, fwd_ahead, cw, ccw), (gate_w, up_w, down_w, gate_x, up_x, down_x)
     )
     grad_pieces = (grad_wide, cw, ccw)
-    back_wide = widen(back_buf, (one, two, three), place)
-    cw, ccw, *fwd_terms = together(
-        *both_ways(stacked(cw[half:CAP], back_wide), stacked(ccw[CAP:], back_wide)), *fwd_terms
+    back_wide = widen(back_buf, (one, two, three), place ^ 3)
+    cw, ccw, down_x, up_x, *fwd_terms = together(
+        *both_ways(stacked(cw[half:CAP], back_wide), stacked(ccw[CAP:], back_wide)),
+        down_x,
+        up_x,
+        *fwd_terms,
     )
     fwd_own, fwd_to_behind, fwd_to_ahead, fwd_to_far = fwd_terms
 
@@ -415,7 +422,7 @@
         *back_terms,
     )
     back_own, back_to_behind, back_to_ahead, back_to_far = back_terms[:4]
-    hidden_keep, hidden_send, back_rows = back_terms[4:]
+    hidden, pair_grads, hidden_send, back_rows = back_terms[4:]
 
     fwd_total = add_parts(fwd_own, (p0, p1))
     f0, f1, hidden_x, back_rows_x, *fwd_blocks = together(
@@ -425,15 +432,18 @@
         *split_mp(fwd_total, place),
     )
 
-    p0, p1, one, two, three, *grads = together(
+    units = gate_w.shape[0]
+    p0, p1, one, two, three, grad_down = together(
         *near_with_far(back_to_behind, back_to_ahead, f0, f1),
         *send_mp(fwd_blocks[1:]),
-        *run_weights(hidden_keep, hidden_x, grad_rows, grad_rows_x, back_rows, back_rows_x),
-    )
-    grad_down, grad_gate, grad_up = grads
+        *run_weights(units, hidden, hidden_x[:units], grad_rows, grad_rows_x),
+    )
 
     back_here, *back_sent = split_mp(add_parts(back_own, (p0, p1)), place)
-    back_sent = send_mp(back_sent)
+    grad_gate, grad_up, *back_sent = together(
+        *run_weights(units, pair_grads, hidden_x[units:], back_rows, back_rows_x),
+        *send_mp(back_sent),
+    )
     fwd_sum = add_parts(fwd_blocks[0], (one, two, three))
     fwd_row_gate = jnp.sum(jnp.where(fwd_pick, fwd_gate[None, :], 0.0), axis=1)
     expert_out = unpack(fwd_pick, (fwd_sum * fwd_row_gate[:, None]).astype(jnp.bfloat16))

time: 175 us -> 176 us (level)
  starting transfers between devices: 58.7 us -> 49 us
  waiting for transfers between devices: 59.2 us -> 66.6 us
  other arithmetic: 6.28 us -> 12.5 us
  Pallas kernels: 36.7 us -> 33.5 us
  local copies, waits for them, and re-layouts: 4.64 us -> 7.39 us
    ppermute x12 -> x15, waiting for transfers between devices: 16.9 us -> 31.4 us  [along_mp(): return lax.ppermute(array, 'mp', [(i, i ^ flip) for i in range(n)])]
    ppermute x2 -> x1, starting transfers between devices: 14.9 us -> 7.78 us  [mirrored(): lax.ppermute(array, ('section', 'mp'), [(i, last - i) for i in range(last...]
    ppermute x2 -> x1, waiting for transfers between devices: 15.1 us -> 7.98 us  [mirrored(): lax.ppermute(array, ('section', 'mp'), [(i, last - i) for i in range(last...]
    ppermute x12 -> x15, starting transfers between devices: 23.3 us -> 18.1 us  [along_mp(): return lax.ppermute(array, 'mp', [(i, i ^ flip) for i in range(n)])]
    ppermute x14, starting transfers between devices: 19.3 us -> 22.4 us  [along_y(): lax.ppermute(array, 'expert', [(i, (i + 2 * step) % n) for i in range(n)])]
    unnamed x48 -> x74, local copies, waits for them, and re-layouts: 1.76 us -> 4.81 us
    pallas_call x1, Pallas kernels: 9.66 us -> 6.79 us  [run_fwd(): pl.pallas_call(fwd_kernel, out_shape=block_shapes(width), in_specs=[HBM]...]
    pallas_call x1, Pallas kernels: 5.19 us -> 2.53 us  [run_grad(): pl.pallas_call(grad_kernel, out_shape=(jax.ShapeDtypeStruct((2 * units, 4...]
  transfers between devices with their start and end apart: 34 -> 36, of which waited for: 17 -> 17; matrix products, arithmetic and copies ran while one was open for 3% -> 8% of each run, Pallas kernels for 21% -> 19%
where the time goes in v1:
time: 176 us; the launch traced here: 175 us
  waiting for transfers between devices  66.6 us (38%)
  starting transfers between devices  49 us (28%)
  Pallas kernels  33.5 us (19%)
  other arithmetic  12.5 us (7%)
  local copies, waits for them, and re-layouts  7.39 us (4%)
  matrix products  3.53 us (2%)
  between operations  2.76 us (2%)
    ppermute x15, waiting for transfers between devices, along_mp(): return lax.ppermute(array, 'mp', [(i, i ^ flip) for i in range(n)])  31.4 us
    ppermute x14, waiting for transfers between devices, along_y(): lax.ppermute(array, 'expert', [(i, (i + 2 * step) % n) for i in range(n)])  27.2 us
    ppermute x14, starting transfers between devices, along_y(): lax.ppermute(array, 'expert', [(i, (i + 2 * step) % n) for i in range(n)])  22.4 us
    ppermute x15, starting transfers between devices, along_mp(): return lax.ppermute(array, 'mp', [(i, i ^ flip) for i in range(n)])  18.1 us
    pallas_call x1, Pallas kernels, run_back(): pl.pallas_call(back_kernel, out_shape=block_shapes(width) + (hidden(1), h...  12.4 us
    pallas_call x2, Pallas kernels, run_weights(): pl.pallas_call(weight_kernel, grid=(width // step,), out_shape=(jax.Shape...  11.8 us
    ppermute x1, waiting for transfers between devices, mirrored(): lax.ppermute(array, ('section', 'mp'), [(i, last - i) for i in range(last...  7.98 us
    ppermute x1, starting transfers between devices, mirrored(): lax.ppermute(array, ('section', 'mp'), [(i, last - i) for i in range(last...  7.78 us
  transfers between devices with their start and end apart: 36, of which 17 were waited for; matrix products, arithmetic and copies ran while one was open for 8% of the time, Pallas kernels for 19%

profile of v1, /device:TPU:32, one launch (start us, length us, event | category | flops | bytes accessed | tf_op | source)
XLA Modules:
  0.0 175.1 jit_solution(6907032663921790119)
XLA Ops:
  2.6 1.1 convolution_convert_fusion.4
  3.7 1.9 %collective-permute-start = (bf16[64,1024]{1,0:T(8,128)(2,1)S(1)}, bf16[64,1024]{1,0:T(8,128)(2,1)S(1)}, u32[]{:S(2)}, u32[]{:S(2)}) collective-permute-start(bf16[64,1024]{1,0:T(8,128)(2,1)S(1)} %convolution_convert_fusion.4), channel_id=1, source_target_pairs={{0,1},{1,0},{2,3},{3,2},{4,5},{5,4},{6,7},{7,6},{8,9},{9,8},{10,11... | collective-permute-start | bytes 393224 | tf_op jit(solution)/shard_map/ppermute | solution.py:27
  5.6 1.5 collective-permute-start.1
  8.3 7.8 %collective-permute-start.3 = (bf16[128,1024]{1,0:T(8,128)(2,1)S(1)}, bf16[128,1024]{1,0:T(8,128)(2,1)S(1)}, u32[]{:S(2)}, u32[]{:S(2)}) collective-permute-start(bf16[128,1024]{1,0:T(8,128)(2,1)S(1)} %dynamic-slice_bitcast_fusion), channel_id=1, source_target_pairs={{0,227},{1,226},{2,225},{3,224},{32,195},{33,194},{34,193},{35,192... | collective-permute-start | bytes 786440 | tf_op jit(solution)/shard_map/ppermute | solution.py:33
  18.2 1.8 %collective-permute-done.2 = bf16[64,1024]{1,0:T(8,128)(2,1)} collective-permute-done((bf16[64,1024]{1,0:T(8,128)(2,1)S(1)}, bf16[64,1024]{1,0:T(8,128)(2,1)}, u32[]{:S(2)}, u32[]{:S(2)}) %collective-permute-start.2) | collective-permute-done | bytes 131104 | tf_op jit(solution)/shard_map/ppermute | solution.py:27
  20.0 8.0 %collective-permute-done.3 = bf16[128,1024]{1,0:T(8,128)(2,1)S(1)} collective-permute-done((bf16[128,1024]{1,0:T(8,128)(2,1)S(1)}, bf16[128,1024]{1,0:T(8,128)(2,1)S(1)}, u32[]{:S(2)}, u32[]{:S(2)}) %collective-permute-start.3) | collective-permute-done | bytes 262176 | tf_op jit(solution)/shard_map/ppermute | solution.py:33
  28.0 1.3 broadcast_select_fusion.15
  29.5 1.7 collective-permute-start.5
  31.1 1.7 collective-permute-start.6
  33.6 1.7 collective-permute-start.8
  36.3 2.9 %collective-permute-done.7 = bf16[64,1024]{1,0:T(8,128)(2,1)S(1)} collective-permute-done((bf16[64,1024]{1,0:T(8,128)(2,1)S(1)}, bf16[64,1024]{1,0:T(8,128)(2,1)S(1)}, u32[]{:S(2)}, u32[]{:S(2)}) %collective-permute-start.7) | collective-permute-done | bytes 131104 | tf_op jit(solution)/shard_map/ppermute | solution.py:27
  39.2 4.7 %collective-permute-done.8 = bf16[64,1024]{1,0:T(8,128)(2,1)S(1)} collective-permute-done((bf16[64,1024]{1,0:T(8,128)(2,1)S(1)}, bf16[64,1024]{1,0:T(8,128)(2,1)S(1)}, u32[]{:S(2)}, u32[]{:S(2)}) %collective-permute-start.8) | collective-permute-done | bytes 131104 | tf_op jit(solution)/shard_map/ppermute | solution.py:27
  43.9 3.1 %collective-permute-done.9 = bf16[64,1024]{1,0:T(8,128)(2,1)S(1)} collective-permute-done((bf16[64,1024]{1,0:T(8,128)(2,1)S(1)}, bf16[64,1024]{1,0:T(8,128)(2,1)S(1)}, u32[]{:S(2)}, u32[]{:S(2)}) %collective-permute-start.9) | collective-permute-done | bytes 131104 | tf_op jit(solution)/shard_map/ppermute | solution.py:27
  48.8 1.3 pad_maximum_fusion.2
  50.4 3.0 %collective-permute-start.11 = (bf16[96,4096]{1,0:T(8,128)(2,1)}, bf16[96,4096]{1,0:T(8,128)(2,1)}, u32[]{:S(2)}, u32[]{:S(2)}) collective-permute-start(bf16[96,4096]{1,0:T(8,128)(2,1)} %get-tuple-element.183), channel_id=1, source_target_pairs={{0,24},{4,28},{8,0},{12,4},{16,8},{20,12},{24,16},{28,20},{1,25},{... | collective-permute-start | bytes 2359304 | tf_op jit(solution)/shard_map/ppermute | solution.py:17
  53.7 2.4 %collective-permute-start.13 = (bf16[64,1024]{1,0:T(8,128)(2,1)S(1)}, bf16[64,1024]{1,0:T(8,128)(2,1)}, u32[]{:S(2)}, u32[]{:S(2)}) collective-permute-start(bf16[64,1024]{1,0:T(8,128)(2,1)S(1)} %convolution_convert_fusion.2), channel_id=1, source_target_pairs={{0,2},{1,3},{2,0},{3,1},{4,6},{5,7},{6,4},{7,5},{8,10},{9,11},{10,... | collective-permute-start | bytes 393224 | tf_op jit(solution)/shard_map/ppermute | solution.py:27
  57.2 3.1 %collective-permute-done.12 = bf16[64,1024]{1,0:T(8,128)(2,1)} collective-permute-done((bf16[64,1024]{1,0:T(8,128)(2,1)S(1)}, bf16[64,1024]{1,0:T(8,128)(2,1)}, u32[]{:S(2)}, u32[]{:S(2)}) %collective-permute-start.12) | collective-permute-done | bytes 131104 | tf_op jit(solution)/shard_map/ppermute | solution.py:27
  60.2 3.8 %collective-permute-done.13 = bf16[64,1024]{1,0:T(8,128)(2,1)} collective-permute-done((bf16[64,1024]{1,0:T(8,128)(2,1)S(1)}, bf16[64,1024]{1,0:T(8,128)(2,1)}, u32[]{:S(2)}, u32[]{:S(2)}) %collective-permute-start.13) | collective-permute-done | bytes 131104 | tf_op jit(solution)/shard_map/ppermute | solution.py:27
  64.0 3.1 %collective-permute-done.14 = bf16[64,1024]{1,0:T(8,128)(2,1)} collective-permute-done((bf16[64,1024]{1,0:T(8,128)(2,1)S(1)}, bf16[64,1024]{1,0:T(8,128)(2,1)}, u32[]{:S(2)}, u32[]{:S(2)}) %collective-permute-start.14) | collective-permute-done | bytes 131104 | tf_op jit(solution)/shard_map/ppermute | solution.py:27
  67.1 2.8 %collective-permute-done.10.refs_3_.refs_1_ = bf16[96,4096]{1,0:T(8,128)(2,1)S(1)} collective-permute-done((bf16[96,4096]{1,0:T(8,128)(2,1)}, bf16[96,4096]{1,0:T(8,128)(2,1)S(1)}, u32[]{:S(2)}, u32[]{:S(2)}) %collective-permute-start.10) | collective-permute-done | bytes 786464 | tf_op jit(solution)/shard_map/ppermute | solution.py:17
  70.5 1.1 broadcast_select_fusion.7
  74.5 3.0 %collective-permute-start.16 = (bf16[96,4096]{1,0:T(8,128)(2,1)S(1)}, bf16[96,4096]{1,0:T(8,128)(2,1)S(1)}, u32[]{:S(2)}, u32[]{:S(2)}) collective-permute-start(bf16[96,4096]{1,0:T(8,128)(2,1)S(1)} %get-tuple-element.179), channel_id=1, source_target_pairs={{0,24},{4,28},{8,0},{12,4},{16,8},{20,12},{24,16},{28,20},{1,25},{... | collective-permute-start | bytes 2359304 | tf_op jit(solution)/shard_map/ppermute | solution.py:17
  77.5 1.0 copy-done.10
  78.6 1.0 copy-done.13
  79.6 1.0 copy-done.15
  80.6 6.8 %shard_map.155 = (f32[64,4096]{1,0:T(8,128)S(1)}, bf16[64,4096]{1,0:T(8,128)(2,1)S(1)}, bf16[64,4096]{1,0:T(8,128)(2,1)S(1)}, bf16[64,4096]{1,0:T(8,128)(2,1)S(1)}) custom-call(bf16[64,4096]{1,0:T(8,128)(2,1)S(1)} %copy-done.10, bf16[64,4096]{1,0:T(8,128)(2,1)S(1)} %copy-done.13, bf16[64,4096]{1,0:T(8,128)(2,1)S(1)} %copy-done.15, ...), custom_call_target="tpu_custom_call" | custom-call | flops 1 | bytes 1 | tf_op jit(solution)/shard_map/pallas_call | solution.py:255
  87.5 7.4 %collective-permute-done.15.refs_3_.refs_1_ = bf16[96,4096]{1,0:T(8,128)(2,1)S(1)} collective-permute-done((bf16[96,4096]{1,0:T(8,128)(2,1)S(1)}, bf16[96,4096]{1,0:T(8,128)(2,1)S(1)}, u32[]{:S(2)}, u32[]{:S(2)}) %collective-permute-start.15) | collective-permute-done | bytes 786464 | tf_op jit(solution)/shard_map/ppermute | solution.py:17
  95.0 3.3 %collective-permute-start.20 = (bf16[64,4096]{1,0:T(8,128)(2,1)S(1)}, bf16[64,4096]{1,0:T(8,128)(2,1)S(1)}, u32[]{:S(2)}, u32[]{:S(2)}) collective-permute-start(bf16[64,4096]{1,0:T(8,128)(2,1)S(1)} %pad_maximum_fusion.10), channel_id=1, source_target_pairs={{0,24},{4,28},{8,0},{12,4},{16,8},{20,12},{24,16},{28,20},{1,25},{... | collective-permute-start | bytes 1572872 | tf_op jit(solution)/shard_map/ppermute | solution.py:17
  98.6 2.5 %shard_map.156 = (f32[448,256]{1,0:T(8,128)S(1)}, bf16[256,4096]{1,0:T(8,128)(2,1)}) custom-call(bf16[64,4096]{1,0:T(8,128)(2,1)S(1)} %pad_maximum_fusion.7.refs_0_, bf16[96,4096]{1,0:T(8,128)(2,1)S(1)} %collective-permute-done.10.refs_3_.refs_1_, bf16[96,4096]{1,0:T(8,128)(2,1)} %collective-permute-done.11.refs_4_.refs_2_, ...), custom_call_target="tpu_custom_call" | custom-call | flops 1 | bytes 1 | tf_op jit(solution)/shard_map/pallas_call | solution.py:268
  101.1 7.7 %collective-permute-done.20.refs_4_ = bf16[64,4096]{1,0:T(8,128)(2,1)S(1)} collective-permute-done((bf16[64,4096]{1,0:T(8,128)(2,1)S(1)}, bf16[64,4096]{1,0:T(8,128)(2,1)S(1)}, u32[]{:S(2)}, u32[]{:S(2)}) %collective-permute-start.20) | collective-permute-done | bytes 524320 | tf_op jit(solution)/shard_map/ppermute | solution.py:17
  108.8 3.6 %collective-permute-done.19.refs_3_ = bf16[64,4096]{1,0:T(8,128)(2,1)S(1)} collective-permute-done((bf16[64,4096]{1,0:T(8,128)(2,1)S(1)}, bf16[64,4096]{1,0:T(8,128)(2,1)S(1)}, u32[]{:S(2)}, u32[]{:S(2)}) %collective-permute-start.19) | collective-permute-done | bytes 524320 | tf_op jit(solution)/shard_map/ppermute | solution.py:17
  114.5 2.2 %collective-permute-start.21 = (bf16[64,4096]{1,0:T(8,128)(2,1)}, bf16[64,4096]{1,0:T(8,128)(2,1)}, u32[]{:S(2)}, u32[]{:S(2)}) collective-permute-start(bf16[64,4096]{1,0:T(8,128)(2,1)} %add_convert_fusion.3), channel_id=1, source_target_pairs={{0,8},{4,12},{8,16},{12,20},{16,24},{20,28},{24,0},{28,4},{1,9},{5... | collective-permute-start | bytes 1572872 | tf_op jit(solution)/shard_map/ppermute | solution.py:17
  117.5 12.4 %shard_map.157 = (f32[64,4096]{1,0:T(8,128)}, bf16[64,4096]{1,0:T(8,128)(2,1)}, bf16[64,4096]{1,0:T(8,128)(2,1)}, bf16[64,4096]{1,0:T(8,128)(2,1)}, bf16[224,256...) custom-call(bf16[64,4096]{1,0:T(8,128)(2,1)} %pad_maximum_fusion.8.refs_0_, ...), custom_call_target="tpu_custom_call" | custom-call | flops 1 | bytes 1 | tf_op jit(solution)/shard_map/pallas_call | solution.py:288
  130.5 1.1 fusion.20
  132.2 2.7 %collective-permute-start.25 = (bf16[32,4096]{1,0:T(8,128)(2,1)S(1)}, bf16[32,4096]{1,0:T(8,128)(2,1)S(1)}, u32[]{:S(2)}, u32[]{:S(2)}) collective-permute-start(bf16[32,4096]{1,0:T(8,128)(2,1)S(1)} %get-tuple-element.175), channel_id=1, source_target_pairs={{0,24},{4,28},{8,0},{12,4},{16,8},{20,12},{24,16},{28,20},{1,25},{... | collective-permute-start | bytes 786440 | tf_op jit(solution)/shard_map/ppermute | solution.py:17
  134.9 1.4 fusion.19
  136.4 5.2 %collective-permute-done.24 = bf16[32,4096]{1,0:T(8,128)(2,1)S(1)} collective-permute-done((bf16[32,4096]{1,0:T(8,128)(2,1)S(1)}, bf16[32,4096]{1,0:T(8,128)(2,1)S(1)}, u32[]{:S(2)}, u32[]{:S(2)}) %collective-permute-start.24) | collective-permute-done | bytes 262176 | tf_op jit(solution)/shard_map/ppermute | solution.py:17
  141.7 3.0 %collective-permute-start.29 = (bf16[64,4096]{1,0:T(8,128)(2,1)S(1)}, bf16[64,4096]{1,0:T(8,128)(2,1)S(1)}, u32[]{:S(2)}, u32[]{:S(2)}) collective-permute-start(bf16[64,4096]{1,0:T(8,128)(2,1)S(1)} %add_convert_fusion), channel_id=1, source_target_pairs={{0,24},{4,28},{8,0},{12,4},{16,8},{20,12},{24,16},{28,20},{1,25},{... | collective-permute-start | bytes 1572872 | tf_op jit(solution)/shard_map/ppermute | solution.py:17
  145.0 2.4 %collective-permute-start.31 = (bf16[64,1024]{1,0:T(8,128)(2,1)S(1)}, bf16[64,1024]{1,0:T(8,128)(2,1)S(1)}, u32[]{:S(2)}, u32[]{:S(2)}) collective-permute-start(bf16[64,1024]{1,0:T(8,128)(2,1)S(1)} %get-tuple-element.144), channel_id=1, source_target_pairs={{0,2},{1,3},{2,0},{3,1},{4,6},{5,7},{6,4},{7,5},{8,10},{9,11},{10,... | collective-permute-start | bytes 393224 | tf_op jit(solution)/shard_map/ppermute | solution.py:27
  147.4 1.0 collective-permute-start.32
  148.6 6.7 %shard_map.158 = bf16[224,4096]{1,0:T(8,128)(2,1)} custom-call(bf16[224,256]{1,0:T(8,128)(2,1)S(1)} %copy-done.20, bf16[224,256]{1,0:T(8,128)(2,1)S(1)} %slice.54.hidden_x_ref, bf16[256,4096]{1,0:T(8,128)(2,1)} %get-tuple-element.121.rows_ref, bf16[256,4096]{1,0:T(8,128)(2,1)S(1)} %collective-permute-done.23.rows_x_ref), custom_call_target="tpu_custom_call" | custom-call | flops 1 | bytes 1 | tf_op jit(solution)/shard_map/pallas_call | solution.py:305
  155.4 5.0 %shard_map.159 = (bf16[224,4096]{1,0:T(8,128)(2,1)}, bf16[224,4096]{1,0:T(8,128)(2,1)}) custom-call(bf16[448,256]{1,0:T(8,128)(2,1)S(1)} %copy-done.19, bf16[448,256]{1,0:T(8,128)(2,1)S(1)} %slice.55.hidden_x_ref, bf16[256,4096]{1,0:T(8,128)(2,1)S(1)} %copy-done.11, bf16[256,4096]{1,0:T(8,128)(2,1)S(1)} %collective-permute-done.27.rows_x_ref), custom_call_target="tpu_custom_call" | custom-call | flops 1 | bytes 1 | tf_op jit(solution)/shard_map/pallas_call | solution.py:305
  160.7 1.1 collective-permute-start.33
  161.8 1.5 collective-permute-start.34
  163.2 1.0 collective-permute-start.35
  165.3 1.9 %collective-permute-done.33 = bf16[64,1024]{1,0:T(8,128)(2,1)S(1)} collective-permute-done((bf16[64,1024]{1,0:T(8,128)(2,1)S(1)}, bf16[64,1024]{1,0:T(8,128)(2,1)S(1)}, u32[]{:S(2)}, u32[]{:S(2)}) %collective-permute-start.33) | collective-permute-done | bytes 131104 | tf_op jit(solution)/shard_map/ppermute | solution.py:27
  167.1 4.0 %collective-permute-done.34 = bf16[64,1024]{1,0:T(8,128)(2,1)S(1)} collective-permute-done((bf16[64,1024]{1,0:T(8,128)(2,1)S(1)}, bf16[64,1024]{1,0:T(8,128)(2,1)S(1)}, u32[]{:S(2)}, u32[]{:S(2)}) %collective-permute-start.34) | collective-permute-done | bytes 131104 | tf_op jit(solution)/shard_map/ppermute | solution.py:27
  171.1 3.0 %collective-permute-done.35 = bf16[64,1024]{1,0:T(8,128)(2,1)S(1)} collective-permute-done((bf16[64,1024]{1,0:T(8,128)(2,1)S(1)}, bf16[64,1024]{1,0:T(8,128)(2,1)S(1)}, u32[]{:S(2)}, u32[]{:S(2)}) %collective-permute-start.35) | collective-permute-done | bytes 131104 | tf_op jit(solution)/shard_map/ppermute | solution.py:27
  (160 shorter events, 19.6 us)
Async XLA Ops:
  0.6 7.7 %copy-start = (bf16[1,2,128,1024]{3,2,1,0:T(8,128)(2,1)S(1)}, bf16[1,2,128,1024]{3,2,1,0:T(8,128)(2,1)}, u32[]{:S(2)}) copy-start(bf16[1,2,128,1024]{3,2,1,0:T(8,128)(2,1)} %param.15) | copy-start | bytes 1572868
  0.6 17.3 %copy-start.32 = (bf16[1,128,1024]{2,1,0:T(8,128)(2,1)S(1)}, bf16[1,128,1024]{2,1,0:T(8,128)(2,1)}, u32[]{:S(2)}) copy-start(bf16[1,128,1024]{2,1,0:T(8,128)(2,1)} %param.19) | copy-start | bytes 786436
  0.7 27.4 %collective-permute-start.4 = (bf16[224,4096]{1,0:T(8,128)(2,1)}, bf16[224,4096]{1,0:T(8,128)(2,1)S(1)}, u32[]{:S(2)}, u32[]{:S(2)}) collective-permute-start(bf16[224,4096]{1,0:T(8,128)(2,1)} %bitcast.38), channel_id=1, source_target_pairs={{0,4},{4,0},{8,12},{12,8},{16,20},{20,16},{24,28},{28,24},{1,5},{5... | collective-permute-start | bytes 5505032 | tf_op jit(solution)/shard_map/ppermute | solution.py:22
  3.7 14.5 %collective-permute-start = (bf16[64,1024]{1,0:T(8,128)(2,1)S(1)}, bf16[64,1024]{1,0:T(8,128)(2,1)S(1)}, u32[]{:S(2)}, u32[]{:S(2)}) collective-permute-start(bf16[64,1024]{1,0:T(8,128)(2,1)S(1)} %convolution_convert_fusion.4), channel_id=1, source_target_pairs={{0,1},{1,0},{2,3},{3,2},{4,5},{5,4},{6,7},{7,6},{8,9},{9,8},{10,11... | collective-permute-start | bytes 393224 | tf_op jit(solution)/shard_map/ppermute | solution.py:27
  5.6 12.6 %collective-permute-start.1 = (bf16[64,1024]{1,0:T(8,128)(2,1)S(1)}, bf16[64,1024]{1,0:T(8,128)(2,1)}, u32[]{:S(2)}, u32[]{:S(2)}) collective-permute-start(bf16[64,1024]{1,0:T(8,128)(2,1)S(1)} %convolution_convert_fusion.4), channel_id=1, source_target_pairs={{0,2},{1,3},{2,0},{3,1},{4,6},{5,7},{6,4},{7,5},{8,10},{9,11},{10,... | collective-permute-start | bytes 393224 | tf_op jit(solution)/shard_map/ppermute | solution.py:27
  7.2 12.9 %collective-permute-start.2 = (bf16[64,1024]{1,0:T(8,128)(2,1)S(1)}, bf16[64,1024]{1,0:T(8,128)(2,1)}, u32[]{:S(2)}, u32[]{:S(2)}) collective-permute-start(bf16[64,1024]{1,0:T(8,128)(2,1)S(1)} %convolution_convert_fusion.4), channel_id=1, source_target_pairs={{0,3},{1,2},{2,1},{3,0},{4,7},{5,6},{6,5},{7,4},{8,11},{9,10},{10,... | collective-permute-start | bytes 393224 | tf_op jit(solution)/shard_map/ppermute | solution.py:27
  8.3 19.7 %collective-permute-start.3 = (bf16[128,1024]{1,0:T(8,128)(2,1)S(1)}, bf16[128,1024]{1,0:T(8,128)(2,1)S(1)}, u32[]{:S(2)}, u32[]{:S(2)}) collective-permute-start(bf16[128,1024]{1,0:T(8,128)(2,1)S(1)} %dynamic-slice_bitcast_fusion), channel_id=1, source_target_pairs={{0,227},{1,226},{2,225},{3,224},{32,195},{33,194},{34,193},{35,192... | collective-permute-start | bytes 786440 | tf_op jit(solution)/shard_map/ppermute | solution.py:33
  29.5 19.3 %copy-start.9 = (bf16[64,4096]{1,0:T(8,128)(2,1)}, bf16[64,4096]{1,0:T(8,128)(2,1)S(1)}, u32[]{:S(2)}) copy-start(bf16[64,4096]{1,0:T(8,128)(2,1)S(1)} %pad_maximum_fusion.6.refs_0_) | copy-start | bytes 1572868
  29.5 17.5 %collective-permute-start.5 = (bf16[64,4096]{1,0:T(8,128)(2,1)S(1)}, bf16[64,4096]{1,0:T(8,128)(2,1)S(1)}, u32[]{:S(2)}, u32[]{:S(2)}) collective-permute-start(bf16[64,4096]{1,0:T(8,128)(2,1)S(1)} %pad_maximum_fusion.6.refs_0_), channel_id=1, source_target_pairs={{0,8},{4,12},{8,16},{12,20},{16,24},{20,28},{24,0},{28,4},{1,9},{5... | collective-permute-start | bytes 1572872 | tf_op jit(solution)/shard_map/ppermute | solution.py:17
  31.1 15.9 %collective-permute-start.6 = (bf16[64,4096]{1,0:T(8,128)(2,1)S(1)}, bf16[64,4096]{1,0:T(8,128)(2,1)S(1)}, u32[]{:S(2)}, u32[]{:S(2)}) collective-permute-start(bf16[64,4096]{1,0:T(8,128)(2,1)S(1)} %pad_maximum_fusion.6.refs_0_), channel_id=1, source_target_pairs={{0,24},{4,28},{8,0},{12,4},{16,8},{20,12},{24,16},{28,20},{1,25},{... | collective-permute-start | bytes 1572872 | tf_op jit(solution)/shard_map/ppermute | solution.py:17
  32.8 6.4 %collective-permute-start.7 = (bf16[64,1024]{1,0:T(8,128)(2,1)S(1)}, bf16[64,1024]{1,0:T(8,128)(2,1)S(1)}, u32[]{:S(2)}, u32[]{:S(2)}) collective-permute-start(bf16[64,1024]{1,0:T(8,128)(2,1)S(1)} %convolution_convert_fusion.3), channel_id=1, source_target_pairs={{0,1},{1,0},{2,3},{3,2},{4,5},{5,4},{6,7},{7,6},{8,9},{9,8},{10,11... | collective-permute-start | bytes 393224 | tf_op jit(solution)/shard_map/ppermute | solution.py:27
  33.6 10.3 %collective-permute-start.8 = (bf16[64,1024]{1,0:T(8,128)(2,1)S(1)}, bf16[64,1024]{1,0:T(8,128)(2,1)S(1)}, u32[]{:S(2)}, u32[]{:S(2)}) collective-permute-start(bf16[64,1024]{1,0:T(8,128)(2,1)S(1)} %convolution_convert_fusion.3), channel_id=1, source_target_pairs={{0,2},{1,3},{2,0},{3,1},{4,6},{5,7},{6,4},{7,5},{8,10},{9,11},{10,... | collective-permute-start | bytes 393224 | tf_op jit(solution)/shard_map/ppermute | solution.py:27
  35.3 11.7 %collective-permute-start.9 = (bf16[64,1024]{1,0:T(8,128)(2,1)S(1)}, bf16[64,1024]{1,0:T(8,128)(2,1)S(1)}, u32[]{:S(2)}, u32[]{:S(2)}) collective-permute-start(bf16[64,1024]{1,0:T(8,128)(2,1)S(1)} %convolution_convert_fusion.3), channel_id=1, source_target_pairs={{0,3},{1,2},{2,1},{3,0},{4,7},{5,6},{6,5},{7,4},{8,11},{9,10},{10,... | collective-permute-start | bytes 393224 | tf_op jit(solution)/shard_map/ppermute | solution.py:27
  48.8 21.1 %copy-start.1 = (bf16[1,224,4096]{2,1,0:T(8,128)(2,1)S(1)}, bf16[1,224,4096]{2,1,0:T(8,128)(2,1)}, u32[]{:S(2)}) copy-start(bf16[1,224,4096]{2,1,0:T(8,128)(2,1)} %param.23) | copy-start | bytes 5505028
  50.2 19.8 %collective-permute-start.10 = (bf16[96,4096]{1,0:T(8,128)(2,1)}, bf16[96,4096]{1,0:T(8,128)(2,1)S(1)}, u32[]{:S(2)}, u32[]{:S(2)}) collective-permute-start(bf16[96,4096]{1,0:T(8,128)(2,1)} %get-tuple-element.184), channel_id=1, source_target_pairs={{0,8},{4,12},{8,16},{12,20},{16,24},{20,28},{24,0},{28,4},{1,9},{5... | collective-permute-start | bytes 2359304 | tf_op jit(solution)/shard_map/ppermute | solution.py:17
  50.4 19.6 %collective-permute-start.11 = (bf16[96,4096]{1,0:T(8,128)(2,1)}, bf16[96,4096]{1,0:T(8,128)(2,1)}, u32[]{:S(2)}, u32[]{:S(2)}) collective-permute-start(bf16[96,4096]{1,0:T(8,128)(2,1)} %get-tuple-element.183), channel_id=1, source_target_pairs={{0,24},{4,28},{8,0},{12,4},{16,8},{20,12},{24,16},{28,20},{1,25},{... | collective-permute-start | bytes 2359304 | tf_op jit(solution)/shard_map/ppermute | solution.py:17
  53.6 6.6 %collective-permute-start.12 = (bf16[64,1024]{1,0:T(8,128)(2,1)S(1)}, bf16[64,1024]{1,0:T(8,128)(2,1)}, u32[]{:S(2)}, u32[]{:S(2)}) collective-permute-start(bf16[64,1024]{1,0:T(8,128)(2,1)S(1)} %convolution_convert_fusion.2), channel_id=1, source_target_pairs={{0,1},{1,0},{2,3},{3,2},{4,5},{5,4},{6,7},{7,6},{8,9},{9,8},{10,11... | collective-permute-start | bytes 393224 | tf_op jit(solution)/shard_map/ppermute | solution.py:27
  53.7 10.3 %collective-permute-start.13 = (bf16[64,1024]{1,0:T(8,128)(2,1)S(1)}, bf16[64,1024]{1,0:T(8,128)(2,1)}, u32[]{:S(2)}, u32[]{:S(2)}) collective-permute-start(bf16[64,1024]{1,0:T(8,128)(2,1)S(1)} %convolution_convert_fusion.2), channel_id=1, source_target_pairs={{0,2},{1,3},{2,0},{3,1},{4,6},{5,7},{6,4},{7,5},{8,10},{9,11},{10,... | collective-permute-start | bytes 393224 | tf_op jit(solution)/shard_map/ppermute | solution.py:27
  56.1 11.0 %collective-permute-start.14 = (bf16[64,1024]{1,0:T(8,128)(2,1)S(1)}, bf16[64,1024]{1,0:T(8,128)(2,1)}, u32[]{:S(2)}, u32[]{:S(2)}) collective-permute-start(bf16[64,1024]{1,0:T(8,128)(2,1)S(1)} %convolution_convert_fusion.2), channel_id=1, source_target_pairs={{0,3},{1,2},{2,1},{3,0},{4,7},{5,6},{6,5},{7,4},{8,11},{9,10},{10,... | collective-permute-start | bytes 393224 | tf_op jit(solution)/shard_map/ppermute | solution.py:27
  69.9 7.5 %collective-permute-start.17 = (bf16[224,4096]{1,0:T(8,128)(2,1)S(1)}, bf16[224,4096]{1,0:T(8,128)(2,1)S(1)}, u32[]{:S(2)}, u32[]{:S(2)}) collective-permute-start(bf16[224,4096]{1,0:T(8,128)(2,1)S(1)} %bitcast.35), channel_id=1, source_target_pairs={{0,4},{4,0},{8,12},{12,8},{16,20},{20,16},{24,28},{28,24},{1,5},{5... | collective-permute-start | bytes 5505032 | tf_op jit(solution)/shard_map/ppermute | solution.py:22
  69.9 7.5 %collective-permute-start.18 = (bf16[224,4096]{1,0:T(8,128)(2,1)}, bf16[224,4096]{1,0:T(8,128)(2,1)S(1)}, u32[]{:S(2)}, u32[]{:S(2)}) collective-permute-start(bf16[224,4096]{1,0:T(8,128)(2,1)} %bitcast.41), channel_id=1, source_target_pairs={{0,4},{4,0},{8,12},{12,8},{16,20},{20,16},{24,28},{28,24},{1,5},{5... | collective-permute-start | bytes 5505032 | tf_op jit(solution)/shard_map/ppermute | solution.py:22
  70.5 7.0 %copy-start.5 = (bf16[224,4096]{1,0:T(8,128)(2,1)S(1)}, bf16[224,4096]{1,0:T(8,128)(2,1)}, u32[]{:S(2)}) copy-start(bf16[224,4096]{1,0:T(8,128)(2,1)} %copy-done.4) | copy-start | bytes 5505028
  73.8 21.0 %collective-permute-start.15 = (bf16[96,4096]{1,0:T(8,128)(2,1)S(1)}, bf16[96,4096]{1,0:T(8,128)(2,1)S(1)}, u32[]{:S(2)}, u32[]{:S(2)}) collective-permute-start(bf16[96,4096]{1,0:T(8,128)(2,1)S(1)} %get-tuple-element.180), channel_id=1, source_target_pairs={{0,8},{4,12},{8,16},{12,20},{16,24},{20,28},{24,0},{28,4},{1,9},{5... | collective-permute-start | bytes 2359304 | tf_op jit(solution)/shard_map/ppermute | solution.py:17
  74.5 20.4 %collective-permute-start.16 = (bf16[96,4096]{1,0:T(8,128)(2,1)S(1)}, bf16[96,4096]{1,0:T(8,128)(2,1)S(1)}, u32[]{:S(2)}, u32[]{:S(2)}) collective-permute-start(bf16[96,4096]{1,0:T(8,128)(2,1)S(1)} %get-tuple-element.179), channel_id=1, source_target_pairs={{0,24},{4,28},{8,0},{12,4},{16,8},{20,12},{24,16},{28,20},{1,25},{... | collective-permute-start | bytes 2359304 | tf_op jit(solution)/shard_map/ppermute | solution.py:17
  80.6 6.8 %copy-start.6 = (bf16[224,4096]{1,0:T(8,128)(2,1)}, bf16[224,4096]{1,0:T(8,128)(2,1)S(1)}, u32[]{:S(2)}) copy-start(bf16[224,4096]{1,0:T(8,128)(2,1)S(1)} %collective-permute-done.18.refs_9_) | copy-start | bytes 5505028
  87.5 10.9 %copy-start.16 = (f32[64,4096]{1,0:T(8,128)}, f32[64,4096]{1,0:T(8,128)S(1)}, u32[]{:S(2)}) copy-start(f32[64,4096]{1,0:T(8,128)S(1)} %get-tuple-element.135) | copy-start | bytes 3145732
  95.0 13.8 %collective-permute-start.20 = (bf16[64,4096]{1,0:T(8,128)(2,1)S(1)}, bf16[64,4096]{1,0:T(8,128)(2,1)S(1)}, u32[]{:S(2)}, u32[]{:S(2)}) collective-permute-start(bf16[64,4096]{1,0:T(8,128)(2,1)S(1)} %pad_maximum_fusion.10), channel_id=1, source_target_pairs={{0,24},{4,28},{8,0},{12,4},{16,8},{20,12},{24,16},{28,20},{1,25},{... | collective-permute-start | bytes 1572872 | tf_op jit(solution)/shard_map/ppermute | solution.py:17
  98.4 14.0 %collective-permute-start.19 = (bf16[64,4096]{1,0:T(8,128)(2,1)S(1)}, bf16[64,4096]{1,0:T(8,128)(2,1)S(1)}, u32[]{:S(2)}, u32[]{:S(2)}) collective-permute-start(bf16[64,4096]{1,0:T(8,128)(2,1)S(1)} %pad_maximum_fusion.9), channel_id=1, source_target_pairs={{0,8},{4,12},{8,16},{12,20},{16,24},{20,28},{24,0},{28,4},{1,9},{5... | collective-permute-start | bytes 1572872 | tf_op jit(solution)/shard_map/ppermute | solution.py:17
  101.1 13.4 %copy-start.18 = (f32[448,256]{1,0:T(8,128)}, f32[448,256]{1,0:T(8,128)S(1)}, u32[]{:S(2)}) copy-start(f32[448,256]{1,0:T(8,128)S(1)} %get-tuple-element.122.refs_5_) | copy-start | bytes 1376260
  112.5 18.1 %collective-permute-start.23 = (bf16[256,4096]{1,0:T(8,128)(2,1)}, bf16[256,4096]{1,0:T(8,128)(2,1)S(1)}, u32[]{:S(2)}, u32[]{:S(2)}) collective-permute-start(bf16[256,4096]{1,0:T(8,128)(2,1)} %get-tuple-element.121.rows_ref), channel_id=1, source_target_pairs={{0,4},{4,0},{8,12},{12,8},{16,20},{20,16},{24,28},{28,24},{1,5},{5... | collective-permute-start | bytes 6291464 | tf_op jit(solution)/shard_map/ppermute | solution.py:22
  113.5 16.5 %collective-permute-start.22 = (bf16[64,4096]{1,0:T(8,128)(2,1)}, bf16[64,4096]{1,0:T(8,128)(2,1)}, u32[]{:S(2)}, u32[]{:S(2)}) collective-permute-start(bf16[64,4096]{1,0:T(8,128)(2,1)} %add_convert_fusion.2), channel_id=1, source_target_pairs={{0,24},{4,28},{8,0},{12,4},{16,8},{20,12},{24,16},{28,20},{1,25},{... | collective-permute-start | bytes 1572872 | tf_op jit(solution)/shard_map/ppermute | solution.py:17
  114.5 16.0 %collective-permute-start.21 = (bf16[64,4096]{1,0:T(8,128)(2,1)}, bf16[64,4096]{1,0:T(8,128)(2,1)}, u32[]{:S(2)}, u32[]{:S(2)}) collective-permute-start(bf16[64,4096]{1,0:T(8,128)(2,1)} %add_convert_fusion.3), channel_id=1, source_target_pairs={{0,8},{4,12},{8,16},{12,20},{16,24},{20,28},{24,0},{28,4},{1,9},{5... | collective-permute-start | bytes 1572872 | tf_op jit(solution)/shard_map/ppermute | solution.py:17
  130.5 11.1 %collective-permute-start.27 = (bf16[256,4096]{1,0:T(8,128)(2,1)}, bf16[256,4096]{1,0:T(8,128)(2,1)S(1)}, u32[]{:S(2)}, u32[]{:S(2)}) collective-permute-start(bf16[256,4096]{1,0:T(8,128)(2,1)} %get-tuple-element.134.rows_ref), channel_id=1, source_target_pairs={{0,4},{4,0},{8,12},{12,8},{16,20},{20,16},{24,28},{28,24},{1,5},{5... | collective-permute-start | bytes 6291464 | tf_op jit(solution)/shard_map/ppermute | solution.py:22
  131.6 10.0 %collective-permute-start.24 = (bf16[32,4096]{1,0:T(8,128)(2,1)S(1)}, bf16[32,4096]{1,0:T(8,128)(2,1)S(1)}, u32[]{:S(2)}, u32[]{:S(2)}) collective-permute-start(bf16[32,4096]{1,0:T(8,128)(2,1)S(1)} %get-tuple-element.176), channel_id=1, source_target_pairs={{0,8},{4,12},{8,16},{12,20},{16,24},{20,28},{24,0},{28,4},{1,9},{5... | collective-permute-start | bytes 786440 | tf_op jit(solution)/shard_map/ppermute | solution.py:17
  132.2 9.4 %collective-permute-start.25 = (bf16[32,4096]{1,0:T(8,128)(2,1)S(1)}, bf16[32,4096]{1,0:T(8,128)(2,1)S(1)}, u32[]{:S(2)}, u32[]{:S(2)}) collective-permute-start(bf16[32,4096]{1,0:T(8,128)(2,1)S(1)} %get-tuple-element.175), channel_id=1, source_target_pairs={{0,24},{4,28},{8,0},{12,4},{16,8},{20,12},{24,16},{28,20},{1,25},{... | collective-permute-start | bytes 786440 | tf_op jit(solution)/shard_map/ppermute | solution.py:17
  134.9 6.7 %collective-permute-start.26 = (bf16[672,256]{1,0:T(8,128)(2,1)}, bf16[672,256]{1,0:T(8,128)(2,1)S(1)}, u32[]{:S(2)}, u32[]{:S(2)}) collective-permute-start(bf16[672,256]{1,0:T(8,128)(2,1)} %get-tuple-element.133), channel_id=1, source_target_pairs={{0,4},{4,0},{8,12},{12,8},{16,20},{20,16},{24,28},{28,24},{1,5},{5... | collective-permute-start | bytes 1032200 | tf_op jit(solution)/shard_map/ppermute | solution.py:22
  136.3 8.4 %copy-start.30 = (bf16[64,4096]{1,0:T(8,128)(2,1)S(1)}, bf16[64,4096]{1,0:T(8,128)(2,1)}, u32[]{:S(2)}) copy-start(bf16[64,4096]{1,0:T(8,128)(2,1)} %get-tuple-element.139) | copy-start | bytes 1572868
  136.3 12.1 %copy-start.35 = (s32[1,128,2]{1,2,0:T(2,128)S(1)}, s32[1,128,2]{1,2,0:T(2,128)}, u32[]{:S(2)}) copy-start(s32[1,128,2]{1,2,0:T(2,128)} %param.13) | copy-start | bytes 3076
  136.4 12.1 %copy-start.36 = (f32[1,128,2]{1,2,0:T(2,128)S(1)}, f32[1,128,2]{1,2,0:T(2,128)}, u32[]{:S(2)}) copy-start(f32[1,128,2]{1,2,0:T(2,128)} %param.14) | copy-start | bytes 3076
  136.4 12.2 %copy-start.20 = (bf16[224,256]{1,0:T(8,128)(2,1)S(1)}, bf16[224,256]{1,0:T(8,128)(2,1)}, u32[]{:S(2)}) copy-start(bf16[224,256]{1,0:T(8,128)(2,1)} %get-tuple-element.146.hidden_ref) | copy-start | bytes 344068
  141.7 18.8 %collective-permute-start.29 = (bf16[64,4096]{1,0:T(8,128)(2,1)S(1)}, bf16[64,4096]{1,0:T(8,128)(2,1)S(1)}, u32[]{:S(2)}, u32[]{:S(2)}) collective-permute-start(bf16[64,4096]{1,0:T(8,128)(2,1)S(1)} %add_convert_fusion), channel_id=1, source_target_pairs={{0,24},{4,28},{8,0},{12,4},{16,8},{20,12},{24,16},{28,20},{1,25},{... | collective-permute-start | bytes 1572872 | tf_op jit(solution)/shard_map/ppermute | solution.py:17
  144.8 15.7 %collective-permute-start.28 = (bf16[64,4096]{1,0:T(8,128)(2,1)S(1)}, bf16[64,4096]{1,0:T(8,128)(2,1)S(1)}, u32[]{:S(2)}, u32[]{:S(2)}) collective-permute-start(bf16[64,4096]{1,0:T(8,128)(2,1)S(1)} %add_convert_fusion.1), channel_id=1, source_target_pairs={{0,8},{4,12},{8,16},{12,20},{16,24},{20,28},{24,0},{28,4},{1,9},{5... | collective-permute-start | bytes 1572872 | tf_op jit(solution)/shard_map/ppermute | solution.py:17
  144.9 15.6 %collective-permute-start.30 = (bf16[64,1024]{1,0:T(8,128)(2,1)S(1)}, bf16[64,1024]{1,0:T(8,128)(2,1)S(1)}, u32[]{:S(2)}, u32[]{:S(2)}) collective-permute-start(bf16[64,1024]{1,0:T(8,128)(2,1)S(1)} %get-tuple-element.143), channel_id=1, source_target_pairs={{0,1},{1,0},{2,3},{3,2},{4,5},{5,4},{6,7},{7,6},{8,9},{9,8},{10,11... | collective-permute-start | bytes 393224 | tf_op jit(solution)/shard_map/ppermute | solution.py:27
  145.0 15.5 %collective-permute-start.31 = (bf16[64,1024]{1,0:T(8,128)(2,1)S(1)}, bf16[64,1024]{1,0:T(8,128)(2,1)S(1)}, u32[]{:S(2)}, u32[]{:S(2)}) collective-permute-start(bf16[64,1024]{1,0:T(8,128)(2,1)S(1)} %get-tuple-element.144), channel_id=1, source_target_pairs={{0,2},{1,3},{2,0},{3,1},{4,6},{5,7},{6,4},{7,5},{8,10},{9,11},{10,... | collective-permute-start | bytes 393224 | tf_op jit(solution)/shard_map/ppermute | solution.py:27
  147.4 13.0 %collective-permute-start.32 = (bf16[64,1024]{1,0:T(8,128)(2,1)S(1)}, bf16[64,1024]{1,0:T(8,128)(2,1)S(1)}, u32[]{:S(2)}, u32[]{:S(2)}) collective-permute-start(bf16[64,1024]{1,0:T(8,128)(2,1)S(1)} %get-tuple-element.145), channel_id=1, source_target_pairs={{0,3},{1,2},{2,1},{3,0},{4,7},{5,6},{6,5},{7,4},{8,11},{9,10},{10,... | collective-permute-start | bytes 393224 | tf_op jit(solution)/shard_map/ppermute | solution.py:27
  160.7 6.4 %collective-permute-start.33 = (bf16[64,1024]{1,0:T(8,128)(2,1)S(1)}, bf16[64,1024]{1,0:T(8,128)(2,1)S(1)}, u32[]{:S(2)}, u32[]{:S(2)}) collective-permute-start(bf16[64,1024]{1,0:T(8,128)(2,1)S(1)} %get-tuple-element.171), channel_id=1, source_target_pairs={{0,1},{1,0},{2,3},{3,2},{4,5},{5,4},{6,7},{7,6},{8,9},{9,8},{10,11... | collective-permute-start | bytes 393224 | tf_op jit(solution)/shard_map/ppermute | solution.py:27
  161.8 9.4 %collective-permute-start.34 = (bf16[64,1024]{1,0:T(8,128)(2,1)S(1)}, bf16[64,1024]{1,0:T(8,128)(2,1)S(1)}, u32[]{:S(2)}, u32[]{:S(2)}) collective-permute-start(bf16[64,1024]{1,0:T(8,128)(2,1)S(1)} %get-tuple-element.170), channel_id=1, source_target_pairs={{0,2},{1,3},{2,0},{3,1},{4,6},{5,7},{6,4},{7,5},{8,10},{9,11},{10,... | collective-permute-start | bytes 393224 | tf_op jit(solution)/shard_map/ppermute | solution.py:27
  163.2 10.9 %collective-permute-start.35 = (bf16[64,1024]{1,0:T(8,128)(2,1)S(1)}, bf16[64,1024]{1,0:T(8,128)(2,1)S(1)}, u32[]{:S(2)}, u32[]{:S(2)}) collective-permute-start(bf16[64,1024]{1,0:T(8,128)(2,1)S(1)} %get-tuple-element.169), channel_id=1, source_target_pairs={{0,3},{1,2},{2,1},{3,0},{4,7},{5,6},{6,5},{7,4},{8,11},{9,10},{10,... | collective-permute-start | bytes 393224 | tf_op jit(solution)/shard_map/ppermute | solution.py:27
  (25 other events, 79.3 us)

commit v2 on v1

--- a/solution.py
+++ b/solution.py
@@ -135,15 +135,18 @@
                 preferred_element_type=jnp.float32,
             )
         own_ref[:, columns] = term[:CAP]
-        for index, ref in enumerate(far_refs):
-            ref[:, columns] = term[CAP * (index + 1) : CAP * (index + 2)].astype(jnp.bfloat16)
+        start = CAP
+        for ref in far_refs:
+            rows = ref.shape[0]
+            ref[:, columns] = term[start : start + rows].astype(jnp.bfloat16)
+            start += rows
 
 
 def fwd_kernel(*refs):
     wide, behind, ahead, low, high = refs[:5]
     gate_own, up_own, down_own, gate_x, up_x, down_x = refs[5:11]
-    own_ref, behind_ref, ahead_ref, far_ref = refs[11:15]
-    rows, gate, up, down, sems = refs[15:]
+    own_ref, *far_refs = refs[11:16]
+    rows, gate, up, down, sems = refs[16:]
     half = CAP // 2
     rows_in = fetch(whole(wide, behind, ahead) + ((low, 0, half), (high, 0, half)), rows, sems, 0)
     gate_in = fetch(whole(gate_own, gate_x), gate, sems, 5)
@@ -155,13 +158,14 @@
     arrive(up_in)
     hidden = (pre * jax.nn.sigmoid(pre) * times_rows(up[...], rows[...])).astype(jnp.bfloat16)
     arrive(down_in)
-    spread_kernel_part(((hidden, down),), own_ref, (behind_ref, ahead_ref, far_ref))
+    spread_kernel_part(((hidden, down),), own_ref, far_refs)
 
 
 def later_rows(refs):
-    wide, behind, ahead, low, high = refs
+    sent, behind, ahead, low, high = refs
     half = CAP // 2
-    return whole(wide) + (
+    return (
+        (sent, half, CAP),
         (behind, half, CAP),
         (ahead, half, CAP),
         (low, 0, half),
@@ -181,21 +185,48 @@
     keep.wait()
 
 
+def chunk_copies(sources, target, columns, sems):
+    copies = []
+    into = 0
+    for index, (ref, start, rows) in enumerate(sources):
+        copies.append(
+            pltpu.make_async_copy(
+                ref.at[pl.ds(start, rows), columns],
+                target.at[pl.ds(into, rows), columns],
+                sems.at[index],
+            )
+        )
+        into += rows
+    return copies
+
+
 def back_kernel(*refs):
+    pieces = later_rows(refs[:5])
     hidden_grad_ref, gate_own, up_own, gate_x, up_x = refs[5:10]
-    own_ref, behind_ref, ahead_ref, far_ref, first_ref, keep_ref, send_ref, rows_out = refs[10:18]
-    rows, gate, up, sems = refs[18:]
+    block_outs, first_out, keep_out, send_out, rows_out = refs[10:15], *refs[15:19]
+    rows, gate, up, block_own, block_far, hidden_all, in_sems, out_sems, rows_sem = refs[19:]
     units = gate_own.shape[0]
-    rows_in = fetch(later_rows(refs[:5]), rows, sems, 0)
-    gate_in = fetch(whole(gate_own, gate_x), gate, sems, 5)
-    up_in = fetch(whole(up_own, up_x), up, sems, 7)
-    arrive(rows_in)
-    rows_back = pltpu.make_async_copy(rows, rows_out, sems.at[9])
+    width = rows.shape[1]
+    step = width // CHUNKS
+    loads = []
+    for chunk in range(CHUNKS):
+        columns = pl.ds(chunk * step, step)
+        loads.append(
+            chunk_copies(pieces, rows, columns, in_sems.at[chunk, 0])
+            + chunk_copies(whole(gate_own, gate_x), gate, columns, in_sems.at[chunk, 1])
+            + chunk_copies(whole(up_own, up_x), up, columns, in_sems.at[chunk, 2])
+        )
+    for copies in loads:
+        for copy in copies:
+            copy.start()
+    pre_gate, pre_up = 0.0, 0.0
+    for chunk, copies in enumerate(loads):
+        columns = slice(chunk * step, (chunk + 1) * step)
+        arrive(copies)
+        pre_gate = pre_gate + times_rows(gate[:, columns], rows[:, columns])
+        pre_up = pre_up + times_rows(up[:, columns], rows[:, columns])
+    rows_back = pltpu.make_async_copy(rows, rows_out, rows_sem.at[0])
     rows_back.start()
-    arrive(gate_in)
-    pre_gate = times_rows(gate[...], rows[...])
-    arrive(up_in)
-    pre_up = times_rows(up[...], rows[...])
     sigmoid_pre = jax.nn.sigmoid(pre_gate)
     activated = pre_gate * sigmoid_pre
     hidden_grad = hidden_grad_ref[...]
@@ -204,16 +235,46 @@
         hidden_grad * pre_up * sigmoid_pre * (1.0 + pre_gate * (1.0 - sigmoid_pre))
     ).astype(jnp.bfloat16)
     up_grad = (hidden_grad * activated).astype(jnp.bfloat16)
-    first_ref[...] = hidden[:units]
-    keep_ref[:units] = gate_grad[:units]
-    keep_ref[units:] = up_grad[:units]
-    send_ref[:units] = hidden[units:]
-    send_ref[units : 2 * units] = gate_grad[units:]
-    send_ref[2 * units :] = up_grad[units:]
-    spread_kernel_part(
-        ((gate_grad, gate), (up_grad, up)), own_ref, (behind_ref, ahead_ref, far_ref)
-    )
+    ordered = (
+        hidden[:units],
+        gate_grad[:units],
+        up_grad[:units],
+        hidden[units:],
+        gate_grad[units:],
+        up_grad[units:],
+    )
+    for index, array in enumerate(ordered):
+        hidden_all[units * index : units * (index + 1)] = array
+    stores = []
+    for index, (out, start) in enumerate(((first_out, 0), (keep_out, 1), (send_out, 3))):
+        part = pl.ds(units * start, out.shape[0])
+        stores.append(pltpu.make_async_copy(hidden_all.at[part], out, rows_sem.at[index + 1]))
+        stores[-1].start()
+    for chunk in range(CHUNKS):
+        columns = slice(chunk * step, (chunk + 1) * step)
+        term = 0.0
+        for array, weight in ((gate_grad, gate), (up_grad, up)):
+            term = term + lax.dot_general(
+                array,
+                weight[:, columns],
+                (((0,), (0,)), ((), ())),
+                preferred_element_type=jnp.float32,
+            )
+        block_own[:, columns] = term[:CAP]
+        block_far[:, columns] = term[CAP:].astype(jnp.bfloat16)
+        columns = pl.ds(chunk * step, step)
+        start = 0
+        for index, out in enumerate(block_outs):
+            source = block_own if index == 0 else block_far.at[pl.ds(start, out.shape[0])]
+            start += out.shape[0] if index else 0
+            stores.append(
+                pltpu.make_async_copy(
+                    source.at[:, columns], out.at[:, columns], out_sems.at[chunk, index]
+                )
+            )
+            stores[-1].start()
     rows_back.wait()
+    arrive(stores)
 
 
 def weight_kernel(hidden_ref, hidden_x_ref, rows_ref, rows_x_ref, *outs):
@@ -229,13 +290,16 @@
 
 HBM = pl.BlockSpec(memory_space=pltpu.HBM)
 VMEM = pl.BlockSpec(memory_space=pltpu.VMEM)
+CHUNKS = 4
 PARAMS = pltpu.CompilerParams(vmem_limit_bytes=30 * 2**20)
 SMALL = pl.CostEstimate(flops=1, bytes_accessed=1, transcendentals=0)
 
 
 def block_shapes(width):
-    narrow = jax.ShapeDtypeStruct((CAP, width), jnp.bfloat16)
-    return (jax.ShapeDtypeStruct((CAP, width), jnp.float32), narrow, narrow, narrow)
+    sent = (CAP, CAP, CAP // 2, CAP // 2)
+    return (jax.ShapeDtypeStruct((CAP, width), jnp.float32),) + tuple(
+        jax.ShapeDtypeStruct((rows, width), jnp.bfloat16) for rows in sent
+    )
 
 
 def rows_shape(width):
@@ -256,7 +320,7 @@
         fwd_kernel,
         out_shape=block_shapes(width),
         in_specs=[HBM] * 11,
-        out_specs=(VMEM,) * 4,
+        out_specs=(VMEM,) * 5,
         scratch_shapes=scratch(units, width, 3, 11),
         compiler_params=PARAMS,
         cost_estimate=SMALL,
@@ -289,8 +353,18 @@
         back_kernel,
         out_shape=block_shapes(width) + (hidden(1), hidden(2), hidden(3), rows_shape(width)),
         in_specs=[HBM] * 5 + [VMEM] + [HBM] * 4,
-        out_specs=(VMEM,) * 7 + (HBM,),
-        scratch_shapes=scratch(units, width, 2, 10),
+        out_specs=(HBM,) * 9,
+        scratch_shapes=[
+            pltpu.VMEM((4 * CAP, width), jnp.bfloat16),
+            pltpu.VMEM((2 * units, width), jnp.bfloat16),
+            pltpu.VMEM((2 * units, width), jnp.bfloat16),
+            pltpu.VMEM((CAP, width), jnp.float32),
+            pltpu.VMEM((3 * CAP, width), jnp.bfloat16),
+            pltpu.VMEM((6 * units, 4 * CAP), jnp.bfloat16),
+            pltpu.SemaphoreType.DMA((CHUNKS, 3, 5)),
+            pltpu.SemaphoreType.DMA((CHUNKS, 5)),
+            pltpu.SemaphoreType.DMA((4,)),
+        ],
         compiler_params=pltpu.CompilerParams(vmem_limit_bytes=56 * 2**20),
         cost_estimate=SMALL,
     )(*pieces, hidden_grad, *weights)
@@ -298,7 +372,7 @@
 
 def run_weights(units, hidden, hidden_x, rows, rows_x):
     width = rows.shape[1]
-    step = min(width, 512)
+    step = min(width, 1024)
     outs = hidden.shape[0] // units
     held = pl.BlockSpec(hidden.shape, lambda i: (0, 0))
     columns = pl.BlockSpec((rows.shape[0], step), lambda i: (0, i))
@@ -373,8 +447,9 @@
     back_gate, back_slot = routing(back_ids[0], back_weights[0], expert)
     back_pick = picker_of(back_slot)
     grad_tokens = (back_gate[:, None] * upstream[0].astype(jnp.float32)).astype(jnp.bfloat16)
-    one, two, three, held_rows, gate_x, grad_buf = together(
-        *ask_mp(fwd_buf), mirrored(held_rows), other_core(gate_w), pack(back_pick, grad_tokens)
+    held_rows = mirrored(held_rows)
+    one, two, three, gate_x, grad_buf = together(
+        *ask_mp(fwd_buf), other_core(gate_w), pack(back_pick, grad_tokens)
     )
 
     fwd_wide = widen(fwd_buf, (one, two, three), place)
@@ -384,8 +459,9 @@
 
     grad_wide = widen(grad_buf, (one, two, three), place)
     back_buf = pack(back_pick, held_rows)
+    grad_sent = stacked(fwd_behind[:half], grad_wide)
     cw, ccw, one, two, three, up_w, down_w = together(
-        *both_ways(stacked(fwd_behind[:half], grad_wide), stacked(fwd_ahead[half:], grad_wide)),
+        *both_ways(grad_sent, stacked(fwd_ahead[half:], grad_wide)),
         *ask_mp(back_buf),
         up_w,
         down_w,
@@ -395,22 +471,21 @@
     fwd_terms = run_fwd(
         (fwd_wide, fwd_behind, fwd_ahead, cw, ccw), (gate_w, up_w, down_w, gate_x, up_x, down_x)
     )
-    grad_pieces = (grad_wide, cw, ccw)
+    grad_pieces = (grad_sent, cw, ccw)
     back_wide = widen(back_buf, (one, two, three), place ^ 3)
+    back_sent = stacked(cw[half:CAP], back_wide)
     cw, ccw, down_x, up_x, *fwd_terms = together(
-        *both_ways(stacked(cw[half:CAP], back_wide), stacked(ccw[CAP:], back_wide)),
+        *both_ways(back_sent, stacked(ccw[CAP:], back_wide)),
         down_x,
         up_x,
         *fwd_terms,
     )
-    fwd_own, fwd_to_behind, fwd_to_ahead, fwd_to_far = fwd_terms
+    fwd_own, fwd_to_behind, fwd_to_ahead, fwd_low, fwd_high = fwd_terms
 
     hidden_grad, grad_rows = run_grad((*grad_pieces, cw, ccw), (down_w, down_x))
-    back_pieces = (back_wide, cw, ccw)
+    back_pieces = (back_sent, cw, ccw)
     cw, ccw, hidden_grad, grad_rows = together(
-        *both_ways(
-            stacked(cw[half:CAP], fwd_to_far[:half]), stacked(ccw[CAP:], fwd_to_far[half:])
-        ),
+        *both_ways(stacked(cw[half:CAP], fwd_low), stacked(ccw[CAP:], fwd_high)),
         hidden_grad,
         grad_rows,
     )
@@ -421,22 +496,23 @@
         other_core(grad_rows),
         *back_terms,
     )
-    back_own, back_to_behind, back_to_ahead, back_to_far = back_terms[:4]
-    hidden, pair_grads, hidden_send, back_rows = back_terms[4:]
+    back_own, back_to_behind, back_to_ahead, back_low, back_high = back_terms[:5]
+    hidden, pair_grads, hidden_send, back_rows = back_terms[5:]
 
     fwd_total = add_parts(fwd_own, (p0, p1))
     f0, f1, hidden_x, back_rows_x, *fwd_blocks = together(
-        *both_ways(back_to_far[:half], back_to_far[half:]),
+        *both_ways(back_low, back_high),
         other_core(hidden_send),
         other_core(back_rows),
         *split_mp(fwd_total, place),
     )
 
     units = gate_w.shape[0]
-    p0, p1, one, two, three, grad_down = together(
+    p0, p1, one, two, three, grad_down, pair_grads = together(
         *near_with_far(back_to_behind, back_to_ahead, f0, f1),
         *send_mp(fwd_blocks[1:]),
         *run_weights(units, hidden, hidden_x[:units], grad_rows, grad_rows_x),
+        pair_grads,
     )
 
     back_here, *back_sent = split_mp(add_parts(back_own, (p0, p1)), place)

time: 176 us -> 172 us (0.977)
  Pallas kernels: 33.5 us -> 27.2 us
  waiting for transfers between devices: 66.6 us -> 72.6 us
  other arithmetic: 12.5 us -> 7.69 us
    ppermute x15, waiting for transfers between devices: 31.4 us -> 35 us  [along_mp(): return lax.ppermute(array, 'mp', [(i, i ^ flip) for i in range(n)])]
    pallas_call x2, Pallas kernels: 11.8 us -> 8.12 us  [run_weights(): pl.pallas_call(weight_kernel, grid=(width // step,), out_shape=(jax.Shape...]
    pallas_call x1, Pallas kernels: 12.4 us -> 9.67 us  [run_back(): pl.pallas_call(back_kernel, out_shape=block_shapes(width) + (hidden(1), h...]
    ppermute x14, waiting for transfers between devices: 27.2 us -> 29.9 us  [along_y(): lax.ppermute(array, 'expert', [(i, (i + 2 * step) % n) for i in range(n)])]
    select_n x8, other arithmetic: 3.69 us -> 1.34 us  [swapped(): return (jnp.where(flag, second, first), jnp.where(flag, first, second))]
    unnamed x74 -> x62, local copies, waits for them, and re-layouts: 4.81 us -> 6.06 us
  transfers between devices with their start and end apart: 36 -> 36, of which waited for: 17 -> 21; matrix products, arithmetic and copies ran while one was open for 8% -> 6% of each run, Pallas kernels for 19% -> 16%
where the time goes in v2:
time: 172 us; the launch traced here: 171 us
  waiting for transfers between devices  72.6 us (42%)
  starting transfers between devices  49.1 us (29%)
  Pallas kernels  27.2 us (16%)
  other arithmetic  7.69 us (4%)
  local copies, waits for them, and re-layouts  7.67 us (4%)
  matrix products  4.47 us (3%)
  between operations  2.63 us (2%)
    ppermute x15, waiting for transfers between devices, along_mp(): return lax.ppermute(array, 'mp', [(i, i ^ flip) for i in range(n)])  35 us
    ppermute x14, waiting for transfers between devices, along_y(): lax.ppermute(array, 'expert', [(i, (i + 2 * step) % n) for i in range(n)])  29.9 us
    ppermute x14, starting transfers between devices, along_y(): lax.ppermute(array, 'expert', [(i, (i + 2 * step) % n) for i in range(n)])  21.6 us
    ppermute x15, starting transfers between devices, along_mp(): return lax.ppermute(array, 'mp', [(i, i ^ flip) for i in range(n)])  18.7 us
    pallas_call x1, Pallas kernels, run_back(): pl.pallas_call(back_kernel, out_shape=block_shapes(width) + (hidden(1), h...  9.67 us
    pallas_call x2, Pallas kernels, run_weights(): pl.pallas_call(weight_kernel, grid=(width // step,), out_shape=(jax.Shape...  8.12 us
    ppermute x1, starting transfers between devices, mirrored(): lax.ppermute(array, ('section', 'mp'), [(i, last - i) for i in range(last...  7.5 us
    ppermute x1, waiting for transfers between devices, mirrored(): lax.ppermute(array, ('section', 'mp'), [(i, last - i) for i in range(last...  7.46 us
  transfers between devices with their start and end apart: 36, of which 21 were waited for; matrix products, arithmetic and copies ran while one was open for 6% of the time, Pallas kernels for 16%

profile of v2, /device:TPU:32, one launch (start us, length us, event | category | flops | bytes accessed | tf_op | source)
XLA Modules:
  0.0 171.3 jit_solution(13911544675236987686)
XLA Ops:
  2.6 1.1 convolution_convert_fusion.4
  3.7 1.9 %collective-permute-start = (bf16[64,1024]{1,0:T(8,128)(2,1)S(1)}, bf16[64,1024]{1,0:T(8,128)(2,1)S(1)}, u32[]{:S(2)}, u32[]{:S(2)}) collective-permute-start(bf16[64,1024]{1,0:T(8,128)(2,1)S(1)} %convolution_convert_fusion.4), channel_id=1, source_target_pairs={{0,1},{1,0},{2,3},{3,2},{4,5},{5,4},{6,7},{7,6},{8,9},{9,8},{10,11... | collective-permute-start | bytes 393224 | tf_op jit(solution)/shard_map/ppermute | solution.py:27
  5.6 1.5 collective-permute-start.1
  9.5 1.2 convolution_convert_fusion.3
  11.5 5.2 %collective-permute-done.1 = bf16[64,1024]{1,0:T(8,128)(2,1)S(1)} collective-permute-done((bf16[64,1024]{1,0:T(8,128)(2,1)S(1)}, bf16[64,1024]{1,0:T(8,128)(2,1)S(1)}, u32[]{:S(2)}, u32[]{:S(2)}) %collective-permute-start.1) | collective-permute-done | bytes 131104 | tf_op jit(solution)/shard_map/ppermute | solution.py:27
  16.7 3.3 %collective-permute-done.2 = bf16[64,1024]{1,0:T(8,128)(2,1)S(1)} collective-permute-done((bf16[64,1024]{1,0:T(8,128)(2,1)S(1)}, bf16[64,1024]{1,0:T(8,128)(2,1)S(1)}, u32[]{:S(2)}, u32[]{:S(2)}) %collective-permute-start.2) | collective-permute-done | bytes 131104 | tf_op jit(solution)/shard_map/ppermute | solution.py:27
  21.2 1.5 collective-permute-start.4
  22.7 1.7 collective-permute-start.5
  25.1 7.5 %collective-permute-start.9 = (bf16[128,1024]{1,0:T(8,128)(2,1)S(1)}, bf16[128,1024]{1,0:T(8,128)(2,1)S(1)}, u32[]{:S(2)}, u32[]{:S(2)}) collective-permute-start(bf16[128,1024]{1,0:T(8,128)(2,1)S(1)} %dynamic-slice_bitcast_fusion), channel_id=1, source_target_pairs={{0,227},{1,226},{2,225},{3,224},{32,195},{33,194},{34,193},{35,192... | collective-permute-start | bytes 786440 | tf_op jit(solution)/shard_map/ppermute | solution.py:33
  32.6 2.5 %collective-permute-start.7 = (bf16[64,1024]{1,0:T(8,128)(2,1)S(1)}, bf16[64,1024]{1,0:T(8,128)(2,1)S(1)}, u32[]{:S(2)}, u32[]{:S(2)}) collective-permute-start(bf16[64,1024]{1,0:T(8,128)(2,1)S(1)} %convolution_convert_fusion.3), channel_id=1, source_target_pairs={{0,2},{1,3},{2,0},{3,1},{4,6},{5,7},{6,4},{7,5},{8,10},{9,11},{10,... | collective-permute-start | bytes 393224 | tf_op jit(solution)/shard_map/ppermute | solution.py:27
  35.1 7.5 %collective-permute-done.9 = bf16[128,1024]{1,0:T(8,128)(2,1)S(1)} collective-permute-done((bf16[128,1024]{1,0:T(8,128)(2,1)S(1)}, bf16[128,1024]{1,0:T(8,128)(2,1)S(1)}, u32[]{:S(2)}, u32[]{:S(2)}) %collective-permute-start.9) | collective-permute-done | bytes 262176 | tf_op jit(solution)/shard_map/ppermute | solution.py:33
  42.5 1.6 collective-permute-start.8
  44.7 4.2 %collective-permute-done.8 = bf16[64,1024]{1,0:T(8,128)(2,1)S(1)} collective-permute-done((bf16[64,1024]{1,0:T(8,128)(2,1)S(1)}, bf16[64,1024]{1,0:T(8,128)(2,1)S(1)}, u32[]{:S(2)}, u32[]{:S(2)}) %collective-permute-start.8) | collective-permute-done | bytes 131104 | tf_op jit(solution)/shard_map/ppermute | solution.py:27
  49.8 1.3 pad_maximum_fusion.2
  51.4 3.0 %collective-permute-start.11 = (bf16[96,4096]{1,0:T(8,128)(2,1)}, bf16[96,4096]{1,0:T(8,128)(2,1)}, u32[]{:S(2)}, u32[]{:S(2)}) collective-permute-start(bf16[96,4096]{1,0:T(8,128)(2,1)} %get-tuple-element.187), channel_id=1, source_target_pairs={{0,24},{4,28},{8,0},{12,4},{16,8},{20,12},{24,16},{28,20},{1,25},{... | collective-permute-start | bytes 2359304 | tf_op jit(solution)/shard_map/ppermute | solution.py:17
  54.7 2.5 %collective-permute-start.13 = (bf16[64,1024]{1,0:T(8,128)(2,1)S(1)}, bf16[64,1024]{1,0:T(8,128)(2,1)S(1)}, u32[]{:S(2)}, u32[]{:S(2)}) collective-permute-start(bf16[64,1024]{1,0:T(8,128)(2,1)S(1)} %convolution_convert_fusion.2), channel_id=1, source_target_pairs={{0,2},{1,3},{2,0},{3,1},{4,6},{5,7},{6,4},{7,5},{8,10},{9,11},{10,... | collective-permute-start | bytes 393224 | tf_op jit(solution)/shard_map/ppermute | solution.py:27
  58.1 2.9 %collective-permute-done.12 = bf16[64,1024]{1,0:T(8,128)(2,1)S(1)} collective-permute-done((bf16[64,1024]{1,0:T(8,128)(2,1)S(1)}, bf16[64,1024]{1,0:T(8,128)(2,1)S(1)}, u32[]{:S(2)}, u32[]{:S(2)}) %collective-permute-start.12) | collective-permute-done | bytes 131104 | tf_op jit(solution)/shard_map/ppermute | solution.py:27
  61.1 3.8 %collective-permute-done.13 = bf16[64,1024]{1,0:T(8,128)(2,1)S(1)} collective-permute-done((bf16[64,1024]{1,0:T(8,128)(2,1)S(1)}, bf16[64,1024]{1,0:T(8,128)(2,1)S(1)}, u32[]{:S(2)}, u32[]{:S(2)}) %collective-permute-start.13) | collective-permute-done | bytes 131104 | tf_op jit(solution)/shard_map/ppermute | solution.py:27
  64.8 3.1 %collective-permute-done.14 = bf16[64,1024]{1,0:T(8,128)(2,1)} collective-permute-done((bf16[64,1024]{1,0:T(8,128)(2,1)S(1)}, bf16[64,1024]{1,0:T(8,128)(2,1)}, u32[]{:S(2)}, u32[]{:S(2)}) %collective-permute-start.14) | collective-permute-done | bytes 131104 | tf_op jit(solution)/shard_map/ppermute | solution.py:27
  68.0 2.8 %collective-permute-done.10.refs_3_.refs_1_ = bf16[96,4096]{1,0:T(8,128)(2,1)S(1)} collective-permute-done((bf16[96,4096]{1,0:T(8,128)(2,1)}, bf16[96,4096]{1,0:T(8,128)(2,1)S(1)}, u32[]{:S(2)}, u32[]{:S(2)}) %collective-permute-start.10) | collective-permute-done | bytes 786464 | tf_op jit(solution)/shard_map/ppermute | solution.py:17
  71.3 1.1 slice.33
  74.0 3.2 %collective-permute-start.16 = (bf16[96,4096]{1,0:T(8,128)(2,1)S(1)}, bf16[96,4096]{1,0:T(8,128)(2,1)S(1)}, u32[]{:S(2)}, u32[]{:S(2)}) collective-permute-start(bf16[96,4096]{1,0:T(8,128)(2,1)S(1)} %get-tuple-element.183), channel_id=1, source_target_pairs={{0,24},{4,28},{8,0},{12,4},{16,8},{20,12},{24,16},{28,20},{1,25},{... | collective-permute-start | bytes 2359304 | tf_op jit(solution)/shard_map/ppermute | solution.py:17
  78.4 1.0 copy-done.15
  79.5 1.0 copy-done.17
  80.5 6.8 %shard_map.155 = (f32[64,4096]{1,0:T(8,128)S(1)}, bf16[64,4096]{1,0:T(8,128)(2,1)S(1)}, bf16[64,4096]{1,0:T(8,128)(2,1)S(1)}, bf16[32,4096]{1,0:T(8,128)(2,1)S(1)}, bf16[32,4096]{1,0:T(8,128)(2,1)S(1)}) custom-call(bf16[64,4096]{1,0:T(8,128)(2,1)S(1)} %copy-done.10, bf16[64,4096]{1,0:T(8,128)(2,1)S(1)} %copy-done.15, bf16[64,4096]{1,0:T(8,128)(2,1)S(1)} %copy-done.17, ...), custom_call_target="tpu_custom_call" | custom-call | flops 1 | bytes 1 | tf_op jit(solution)/shard_map/pallas_call | solution.py:319
  87.4 7.3 %collective-permute-done.15.refs_3_.refs_1_ = bf16[96,4096]{1,0:T(8,128)(2,1)S(1)} collective-permute-done((bf16[96,4096]{1,0:T(8,128)(2,1)S(1)}, bf16[96,4096]{1,0:T(8,128)(2,1)S(1)}, u32[]{:S(2)}, u32[]{:S(2)}) %collective-permute-start.15) | collective-permute-done | bytes 786464 | tf_op jit(solution)/shard_map/ppermute | solution.py:17
  94.8 3.1 %collective-permute-start.20 = (bf16[64,4096]{1,0:T(8,128)(2,1)S(1)}, bf16[64,4096]{1,0:T(8,128)(2,1)S(1)}, u32[]{:S(2)}, u32[]{:S(2)}) collective-permute-start(bf16[64,4096]{1,0:T(8,128)(2,1)S(1)} %pad_maximum_fusion.8), channel_id=1, source_target_pairs={{0,24},{4,28},{8,0},{12,4},{16,8},{20,12},{24,16},{28,20},{1,25},{... | collective-permute-start | bytes 1572872 | tf_op jit(solution)/shard_map/ppermute | solution.py:17
  98.1 2.6 %shard_map.156 = (f32[448,256]{1,0:T(8,128)S(1)}, bf16[256,4096]{1,0:T(8,128)(2,1)S(1)}) custom-call(bf16[96,4096]{1,0:T(8,128)(2,1)} %get-tuple-element.188.refs_0_, bf16[96,4096]{1,0:T(8,128)(2,1)S(1)} %collective-permute-done.10.refs_3_.refs_1_, bf16[96,4096]{1,0:T(8,128)(2,1)} %collective-permute-done.11.refs_4_.refs_2_, ...), custom_call_target="tpu_custom_call" | custom-call | flops 1 | bytes 1 | tf_op jit(solution)/shard_map/pallas_call | solution.py:332
  100.7 7.6 %collective-permute-done.20.refs_4_ = bf16[64,4096]{1,0:T(8,128)(2,1)S(1)} collective-permute-done((bf16[64,4096]{1,0:T(8,128)(2,1)S(1)}, bf16[64,4096]{1,0:T(8,128)(2,1)S(1)}, u32[]{:S(2)}, u32[]{:S(2)}) %collective-permute-start.20) | collective-permute-done | bytes 524320 | tf_op jit(solution)/shard_map/ppermute | solution.py:17
  108.3 3.6 %collective-permute-done.19.refs_3_ = bf16[64,4096]{1,0:T(8,128)(2,1)S(1)} collective-permute-done((bf16[64,4096]{1,0:T(8,128)(2,1)S(1)}, bf16[64,4096]{1,0:T(8,128)(2,1)S(1)}, u32[]{:S(2)}, u32[]{:S(2)}) %collective-permute-start.19) | collective-permute-done | bytes 524320 | tf_op jit(solution)/shard_map/ppermute | solution.py:17
  112.7 1.9 %collective-permute-start.21 = (bf16[64,4096]{1,0:T(8,128)(2,1)S(1)}, bf16[64,4096]{1,0:T(8,128)(2,1)S(1)}, u32[]{:S(2)}, u32[]{:S(2)}) collective-permute-start(bf16[64,4096]{1,0:T(8,128)(2,1)S(1)} %add_convert_fusion.3), channel_id=1, source_target_pairs={{0,8},{4,12},{8,16},{12,20},{16,24},{20,28},{24,0},{28,4},{1,9},{5... | collective-permute-start | bytes 1572872 | tf_op jit(solution)/shard_map/ppermute | solution.py:17
  114.6 9.7 %shard_map.157 = (f32[64,4096]{1,0:T(8,128)}, bf16[64,4096]{1,0:T(8,128)(2,1)}, bf16[64,4096]{1,0:T(8,128)(2,1)}, bf16[32,4096]{1,0:T(8,128)(2,1)}, bf16[32,4096...) custom-call(bf16[96,4096]{1,0:T(8,128)(2,1)} %copy-done.22, ...), custom_call_target="tpu_custom_call" | custom-call | flops 1 | bytes 1 | tf_op jit(solution)/shard_map/pallas_call | solution.py:352
  124.3 2.2 %collective-permute-done.22 = bf16[64,4096]{1,0:T(8,128)(2,1)S(1)} collective-permute-done((bf16[64,4096]{1,0:T(8,128)(2,1)S(1)}, bf16[64,4096]{1,0:T(8,128)(2,1)S(1)}, u32[]{:S(2)}, u32[]{:S(2)}) %collective-permute-start.22) | collective-permute-done | bytes 524320 | tf_op jit(solution)/shard_map/ppermute | solution.py:17
  126.4 1.7 collective-permute-done.21
  129.9 2.7 %collective-permute-start.25 = (bf16[32,4096]{1,0:T(8,128)(2,1)}, bf16[32,4096]{1,0:T(8,128)(2,1)S(1)}, u32[]{:S(2)}, u32[]{:S(2)}) collective-permute-start(bf16[32,4096]{1,0:T(8,128)(2,1)} %get-tuple-element.139), channel_id=1, source_target_pairs={{0,24},{4,28},{8,0},{12,4},{16,8},{20,12},{24,16},{28,20},{1,25},{... | collective-permute-start | bytes 786440 | tf_op jit(solution)/shard_map/ppermute | solution.py:17
  132.6 1.5 fusion.19
  134.3 4.7 %collective-permute-done.24 = bf16[32,4096]{1,0:T(8,128)(2,1)S(1)} collective-permute-done((bf16[32,4096]{1,0:T(8,128)(2,1)}, bf16[32,4096]{1,0:T(8,128)(2,1)S(1)}, u32[]{:S(2)}, u32[]{:S(2)}) %collective-permute-start.24) | collective-permute-done | bytes 262176 | tf_op jit(solution)/shard_map/ppermute | solution.py:17
  139.1 3.0 %collective-permute-start.29 = (bf16[64,4096]{1,0:T(8,128)(2,1)S(1)}, bf16[64,4096]{1,0:T(8,128)(2,1)S(1)}, u32[]{:S(2)}, u32[]{:S(2)}) collective-permute-start(bf16[64,4096]{1,0:T(8,128)(2,1)S(1)} %add_convert_fusion), channel_id=1, source_target_pairs={{0,24},{4,28},{8,0},{12,4},{16,8},{20,12},{24,16},{28,20},{1,25},{... | collective-permute-start | bytes 1572872 | tf_op jit(solution)/shard_map/ppermute | solution.py:17
  142.3 1.2 collective-permute-start.30
  143.5 2.0 %collective-permute-start.31 = (bf16[64,1024]{1,0:T(8,128)(2,1)S(1)}, bf16[64,1024]{1,0:T(8,128)(2,1)S(1)}, u32[]{:S(2)}, u32[]{:S(2)}) collective-permute-start(bf16[64,1024]{1,0:T(8,128)(2,1)S(1)} %get-tuple-element.151), channel_id=1, source_target_pairs={{0,2},{1,3},{2,0},{3,1},{4,6},{5,7},{6,4},{7,5},{8,10},{9,11},{10,... | collective-permute-start | bytes 393224 | tf_op jit(solution)/shard_map/ppermute | solution.py:27
  146.1 3.0 %shard_map.158 = bf16[224,4096]{1,0:T(8,128)(2,1)} custom-call(bf16[224,256]{1,0:T(8,128)(2,1)S(1)} %copy-done.21, bf16[224,256]{1,0:T(8,128)(2,1)S(1)} %slice.38.hidden_x_ref, bf16[256,4096]{1,0:T(8,128)(2,1)S(1)} %copy-done.12, bf16[256,4096]{1,0:T(8,128)(2,1)S(1)} %collective-permute-done.23.rows_x_ref), custom_call_target="tpu_custom_call" | custom-call | flops 1 | bytes 1 | tf_op jit(solution)/shard_map/pallas_call | solution.py:379
  149.2 4.1 %collective-permute-done.31 = bf16[64,1024]{1,0:T(8,128)(2,1)S(1)} collective-permute-done((bf16[64,1024]{1,0:T(8,128)(2,1)S(1)}, bf16[64,1024]{1,0:T(8,128)(2,1)S(1)}, u32[]{:S(2)}, u32[]{:S(2)}) %collective-permute-start.31) | collective-permute-done | bytes 131104 | tf_op jit(solution)/shard_map/ppermute | solution.py:27
  153.2 2.7 %collective-permute-done.32 = bf16[64,1024]{1,0:T(8,128)(2,1)S(1)} collective-permute-done((bf16[64,1024]{1,0:T(8,128)(2,1)S(1)}, bf16[64,1024]{1,0:T(8,128)(2,1)S(1)}, u32[]{:S(2)}, u32[]{:S(2)}) %collective-permute-start.32) | collective-permute-done | bytes 131104 | tf_op jit(solution)/shard_map/ppermute | solution.py:27
  156.2 1.1 collective-permute-start.33
  157.3 2.1 %collective-permute-start.34 = (bf16[64,1024]{1,0:T(8,128)(2,1)S(1)}, bf16[64,1024]{1,0:T(8,128)(2,1)S(1)}, u32[]{:S(2)}, u32[]{:S(2)}) collective-permute-start(bf16[64,1024]{1,0:T(8,128)(2,1)S(1)} %get-tuple-element.178), channel_id=1, source_target_pairs={{0,2},{1,3},{2,0},{3,1},{4,6},{5,7},{6,4},{7,5},{8,10},{9,11},{10,... | collective-permute-start | bytes 393224 | tf_op jit(solution)/shard_map/ppermute | solution.py:27
  159.8 5.1 %shard_map.159 = (bf16[224,4096]{1,0:T(8,128)(2,1)}, bf16[224,4096]{1,0:T(8,128)(2,1)}) custom-call(bf16[448,256]{1,0:T(8,128)(2,1)S(1)} %copy-done.20, bf16[448,256]{1,0:T(8,128)(2,1)S(1)} %slice.39.hidden_x_ref, bf16[256,4096]{1,0:T(8,128)(2,1)S(1)} %copy-done.13, bf16[256,4096]{1,0:T(8,128)(2,1)} %collective-permute-done.27.rows_x_ref), custom_call_target="tpu_custom_call" | custom-call | flops 1 | bytes 1 | tf_op jit(solution)/shard_map/pallas_call | solution.py:379
  165.9 1.6 collective-permute-done.34
  167.5 2.8 %collective-permute-done.35 = bf16[64,1024]{1,0:T(8,128)(2,1)S(1)} collective-permute-done((bf16[64,1024]{1,0:T(8,128)(2,1)S(1)}, bf16[64,1024]{1,0:T(8,128)(2,1)S(1)}, u32[]{:S(2)}, u32[]{:S(2)}) %collective-permute-start.35) | collective-permute-done | bytes 131104 | tf_op jit(solution)/shard_map/ppermute | solution.py:27
  (144 shorter events, 18.1 us)
Async XLA Ops:
  0.6 24.4 %copy-start = (bf16[1,2,128,1024]{3,2,1,0:T(8,128)(2,1)S(1)}, bf16[1,2,128,1024]{3,2,1,0:T(8,128)(2,1)}, u32[]{:S(2)}) copy-start(bf16[1,2,128,1024]{3,2,1,0:T(8,128)(2,1)} %param.15) | copy-start | bytes 1572868
  0.6 19.3 %collective-permute-start.3 = (bf16[224,4096]{1,0:T(8,128)(2,1)}, bf16[224,4096]{1,0:T(8,128)(2,1)S(1)}, u32[]{:S(2)}, u32[]{:S(2)}) collective-permute-start(bf16[224,4096]{1,0:T(8,128)(2,1)} %bitcast.38), channel_id=1, source_target_pairs={{0,4},{4,0},{8,12},{12,8},{16,20},{20,16},{24,28},{28,24},{1,5},{5... | collective-permute-start | bytes 5505032 | tf_op jit(solution)/shard_map/ppermute | solution.py:22
  3.7 7.8 %collective-permute-start = (bf16[64,1024]{1,0:T(8,128)(2,1)S(1)}, bf16[64,1024]{1,0:T(8,128)(2,1)S(1)}, u32[]{:S(2)}, u32[]{:S(2)}) collective-permute-start(bf16[64,1024]{1,0:T(8,128)(2,1)S(1)} %convolution_convert_fusion.4), channel_id=1, source_target_pairs={{0,1},{1,0},{2,3},{3,2},{4,5},{5,4},{6,7},{7,6},{8,9},{9,8},{10,11... | collective-permute-start | bytes 393224 | tf_op jit(solution)/shard_map/ppermute | solution.py:27
  5.6 11.0 %collective-permute-start.1 = (bf16[64,1024]{1,0:T(8,128)(2,1)S(1)}, bf16[64,1024]{1,0:T(8,128)(2,1)S(1)}, u32[]{:S(2)}, u32[]{:S(2)}) collective-permute-start(bf16[64,1024]{1,0:T(8,128)(2,1)S(1)} %convolution_convert_fusion.4), channel_id=1, source_target_pairs={{0,2},{1,3},{2,0},{3,1},{4,6},{5,7},{6,4},{7,5},{8,10},{9,11},{10,... | collective-permute-start | bytes 393224 | tf_op jit(solution)/shard_map/ppermute | solution.py:27
  7.2 12.8 %collective-permute-start.2 = (bf16[64,1024]{1,0:T(8,128)(2,1)S(1)}, bf16[64,1024]{1,0:T(8,128)(2,1)S(1)}, u32[]{:S(2)}, u32[]{:S(2)}) collective-permute-start(bf16[64,1024]{1,0:T(8,128)(2,1)S(1)} %convolution_convert_fusion.4), channel_id=1, source_target_pairs={{0,3},{1,2},{2,1},{3,0},{4,7},{5,6},{6,5},{7,4},{8,11},{9,10},{10,... | collective-permute-start | bytes 393224 | tf_op jit(solution)/shard_map/ppermute | solution.py:27
  21.2 28.6 %copy-start.9 = (bf16[64,4096]{1,0:T(8,128)(2,1)}, bf16[64,4096]{1,0:T(8,128)(2,1)S(1)}, u32[]{:S(2)}) copy-start(bf16[64,4096]{1,0:T(8,128)(2,1)S(1)} %pad_maximum_fusion.6.refs_0_) | copy-start | bytes 1572868
  21.2 27.7 %collective-permute-start.4 = (bf16[64,4096]{1,0:T(8,128)(2,1)S(1)}, bf16[64,4096]{1,0:T(8,128)(2,1)S(1)}, u32[]{:S(2)}, u32[]{:S(2)}) collective-permute-start(bf16[64,4096]{1,0:T(8,128)(2,1)S(1)} %pad_maximum_fusion.6.refs_0_), channel_id=1, source_target_pairs={{0,8},{4,12},{8,16},{12,20},{16,24},{20,28},{24,0},{28,4},{1,9},{5... | collective-permute-start | bytes 1572872 | tf_op jit(solution)/shard_map/ppermute | solution.py:17
  22.7 26.2 %collective-permute-start.5 = (bf16[64,4096]{1,0:T(8,128)(2,1)S(1)}, bf16[64,4096]{1,0:T(8,128)(2,1)S(1)}, u32[]{:S(2)}, u32[]{:S(2)}) collective-permute-start(bf16[64,4096]{1,0:T(8,128)(2,1)S(1)} %pad_maximum_fusion.6.refs_0_), channel_id=1, source_target_pairs={{0,24},{4,28},{8,0},{12,4},{16,8},{20,12},{24,16},{28,20},{1,25},{... | collective-permute-start | bytes 1572872 | tf_op jit(solution)/shard_map/ppermute | solution.py:17
  25.1 17.4 %collective-permute-start.9 = (bf16[128,1024]{1,0:T(8,128)(2,1)S(1)}, bf16[128,1024]{1,0:T(8,128)(2,1)S(1)}, u32[]{:S(2)}, u32[]{:S(2)}) collective-permute-start(bf16[128,1024]{1,0:T(8,128)(2,1)S(1)} %dynamic-slice_bitcast_fusion), channel_id=1, source_target_pairs={{0,227},{1,226},{2,225},{3,224},{32,195},{33,194},{34,193},{35,192... | collective-permute-start | bytes 786440 | tf_op jit(solution)/shard_map/ppermute | solution.py:33
  32.6 11.6 %collective-permute-start.6 = (bf16[64,1024]{1,0:T(8,128)(2,1)S(1)}, bf16[64,1024]{1,0:T(8,128)(2,1)S(1)}, u32[]{:S(2)}, u32[]{:S(2)}) collective-permute-start(bf16[64,1024]{1,0:T(8,128)(2,1)S(1)} %convolution_convert_fusion.3), channel_id=1, source_target_pairs={{0,1},{1,0},{2,3},{3,2},{4,5},{5,4},{6,7},{7,6},{8,9},{9,8},{10,11... | collective-permute-start | bytes 393224 | tf_op jit(solution)/shard_map/ppermute | solution.py:27
  32.6 12.1 %collective-permute-start.7 = (bf16[64,1024]{1,0:T(8,128)(2,1)S(1)}, bf16[64,1024]{1,0:T(8,128)(2,1)S(1)}, u32[]{:S(2)}, u32[]{:S(2)}) collective-permute-start(bf16[64,1024]{1,0:T(8,128)(2,1)S(1)} %convolution_convert_fusion.3), channel_id=1, source_target_pairs={{0,2},{1,3},{2,0},{3,1},{4,6},{5,7},{6,4},{7,5},{8,10},{9,11},{10,... | collective-permute-start | bytes 393224 | tf_op jit(solution)/shard_map/ppermute | solution.py:27
  42.5 6.3 %collective-permute-start.8 = (bf16[64,1024]{1,0:T(8,128)(2,1)S(1)}, bf16[64,1024]{1,0:T(8,128)(2,1)S(1)}, u32[]{:S(2)}, u32[]{:S(2)}) collective-permute-start(bf16[64,1024]{1,0:T(8,128)(2,1)S(1)} %convolution_convert_fusion.3), channel_id=1, source_target_pairs={{0,3},{1,2},{2,1},{3,0},{4,7},{5,6},{6,5},{7,4},{8,11},{9,10},{10,... | collective-permute-start | bytes 393224 | tf_op jit(solution)/shard_map/ppermute | solution.py:27
  49.8 20.9 %copy-start.1 = (bf16[1,224,4096]{2,1,0:T(8,128)(2,1)S(1)}, bf16[1,224,4096]{2,1,0:T(8,128)(2,1)}, u32[]{:S(2)}) copy-start(bf16[1,224,4096]{2,1,0:T(8,128)(2,1)} %param.23) | copy-start | bytes 5505028
  51.1 19.6 %collective-permute-start.10 = (bf16[96,4096]{1,0:T(8,128)(2,1)}, bf16[96,4096]{1,0:T(8,128)(2,1)S(1)}, u32[]{:S(2)}, u32[]{:S(2)}) collective-permute-start(bf16[96,4096]{1,0:T(8,128)(2,1)} %get-tuple-element.188.refs_0_), channel_id=1, source_target_pairs={{0,8},{4,12},{8,16},{12,20},{16,24},{20,28},{24,0},{28,4},{1,9},{5... | collective-permute-start | bytes 2359304 | tf_op jit(solution)/shard_map/ppermute | solution.py:17
  51.4 19.4 %collective-permute-start.11 = (bf16[96,4096]{1,0:T(8,128)(2,1)}, bf16[96,4096]{1,0:T(8,128)(2,1)}, u32[]{:S(2)}, u32[]{:S(2)}) collective-permute-start(bf16[96,4096]{1,0:T(8,128)(2,1)} %get-tuple-element.187), channel_id=1, source_target_pairs={{0,24},{4,28},{8,0},{12,4},{16,8},{20,12},{24,16},{28,20},{1,25},{... | collective-permute-start | bytes 2359304 | tf_op jit(solution)/shard_map/ppermute | solution.py:17
  54.6 6.5 %collective-permute-start.12 = (bf16[64,1024]{1,0:T(8,128)(2,1)S(1)}, bf16[64,1024]{1,0:T(8,128)(2,1)S(1)}, u32[]{:S(2)}, u32[]{:S(2)}) collective-permute-start(bf16[64,1024]{1,0:T(8,128)(2,1)S(1)} %convolution_convert_fusion.2), channel_id=1, source_target_pairs={{0,1},{1,0},{2,3},{3,2},{4,5},{5,4},{6,7},{7,6},{8,9},{9,8},{10,11... | collective-permute-start | bytes 393224 | tf_op jit(solution)/shard_map/ppermute | solution.py:27
  54.7 10.2 %collective-permute-start.13 = (bf16[64,1024]{1,0:T(8,128)(2,1)S(1)}, bf16[64,1024]{1,0:T(8,128)(2,1)S(1)}, u32[]{:S(2)}, u32[]{:S(2)}) collective-permute-start(bf16[64,1024]{1,0:T(8,128)(2,1)S(1)} %convolution_convert_fusion.2), channel_id=1, source_target_pairs={{0,2},{1,3},{2,0},{3,1},{4,6},{5,7},{6,4},{7,5},{8,10},{9,11},{10,... | collective-permute-start | bytes 393224 | tf_op jit(solution)/shard_map/ppermute | solution.py:27
  57.2 10.8 %collective-permute-start.14 = (bf16[64,1024]{1,0:T(8,128)(2,1)S(1)}, bf16[64,1024]{1,0:T(8,128)(2,1)}, u32[]{:S(2)}, u32[]{:S(2)}) collective-permute-start(bf16[64,1024]{1,0:T(8,128)(2,1)S(1)} %convolution_convert_fusion.2), channel_id=1, source_target_pairs={{0,3},{1,2},{2,1},{3,0},{4,7},{5,6},{6,5},{7,4},{8,11},{9,10},{10,... | collective-permute-start | bytes 393224 | tf_op jit(solution)/shard_map/ppermute | solution.py:27
  70.8 6.4 %collective-permute-start.17 = (bf16[224,4096]{1,0:T(8,128)(2,1)S(1)}, bf16[224,4096]{1,0:T(8,128)(2,1)S(1)}, u32[]{:S(2)}, u32[]{:S(2)}) collective-permute-start(bf16[224,4096]{1,0:T(8,128)(2,1)S(1)} %bitcast.35), channel_id=1, source_target_pairs={{0,4},{4,0},{8,12},{12,8},{16,20},{20,16},{24,28},{28,24},{1,5},{5... | collective-permute-start | bytes 5505032 | tf_op jit(solution)/shard_map/ppermute | solution.py:22
  70.8 6.6 %collective-permute-start.18 = (bf16[224,4096]{1,0:T(8,128)(2,1)}, bf16[224,4096]{1,0:T(8,128)(2,1)S(1)}, u32[]{:S(2)}, u32[]{:S(2)}) collective-permute-start(bf16[224,4096]{1,0:T(8,128)(2,1)} %bitcast.41), channel_id=1, source_target_pairs={{0,4},{4,0},{8,12},{12,8},{16,20},{20,16},{24,28},{28,24},{1,5},{5... | collective-permute-start | bytes 5505032 | tf_op jit(solution)/shard_map/ppermute | solution.py:22
  73.7 13.7 %copy-start.22 = (bf16[96,4096]{1,0:T(8,128)(2,1)}, bf16[96,4096]{1,0:T(8,128)(2,1)S(1)}, u32[]{:S(2)}) copy-start(bf16[96,4096]{1,0:T(8,128)(2,1)S(1)} %get-tuple-element.184.refs_0_) | copy-start | bytes 2359300
  73.7 21.0 %collective-permute-start.15 = (bf16[96,4096]{1,0:T(8,128)(2,1)S(1)}, bf16[96,4096]{1,0:T(8,128)(2,1)S(1)}, u32[]{:S(2)}, u32[]{:S(2)}) collective-permute-start(bf16[96,4096]{1,0:T(8,128)(2,1)S(1)} %get-tuple-element.184.refs_0_), channel_id=1, source_target_pairs={{0,8},{4,12},{8,16},{12,20},{16,24},{20,28},{24,0},{28,4},{1,9},{5... | collective-permute-start | bytes 2359304 | tf_op jit(solution)/shard_map/ppermute | solution.py:17
  74.0 20.7 %collective-permute-start.16 = (bf16[96,4096]{1,0:T(8,128)(2,1)S(1)}, bf16[96,4096]{1,0:T(8,128)(2,1)S(1)}, u32[]{:S(2)}, u32[]{:S(2)}) collective-permute-start(bf16[96,4096]{1,0:T(8,128)(2,1)S(1)} %get-tuple-element.183), channel_id=1, source_target_pairs={{0,24},{4,28},{8,0},{12,4},{16,8},{20,12},{24,16},{28,20},{1,25},{... | collective-permute-start | bytes 2359304 | tf_op jit(solution)/shard_map/ppermute | solution.py:17
  94.8 13.5 %collective-permute-start.20 = (bf16[64,4096]{1,0:T(8,128)(2,1)S(1)}, bf16[64,4096]{1,0:T(8,128)(2,1)S(1)}, u32[]{:S(2)}, u32[]{:S(2)}) collective-permute-start(bf16[64,4096]{1,0:T(8,128)(2,1)S(1)} %pad_maximum_fusion.8), channel_id=1, source_target_pairs={{0,24},{4,28},{8,0},{12,4},{16,8},{20,12},{24,16},{28,20},{1,25},{... | collective-permute-start | bytes 1572872 | tf_op jit(solution)/shard_map/ppermute | solution.py:17
  98.0 13.9 %collective-permute-start.19 = (bf16[64,4096]{1,0:T(8,128)(2,1)S(1)}, bf16[64,4096]{1,0:T(8,128)(2,1)S(1)}, u32[]{:S(2)}, u32[]{:S(2)}) collective-permute-start(bf16[64,4096]{1,0:T(8,128)(2,1)S(1)} %pad_maximum_fusion.7), channel_id=1, source_target_pairs={{0,8},{4,12},{8,16},{12,20},{16,24},{20,28},{24,0},{28,4},{1,9},{5... | collective-permute-start | bytes 1572872 | tf_op jit(solution)/shard_map/ppermute | solution.py:17
  100.7 11.7 %copy-start.11 = (bf16[256,4096]{1,0:T(8,128)(2,1)}, bf16[256,4096]{1,0:T(8,128)(2,1)S(1)}, u32[]{:S(2)}) copy-start(bf16[256,4096]{1,0:T(8,128)(2,1)S(1)} %get-tuple-element.126.rows_ref) | copy-start | bytes 6291460
  100.7 11.7 %copy-start.19 = (f32[448,256]{1,0:T(8,128)}, f32[448,256]{1,0:T(8,128)S(1)}, u32[]{:S(2)}) copy-start(f32[448,256]{1,0:T(8,128)S(1)} %get-tuple-element.127.refs_5_) | copy-start | bytes 1376260
  111.9 16.2 %collective-permute-start.23 = (bf16[256,4096]{1,0:T(8,128)(2,1)S(1)}, bf16[256,4096]{1,0:T(8,128)(2,1)S(1)}, u32[]{:S(2)}, u32[]{:S(2)}) collective-permute-start(bf16[256,4096]{1,0:T(8,128)(2,1)S(1)} %get-tuple-element.126.rows_ref), channel_id=1, source_target_pairs={{0,4},{4,0},{8,12},{12,8},{16,20},{20,16},{24,28},{28,24},{1,5},{5... | collective-permute-start | bytes 6291464 | tf_op jit(solution)/shard_map/ppermute | solution.py:22
  112.0 14.4 %collective-permute-start.22 = (bf16[64,4096]{1,0:T(8,128)(2,1)S(1)}, bf16[64,4096]{1,0:T(8,128)(2,1)S(1)}, u32[]{:S(2)}, u32[]{:S(2)}) collective-permute-start(bf16[64,4096]{1,0:T(8,128)(2,1)S(1)} %add_convert_fusion.2), channel_id=1, source_target_pairs={{0,24},{4,28},{8,0},{12,4},{16,8},{20,12},{24,16},{28,20},{1,25},{... | collective-permute-start | bytes 1572872 | tf_op jit(solution)/shard_map/ppermute | solution.py:17
  112.7 15.5 %collective-permute-start.21 = (bf16[64,4096]{1,0:T(8,128)(2,1)S(1)}, bf16[64,4096]{1,0:T(8,128)(2,1)S(1)}, u32[]{:S(2)}, u32[]{:S(2)}) collective-permute-start(bf16[64,4096]{1,0:T(8,128)(2,1)S(1)} %add_convert_fusion.3), channel_id=1, source_target_pairs={{0,8},{4,12},{8,16},{12,20},{16,24},{20,28},{24,0},{28,4},{1,9},{5... | collective-permute-start | bytes 1572872 | tf_op jit(solution)/shard_map/ppermute | solution.py:17
  128.9 10.2 %collective-permute-start.27 = (bf16[256,4096]{1,0:T(8,128)(2,1)}, bf16[256,4096]{1,0:T(8,128)(2,1)}, u32[]{:S(2)}, u32[]{:S(2)}) collective-permute-start(bf16[256,4096]{1,0:T(8,128)(2,1)} %get-tuple-element.141.rows_ref), channel_id=1, source_target_pairs={{0,4},{4,0},{8,12},{12,8},{16,20},{20,16},{24,28},{28,24},{1,5},{5... | collective-permute-start | bytes 6291464 | tf_op jit(solution)/shard_map/ppermute | solution.py:22
  128.9 10.1 %collective-permute-start.26 = (bf16[672,256]{1,0:T(8,128)(2,1)}, bf16[672,256]{1,0:T(8,128)(2,1)S(1)}, u32[]{:S(2)}, u32[]{:S(2)}) collective-permute-start(bf16[672,256]{1,0:T(8,128)(2,1)} %get-tuple-element.140), channel_id=1, source_target_pairs={{0,4},{4,0},{8,12},{12,8},{16,20},{20,16},{24,28},{28,24},{1,5},{5... | collective-permute-start | bytes 1032200 | tf_op jit(solution)/shard_map/ppermute | solution.py:22
  129.4 9.6 %collective-permute-start.24 = (bf16[32,4096]{1,0:T(8,128)(2,1)}, bf16[32,4096]{1,0:T(8,128)(2,1)S(1)}, u32[]{:S(2)}, u32[]{:S(2)}) collective-permute-start(bf16[32,4096]{1,0:T(8,128)(2,1)} %get-tuple-element.138), channel_id=1, source_target_pairs={{0,8},{4,12},{8,16},{12,20},{16,24},{20,28},{24,0},{28,4},{1,9},{5... | collective-permute-start | bytes 786440 | tf_op jit(solution)/shard_map/ppermute | solution.py:17
  129.9 9.1 %collective-permute-start.25 = (bf16[32,4096]{1,0:T(8,128)(2,1)}, bf16[32,4096]{1,0:T(8,128)(2,1)S(1)}, u32[]{:S(2)}, u32[]{:S(2)}) collective-permute-start(bf16[32,4096]{1,0:T(8,128)(2,1)} %get-tuple-element.139), channel_id=1, source_target_pairs={{0,24},{4,28},{8,0},{12,4},{16,8},{20,12},{24,16},{28,20},{1,25},{... | collective-permute-start | bytes 786440 | tf_op jit(solution)/shard_map/ppermute | solution.py:17
  134.2 11.7 %copy-start.29 = (s32[1,128,2]{1,2,0:T(2,128)S(1)}, s32[1,128,2]{1,2,0:T(2,128)}, u32[]{:S(2)}) copy-start(s32[1,128,2]{1,2,0:T(2,128)} %param.13) | copy-start | bytes 3076
  134.2 11.7 %copy-start.30 = (f32[1,128,2]{1,2,0:T(2,128)S(1)}, f32[1,128,2]{1,2,0:T(2,128)}, u32[]{:S(2)}) copy-start(f32[1,128,2]{1,2,0:T(2,128)} %param.14) | copy-start | bytes 3076
  134.3 11.8 %copy-start.12 = (bf16[256,4096]{1,0:T(8,128)(2,1)S(1)}, bf16[256,4096]{1,0:T(8,128)(2,1)}, u32[]{:S(2)}) copy-start(bf16[256,4096]{1,0:T(8,128)(2,1)} %copy-done.11) | copy-start | bytes 6291460
  134.3 11.8 %copy-start.21 = (bf16[224,256]{1,0:T(8,128)(2,1)S(1)}, bf16[224,256]{1,0:T(8,128)(2,1)}, u32[]{:S(2)}) copy-start(bf16[224,256]{1,0:T(8,128)(2,1)} %get-tuple-element.153.hidden_ref) | copy-start | bytes 344068
  139.1 16.8 %collective-permute-start.29 = (bf16[64,4096]{1,0:T(8,128)(2,1)S(1)}, bf16[64,4096]{1,0:T(8,128)(2,1)S(1)}, u32[]{:S(2)}, u32[]{:S(2)}) collective-permute-start(bf16[64,4096]{1,0:T(8,128)(2,1)S(1)} %add_convert_fusion), channel_id=1, source_target_pairs={{0,24},{4,28},{8,0},{12,4},{16,8},{20,12},{24,16},{28,20},{1,25},{... | collective-permute-start | bytes 1572872 | tf_op jit(solution)/shard_map/ppermute | solution.py:17
  142.2 13.7 %collective-permute-start.28 = (bf16[64,4096]{1,0:T(8,128)(2,1)S(1)}, bf16[64,4096]{1,0:T(8,128)(2,1)S(1)}, u32[]{:S(2)}, u32[]{:S(2)}) collective-permute-start(bf16[64,4096]{1,0:T(8,128)(2,1)S(1)} %add_convert_fusion.1), channel_id=1, source_target_pairs={{0,8},{4,12},{8,16},{12,20},{16,24},{20,28},{24,0},{28,4},{1,9},{5... | collective-permute-start | bytes 1572872 | tf_op jit(solution)/shard_map/ppermute | solution.py:17
  142.3 6.8 %collective-permute-start.30 = (bf16[64,1024]{1,0:T(8,128)(2,1)S(1)}, bf16[64,1024]{1,0:T(8,128)(2,1)S(1)}, u32[]{:S(2)}, u32[]{:S(2)}) collective-permute-start(bf16[64,1024]{1,0:T(8,128)(2,1)S(1)} %get-tuple-element.150), channel_id=1, source_target_pairs={{0,1},{1,0},{2,3},{3,2},{4,5},{5,4},{6,7},{7,6},{8,9},{9,8},{10,11... | collective-permute-start | bytes 393224 | tf_op jit(solution)/shard_map/ppermute | solution.py:27
  143.5 9.8 %collective-permute-start.31 = (bf16[64,1024]{1,0:T(8,128)(2,1)S(1)}, bf16[64,1024]{1,0:T(8,128)(2,1)S(1)}, u32[]{:S(2)}, u32[]{:S(2)}) collective-permute-start(bf16[64,1024]{1,0:T(8,128)(2,1)S(1)} %get-tuple-element.151), channel_id=1, source_target_pairs={{0,2},{1,3},{2,0},{3,1},{4,6},{5,7},{6,4},{7,5},{8,10},{9,11},{10,... | collective-permute-start | bytes 393224 | tf_op jit(solution)/shard_map/ppermute | solution.py:27
  145.5 10.5 %collective-permute-start.32 = (bf16[64,1024]{1,0:T(8,128)(2,1)S(1)}, bf16[64,1024]{1,0:T(8,128)(2,1)S(1)}, u32[]{:S(2)}, u32[]{:S(2)}) collective-permute-start(bf16[64,1024]{1,0:T(8,128)(2,1)S(1)} %get-tuple-element.152), channel_id=1, source_target_pairs={{0,3},{1,2},{2,1},{3,0},{4,7},{5,6},{6,5},{7,4},{8,11},{9,10},{10,... | collective-permute-start | bytes 393224 | tf_op jit(solution)/shard_map/ppermute | solution.py:27
  149.1 10.7 %copy-start.13 = (bf16[256,4096]{1,0:T(8,128)(2,1)S(1)}, bf16[256,4096]{1,0:T(8,128)(2,1)}, u32[]{:S(2)}) copy-start(bf16[256,4096]{1,0:T(8,128)(2,1)} %get-tuple-element.141.rows_ref) | copy-start | bytes 6291460
  149.1 10.7 %copy-start.20 = (bf16[448,256]{1,0:T(8,128)(2,1)S(1)}, bf16[448,256]{1,0:T(8,128)(2,1)}, u32[]{:S(2)}) copy-start(bf16[448,256]{1,0:T(8,128)(2,1)} %get-tuple-element.163.hidden_ref) | copy-start | bytes 688132
  156.2 9.7 %collective-permute-start.33 = (bf16[64,1024]{1,0:T(8,128)(2,1)S(1)}, bf16[64,1024]{1,0:T(8,128)(2,1)S(1)}, u32[]{:S(2)}, u32[]{:S(2)}) collective-permute-start(bf16[64,1024]{1,0:T(8,128)(2,1)S(1)} %get-tuple-element.179), channel_id=1, source_target_pairs={{0,1},{1,0},{2,3},{3,2},{4,5},{5,4},{6,7},{7,6},{8,9},{9,8},{10,11... | collective-permute-start | bytes 393224 | tf_op jit(solution)/shard_map/ppermute | solution.py:27
  157.3 10.2 %collective-permute-start.34 = (bf16[64,1024]{1,0:T(8,128)(2,1)S(1)}, bf16[64,1024]{1,0:T(8,128)(2,1)S(1)}, u32[]{:S(2)}, u32[]{:S(2)}) collective-permute-start(bf16[64,1024]{1,0:T(8,128)(2,1)S(1)} %get-tuple-element.178), channel_id=1, source_target_pairs={{0,2},{1,3},{2,0},{3,1},{4,6},{5,7},{6,4},{7,5},{8,10},{9,11},{10,... | collective-permute-start | bytes 393224 | tf_op jit(solution)/shard_map/ppermute | solution.py:27
  159.4 11.0 %collective-permute-start.35 = (bf16[64,1024]{1,0:T(8,128)(2,1)S(1)}, bf16[64,1024]{1,0:T(8,128)(2,1)S(1)}, u32[]{:S(2)}, u32[]{:S(2)}) collective-permute-start(bf16[64,1024]{1,0:T(8,128)(2,1)S(1)} %get-tuple-element.177), channel_id=1, source_target_pairs={{0,3},{1,2},{2,1},{3,0},{4,7},{5,6},{6,5},{7,4},{8,11},{9,10},{10,... | collective-permute-start | bytes 393224 | tf_op jit(solution)/shard_map/ppermute | solution.py:27
  (19 other events, 72.8 us)

commit v3 on v2

--- a/solution.py
+++ b/solution.py
@@ -453,31 +453,31 @@
     )
 
     fwd_wide = widen(fwd_buf, (one, two, three), place)
-    fwd_behind, fwd_ahead, one, two, three, held_rows = together(
-        *both_ways(fwd_wide, fwd_wide), *ask_mp(grad_buf), held_rows
+    back_buf, one, two, three = together(pack(back_pick, held_rows), *ask_mp(grad_buf))
+    back_one, fwd_behind, fwd_ahead, one, two, three, back_buf = together(
+        along_mp(back_buf, 1), *both_ways(fwd_wide, fwd_wide), one, two, three, back_buf
     )
 
     grad_wide = widen(grad_buf, (one, two, three), place)
-    back_buf = pack(back_pick, held_rows)
     grad_sent = stacked(fwd_behind[:half], grad_wide)
-    cw, ccw, one, two, three, up_w, down_w = together(
+    cw, ccw, two, three, up_x, down_w = together(
         *both_ways(grad_sent, stacked(fwd_ahead[half:], grad_wide)),
-        *ask_mp(back_buf),
-        up_w,
+        *(along_mp(back_buf, flip) for flip in (2, 3)),
+        other_core(up_w),
         down_w,
     )
-
-    up_x, down_x = (other_core(up_w), other_core(down_w))
+    one = back_one
+
+    down_x = other_core(down_w)
     fwd_terms = run_fwd(
         (fwd_wide, fwd_behind, fwd_ahead, cw, ccw), (gate_w, up_w, down_w, gate_x, up_x, down_x)
     )
     grad_pieces = (grad_sent, cw, ccw)
     back_wide = widen(back_buf, (one, two, three), place ^ 3)
     back_sent = stacked(cw[half:CAP], back_wide)
-    cw, ccw, down_x, up_x, *fwd_terms = together(
+    cw, ccw, down_x, *fwd_terms = together(
         *both_ways(back_sent, stacked(ccw[CAP:], back_wide)),
         down_x,
-        up_x,
         *fwd_terms,
     )
     fwd_own, fwd_to_behind, fwd_to_ahead, fwd_low, fwd_high = fwd_terms

time: 172 us -> 168 us (0.977)
  local copies, waits for them, and re-layouts: 7.67 us -> 3.37 us
  starting transfers between devices: 49.1 us -> 46.9 us
  other arithmetic: 7.69 us -> 9.79 us
    ppermute x1, waiting for transfers between devices: 7.46 us -> 0.39 us  [mirrored(): lax.ppermute(array, ('section', 'mp'), [(i, last - i) for i in range(last...]
    ppermute x14, waiting for transfers between devices: 29.9 us -> 36.1 us  [along_y(): lax.ppermute(array, 'expert', [(i, (i + 2 * step) % n) for i in range(n)])]
    unnamed x62 -> x60, local copies, waits for them, and re-layouts: 6.06 us -> 1.81 us
    ppermute x15, waiting for transfers between devices: 35 us -> 37.7 us  [along_mp(): return lax.ppermute(array, 'mp', [(i, i ^ flip) for i in range(n)])]
    ppermute x15, starting transfers between devices: 18.7 us -> 16.7 us  [along_mp(): return lax.ppermute(array, 'mp', [(i, i ^ flip) for i in range(n)])]
  transfers between devices with their start and end apart: 36 -> 36, of which waited for: 21 -> 19; matrix products, arithmetic and copies ran while one was open for 6% -> 8% of each run, Pallas kernels for 16% -> 16%
where the time goes in v3:
time: 168 us
  waiting for transfers between devices  74.2 us (44%)
  starting transfers between devices  46.9 us (28%)
  Pallas kernels  27 us (16%)
  other arithmetic  9.79 us (6%)
  matrix products  3.53 us (2%)
  local copies, waits for them, and re-layouts  3.37 us (2%)
  between operations  2.68 us (2%)
    ppermute x15, waiting for transfers between devices, along_mp(): return lax.ppermute(array, 'mp', [(i, i ^ flip) for i in range(n)])  37.7 us
    ppermute x14, waiting for transfers between devices, along_y(): lax.ppermute(array, 'expert', [(i, (i + 2 * step) % n) for i in range(n)])  36.1 us
    ppermute x14, starting transfers between devices, along_y(): lax.ppermute(array, 'expert', [(i, (i + 2 * step) % n) for i in range(n)])  21.7 us
    ppermute x15, starting transfers between devices, along_mp(): return lax.ppermute(array, 'mp', [(i, i ^ flip) for i in range(n)])  16.7 us
    pallas_call x1, Pallas kernels, run_back(): pl.pallas_call(back_kernel, out_shape=block_shapes(width) + (hidden(1), h...  9.69 us
    pallas_call x2, Pallas kernels, run_weights(): pl.pallas_call(weight_kernel, grid=(width // step,), out_shape=(jax.Shape...  8.12 us
    ppermute x1, starting transfers between devices, mirrored(): lax.ppermute(array, ('section', 'mp'), [(i, last - i) for i in range(last...  7.78 us
    pallas_call x1, Pallas kernels, run_fwd(): pl.pallas_call(fwd_kernel, out_shape=block_shapes(width), in_specs=[HBM]...  6.6 us
  transfers between devices with their start and end apart: 36, of which 19 were waited for; matrix products, arithmetic and copies ran while one was open for 8% of the time, Pallas kernels for 16%

profile of v3, /device:TPU:32, one launch (start us, length us, event | category | flops | bytes accessed | tf_op | source)
XLA Modules:
  0.0 167.5 jit_solution(7244188841336592739)
XLA Ops:
  2.6 1.1 convolution_convert_fusion.4
  3.7 1.9 %collective-permute-start.1 = (bf16[64,1024]{1,0:T(8,128)(2,1)S(1)}, bf16[64,1024]{1,0:T(8,128)(2,1)S(1)}, u32[]{:S(2)}, u32[]{:S(2)}) collective-permute-start(bf16[64,1024]{1,0:T(8,128)(2,1)S(1)} %convolution_convert_fusion.4), channel_id=1, source_target_pairs={{0,1},{1,0},{2,3},{3,2},{4,5},{5,4},{6,7},{7,6},{8,9},{9,8},{10,11... | collective-permute-start | bytes 393224 | tf_op jit(solution)/shard_map/ppermute | solution.py:27
  5.6 1.5 collective-permute-start.2
  8.3 7.8 %collective-permute-start = (bf16[128,1024]{1,0:T(8,128)(2,1)S(1)}, bf16[128,1024]{1,0:T(8,128)(2,1)S(1)}, u32[]{:S(2)}, u32[]{:S(2)}) collective-permute-start(bf16[128,1024]{1,0:T(8,128)(2,1)S(1)} %dynamic-slice_bitcast_fusion), channel_id=1, source_target_pairs={{0,227},{1,226},{2,225},{3,224},{32,195},{33,194},{34,193},{35,192... | collective-permute-start | bytes 786440 | tf_op jit(solution)/shard_map/ppermute | solution.py:33
  18.2 1.8 %collective-permute-done.3 = bf16[64,1024]{1,0:T(8,128)(2,1)} collective-permute-done((bf16[64,1024]{1,0:T(8,128)(2,1)S(1)}, bf16[64,1024]{1,0:T(8,128)(2,1)}, u32[]{:S(2)}, u32[]{:S(2)}) %collective-permute-start.3) | collective-permute-done | bytes 131104 | tf_op jit(solution)/shard_map/ppermute | solution.py:27
  20.0 1.3 broadcast_select_fusion.15
  21.5 3.0 %collective-permute-start.10 = (bf16[64,4096]{1,0:T(8,128)(2,1)S(1)}, bf16[64,4096]{1,0:T(8,128)(2,1)S(1)}, u32[]{:S(2)}, u32[]{:S(2)}) collective-permute-start(bf16[64,4096]{1,0:T(8,128)(2,1)S(1)} %pad_maximum_fusion.6.refs_0_), channel_id=1, source_target_pairs={{0,24},{4,28},{8,0},{12,4},{16,8},{20,12},{24,16},{28,20},{1,25},{... | collective-permute-start | bytes 1572872 | tf_op jit(solution)/shard_map/ppermute | solution.py:17
  24.6 3.1 %collective-permute-start.6 = (bf16[64,1024]{1,0:T(8,128)(2,1)S(1)}, bf16[64,1024]{1,0:T(8,128)(2,1)S(1)}, u32[]{:S(2)}, u32[]{:S(2)}) collective-permute-start(bf16[64,1024]{1,0:T(8,128)(2,1)S(1)} %convolution_convert_fusion.2), channel_id=1, source_target_pairs={{0,2},{1,3},{2,0},{3,1},{4,6},{5,7},{6,4},{7,5},{8,10},{9,11},{10,... | collective-permute-start | bytes 393224 | tf_op jit(solution)/shard_map/ppermute | solution.py:27
  28.0 1.0 collective-permute-start.7
  29.2 1.8 %collective-permute-done.5 = bf16[64,1024]{1,0:T(8,128)(2,1)S(1)} collective-permute-done((bf16[64,1024]{1,0:T(8,128)(2,1)S(1)}, bf16[64,1024]{1,0:T(8,128)(2,1)S(1)}, u32[]{:S(2)}, u32[]{:S(2)}) %collective-permute-start.5) | collective-permute-done | bytes 131104 | tf_op jit(solution)/shard_map/ppermute | solution.py:27
  31.0 5.2 %collective-permute-done.6 = bf16[64,1024]{1,0:T(8,128)(2,1)S(1)} collective-permute-done((bf16[64,1024]{1,0:T(8,128)(2,1)S(1)}, bf16[64,1024]{1,0:T(8,128)(2,1)S(1)}, u32[]{:S(2)}, u32[]{:S(2)}) %collective-permute-start.6) | collective-permute-done | bytes 131104 | tf_op jit(solution)/shard_map/ppermute | solution.py:27
  36.2 2.8 %collective-permute-done.7 = bf16[64,1024]{1,0:T(8,128)(2,1)S(1)} collective-permute-done((bf16[64,1024]{1,0:T(8,128)(2,1)S(1)}, bf16[64,1024]{1,0:T(8,128)(2,1)S(1)}, u32[]{:S(2)}, u32[]{:S(2)}) %collective-permute-start.7) | collective-permute-done | bytes 131104 | tf_op jit(solution)/shard_map/ppermute | solution.py:27
  39.0 5.0 %collective-permute-done.8 = bf16[64,1024]{1,0:T(8,128)(2,1)S(1)} collective-permute-done((bf16[64,1024]{1,0:T(8,128)(2,1)S(1)}, bf16[64,1024]{1,0:T(8,128)(2,1)S(1)}, u32[]{:S(2)}, u32[]{:S(2)}) %collective-permute-start.8) | collective-permute-done | bytes 131104 | tf_op jit(solution)/shard_map/ppermute | solution.py:27
  45.1 1.3 pad_maximum_fusion.2
  46.8 2.8 %collective-permute-start.12 = (bf16[96,4096]{1,0:T(8,128)(2,1)}, bf16[96,4096]{1,0:T(8,128)(2,1)}, u32[]{:S(2)}, u32[]{:S(2)}) collective-permute-start(bf16[96,4096]{1,0:T(8,128)(2,1)} %get-tuple-element.193), channel_id=1, source_target_pairs={{0,24},{4,28},{8,0},{12,4},{16,8},{20,12},{24,16},{28,20},{1,25},{... | collective-permute-start | bytes 2359304 | tf_op jit(solution)/shard_map/ppermute | solution.py:17
  49.6 1.0 collective-permute-start.13
  51.2 7.1 %collective-permute-done.13 = bf16[64,1024]{1,0:T(8,128)(2,1)S(1)} collective-permute-done((bf16[64,1024]{1,0:T(8,128)(2,1)S(1)}, bf16[64,1024]{1,0:T(8,128)(2,1)S(1)}, u32[]{:S(2)}, u32[]{:S(2)}) %collective-permute-start.13) | collective-permute-done | bytes 131104 | tf_op jit(solution)/shard_map/ppermute | solution.py:27
  58.3 2.6 %collective-permute-done.14 = bf16[64,1024]{1,0:T(8,128)(2,1)} collective-permute-done((bf16[64,1024]{1,0:T(8,128)(2,1)S(1)}, bf16[64,1024]{1,0:T(8,128)(2,1)}, u32[]{:S(2)}, u32[]{:S(2)}) %collective-permute-start.14) | collective-permute-done | bytes 131104 | tf_op jit(solution)/shard_map/ppermute | solution.py:27
  60.9 4.3 %collective-permute-done.11.refs_3_.refs_1_ = bf16[96,4096]{1,0:T(8,128)(2,1)S(1)} collective-permute-done((bf16[96,4096]{1,0:T(8,128)(2,1)}, bf16[96,4096]{1,0:T(8,128)(2,1)S(1)}, u32[]{:S(2)}, u32[]{:S(2)}) %collective-permute-start.11) | collective-permute-done | bytes 786464 | tf_op jit(solution)/shard_map/ppermute | solution.py:17
  65.2 1.0 slice.33
  66.3 1.0 broadcast_select_fusion.9
  67.6 1.8 %collective-permute-start.16 = (bf16[96,4096]{1,0:T(8,128)(2,1)S(1)}, bf16[96,4096]{1,0:T(8,128)(2,1)S(1)}, u32[]{:S(2)}, u32[]{:S(2)}) collective-permute-start(bf16[96,4096]{1,0:T(8,128)(2,1)S(1)} %get-tuple-element.190.refs_0_), channel_id=1, source_target_pairs={{0,8},{4,12},{8,16},{12,20},{16,24},{20,28},{24,0},{28,4},{1,9},{5... | collective-permute-start | bytes 2359304 | tf_op jit(solution)/shard_map/ppermute | solution.py:17
  69.4 1.7 %collective-permute-start.17 = (bf16[96,4096]{1,0:T(8,128)(2,1)S(1)}, bf16[96,4096]{1,0:T(8,128)(2,1)S(1)}, u32[]{:S(2)}, u32[]{:S(2)}) collective-permute-start(bf16[96,4096]{1,0:T(8,128)(2,1)S(1)} %get-tuple-element.189), channel_id=1, source_target_pairs={{0,24},{4,28},{8,0},{12,4},{16,8},{20,12},{24,16},{28,20},{1,25},{... | collective-permute-start | bytes 2359304 | tf_op jit(solution)/shard_map/ppermute | solution.py:17
  71.1 6.6 %shard_map.155 = (f32[64,4096]{1,0:T(8,128)S(1)}, bf16[64,4096]{1,0:T(8,128)(2,1)S(1)}, bf16[64,4096]{1,0:T(8,128)(2,1)S(1)}, bf16[32,4096]{1,0:T(8,128)(2,1)S(1)}, bf16[32,4096]{1,0:T(8,128)(2,1)S(1)}) custom-call(bf16[64,4096]{1,0:T(8,128)(2,1)S(1)} %copy-done.8, bf16[64,4096]{1,0:T(8,128)(2,1)S(1)} %copy-done.15, bf16[64,4096]{1,0:T(8,128)(2,1)S(1)} %copy-done.13, ...), custom_call_target="tpu_custom_call" | custom-call | flops 1 | bytes 1 | tf_op jit(solution)/shard_map/pallas_call | solution.py:319
  77.8 11.3 %collective-permute-done.16.refs_3_.refs_1_ = bf16[96,4096]{1,0:T(8,128)(2,1)S(1)} collective-permute-done((bf16[96,4096]{1,0:T(8,128)(2,1)S(1)}, bf16[96,4096]{1,0:T(8,128)(2,1)S(1)}, u32[]{:S(2)}, u32[]{:S(2)}) %collective-permute-start.16) | collective-permute-done | bytes 786464 | tf_op jit(solution)/shard_map/ppermute | solution.py:17
  89.2 3.1 %collective-permute-start.20 = (bf16[64,4096]{1,0:T(8,128)(2,1)S(1)}, bf16[64,4096]{1,0:T(8,128)(2,1)S(1)}, u32[]{:S(2)}, u32[]{:S(2)}) collective-permute-start(bf16[64,4096]{1,0:T(8,128)(2,1)S(1)} %pad_maximum_fusion.8), channel_id=1, source_target_pairs={{0,24},{4,28},{8,0},{12,4},{16,8},{20,12},{24,16},{28,20},{1,25},{... | collective-permute-start | bytes 1572872 | tf_op jit(solution)/shard_map/ppermute | solution.py:17
  92.5 2.6 %shard_map.156 = (f32[448,256]{1,0:T(8,128)S(1)}, bf16[256,4096]{1,0:T(8,128)(2,1)S(1)}) custom-call(bf16[96,4096]{1,0:T(8,128)(2,1)} %get-tuple-element.194.refs_0_, bf16[96,4096]{1,0:T(8,128)(2,1)S(1)} %collective-permute-done.11.refs_3_.refs_1_, bf16[96,4096]{1,0:T(8,128)(2,1)} %collective-permute-done.12.refs_4_.refs_2_, ...), custom_call_target="tpu_custom_call" | custom-call | flops 1 | bytes 1 | tf_op jit(solution)/shard_map/pallas_call | solution.py:332
  95.1 8.2 %collective-permute-done.20.refs_4_ = bf16[64,4096]{1,0:T(8,128)(2,1)S(1)} collective-permute-done((bf16[64,4096]{1,0:T(8,128)(2,1)S(1)}, bf16[64,4096]{1,0:T(8,128)(2,1)S(1)}, u32[]{:S(2)}, u32[]{:S(2)}) %collective-permute-start.20) | collective-permute-done | bytes 524320 | tf_op jit(solution)/shard_map/ppermute | solution.py:17
  103.3 3.6 %collective-permute-done.19.refs_3_ = bf16[64,4096]{1,0:T(8,128)(2,1)S(1)} collective-permute-done((bf16[64,4096]{1,0:T(8,128)(2,1)S(1)}, bf16[64,4096]{1,0:T(8,128)(2,1)S(1)}, u32[]{:S(2)}, u32[]{:S(2)}) %collective-permute-start.19) | collective-permute-done | bytes 524320 | tf_op jit(solution)/shard_map/ppermute | solution.py:17
  107.3 0.9 add_convert_fusion.3
  108.2 2.2 %collective-permute-start.21 = (bf16[64,4096]{1,0:T(8,128)(2,1)}, bf16[64,4096]{1,0:T(8,128)(2,1)S(1)}, u32[]{:S(2)}, u32[]{:S(2)}) collective-permute-start(bf16[64,4096]{1,0:T(8,128)(2,1)} %add_convert_fusion.3), channel_id=1, source_target_pairs={{0,8},{4,12},{8,16},{12,20},{16,24},{20,28},{24,0},{28,4},{1,9},{5... | collective-permute-start | bytes 1572872 | tf_op jit(solution)/shard_map/ppermute | solution.py:17
  110.4 9.7 %shard_map.157 = (f32[64,4096]{1,0:T(8,128)}, bf16[64,4096]{1,0:T(8,128)(2,1)}, bf16[64,4096]{1,0:T(8,128)(2,1)}, bf16[32,4096]{1,0:T(8,128)(2,1)}, bf16[32,4096...) custom-call(bf16[96,4096]{1,0:T(8,128)(2,1)} %copy-done.20, ...), custom_call_target="tpu_custom_call" | custom-call | flops 1 | bytes 1 | tf_op jit(solution)/shard_map/pallas_call | solution.py:352
  120.1 1.4 collective-permute-done.22
  121.5 2.7 %collective-permute-done.21 = bf16[64,4096]{1,0:T(8,128)(2,1)S(1)} collective-permute-done((bf16[64,4096]{1,0:T(8,128)(2,1)}, bf16[64,4096]{1,0:T(8,128)(2,1)S(1)}, u32[]{:S(2)}, u32[]{:S(2)}) %collective-permute-start.21) | collective-permute-done | bytes 524320 | tf_op jit(solution)/shard_map/ppermute | solution.py:17
  125.9 2.7 %collective-permute-start.25 = (bf16[32,4096]{1,0:T(8,128)(2,1)}, bf16[32,4096]{1,0:T(8,128)(2,1)S(1)}, u32[]{:S(2)}, u32[]{:S(2)}) collective-permute-start(bf16[32,4096]{1,0:T(8,128)(2,1)} %get-tuple-element.145), channel_id=1, source_target_pairs={{0,24},{4,28},{8,0},{12,4},{16,8},{20,12},{24,16},{28,20},{1,25},{... | collective-permute-start | bytes 786440 | tf_op jit(solution)/shard_map/ppermute | solution.py:17
  128.7 1.5 fusion.19
  130.3 4.7 %collective-permute-done.24 = bf16[32,4096]{1,0:T(8,128)(2,1)S(1)} collective-permute-done((bf16[32,4096]{1,0:T(8,128)(2,1)}, bf16[32,4096]{1,0:T(8,128)(2,1)S(1)}, u32[]{:S(2)}, u32[]{:S(2)}) %collective-permute-start.24) | collective-permute-done | bytes 262176 | tf_op jit(solution)/shard_map/ppermute | solution.py:17
  135.1 3.0 %collective-permute-start.29 = (bf16[64,4096]{1,0:T(8,128)(2,1)S(1)}, bf16[64,4096]{1,0:T(8,128)(2,1)S(1)}, u32[]{:S(2)}, u32[]{:S(2)}) collective-permute-start(bf16[64,4096]{1,0:T(8,128)(2,1)S(1)} %add_convert_fusion), channel_id=1, source_target_pairs={{0,24},{4,28},{8,0},{12,4},{16,8},{20,12},{24,16},{28,20},{1,25},{... | collective-permute-start | bytes 1572872 | tf_op jit(solution)/shard_map/ppermute | solution.py:17
  138.5 3.1 %collective-permute-start.31 = (bf16[64,1024]{1,0:T(8,128)(2,1)S(1)}, bf16[64,1024]{1,0:T(8,128)(2,1)S(1)}, u32[]{:S(2)}, u32[]{:S(2)}) collective-permute-start(bf16[64,1024]{1,0:T(8,128)(2,1)S(1)} %get-tuple-element.157), channel_id=1, source_target_pairs={{0,2},{1,3},{2,0},{3,1},{4,6},{5,7},{6,4},{7,5},{8,10},{9,11},{10,... | collective-permute-start | bytes 393224 | tf_op jit(solution)/shard_map/ppermute | solution.py:27
  142.1 3.0 %shard_map.158 = bf16[224,4096]{1,0:T(8,128)(2,1)} custom-call(bf16[224,256]{1,0:T(8,128)(2,1)S(1)} %copy-done.19, bf16[224,256]{1,0:T(8,128)(2,1)S(1)} %slice.38.hidden_x_ref, bf16[256,4096]{1,0:T(8,128)(2,1)S(1)} %copy-done.10, bf16[256,4096]{1,0:T(8,128)(2,1)S(1)} %collective-permute-done.23.rows_x_ref), custom_call_target="tpu_custom_call" | custom-call | flops 1 | bytes 1 | tf_op jit(solution)/shard_map/pallas_call | solution.py:379
  145.2 4.1 %collective-permute-done.31 = bf16[64,1024]{1,0:T(8,128)(2,1)S(1)} collective-permute-done((bf16[64,1024]{1,0:T(8,128)(2,1)S(1)}, bf16[64,1024]{1,0:T(8,128)(2,1)S(1)}, u32[]{:S(2)}, u32[]{:S(2)}) %collective-permute-start.31) | collective-permute-done | bytes 131104 | tf_op jit(solution)/shard_map/ppermute | solution.py:27
  149.3 2.7 %collective-permute-done.32 = bf16[64,1024]{1,0:T(8,128)(2,1)S(1)} collective-permute-done((bf16[64,1024]{1,0:T(8,128)(2,1)S(1)}, bf16[64,1024]{1,0:T(8,128)(2,1)S(1)}, u32[]{:S(2)}, u32[]{:S(2)}) %collective-permute-start.32) | collective-permute-done | bytes 131104 | tf_op jit(solution)/shard_map/ppermute | solution.py:27
  152.4 3.1 %collective-permute-start.34 = (bf16[64,1024]{1,0:T(8,128)(2,1)S(1)}, bf16[64,1024]{1,0:T(8,128)(2,1)S(1)}, u32[]{:S(2)}, u32[]{:S(2)}) collective-permute-start(bf16[64,1024]{1,0:T(8,128)(2,1)S(1)} %get-tuple-element.184), channel_id=1, source_target_pairs={{0,2},{1,3},{2,0},{3,1},{4,6},{5,7},{6,4},{7,5},{8,10},{9,11},{10,... | collective-permute-start | bytes 393224 | tf_op jit(solution)/shard_map/ppermute | solution.py:27
  155.8 5.1 %shard_map.159 = (bf16[224,4096]{1,0:T(8,128)(2,1)}, bf16[224,4096]{1,0:T(8,128)(2,1)}) custom-call(bf16[448,256]{1,0:T(8,128)(2,1)S(1)} %copy-done.18, bf16[448,256]{1,0:T(8,128)(2,1)S(1)} %slice.39.hidden_x_ref, bf16[256,4096]{1,0:T(8,128)(2,1)S(1)} %copy-done.11, bf16[256,4096]{1,0:T(8,128)(2,1)} %collective-permute-done.27.rows_x_ref), custom_call_target="tpu_custom_call" | custom-call | flops 1 | bytes 1 | tf_op jit(solution)/shard_map/pallas_call | solution.py:379
  160.9 1.0 fusion
  161.9 1.8 %collective-permute-done.34 = bf16[64,1024]{1,0:T(8,128)(2,1)S(1)} collective-permute-done((bf16[64,1024]{1,0:T(8,128)(2,1)S(1)}, bf16[64,1024]{1,0:T(8,128)(2,1)S(1)}, u32[]{:S(2)}, u32[]{:S(2)}) %collective-permute-start.34) | collective-permute-done | bytes 131104 | tf_op jit(solution)/shard_map/ppermute | solution.py:27
  163.7 2.8 %collective-permute-done.35 = bf16[64,1024]{1,0:T(8,128)(2,1)S(1)} collective-permute-done((bf16[64,1024]{1,0:T(8,128)(2,1)S(1)}, bf16[64,1024]{1,0:T(8,128)(2,1)S(1)}, u32[]{:S(2)}, u32[]{:S(2)}) %collective-permute-start.35) | collective-permute-done | bytes 131104 | tf_op jit(solution)/shard_map/ppermute | solution.py:27
  166.5 1.0 fusion.1
  (142 shorter events, 11.0 us)
Async XLA Ops:
  0.6 17.3 %copy-start.27 = (bf16[1,128,1024]{2,1,0:T(8,128)(2,1)S(1)}, bf16[1,128,1024]{2,1,0:T(8,128)(2,1)}, u32[]{:S(2)}) copy-start(bf16[1,128,1024]{2,1,0:T(8,128)(2,1)} %param.19) | copy-start | bytes 786436
  0.7 19.4 %collective-permute-start.4 = (bf16[224,4096]{1,0:T(8,128)(2,1)}, bf16[224,4096]{1,0:T(8,128)(2,1)S(1)}, u32[]{:S(2)}, u32[]{:S(2)}) collective-permute-start(bf16[224,4096]{1,0:T(8,128)(2,1)} %bitcast.38), channel_id=1, source_target_pairs={{0,4},{4,0},{8,12},{12,8},{16,20},{20,16},{24,28},{28,24},{1,5},{5... | collective-permute-start | bytes 5505032 | tf_op jit(solution)/shard_map/ppermute | solution.py:22
  3.7 14.5 %collective-permute-start.1 = (bf16[64,1024]{1,0:T(8,128)(2,1)S(1)}, bf16[64,1024]{1,0:T(8,128)(2,1)S(1)}, u32[]{:S(2)}, u32[]{:S(2)}) collective-permute-start(bf16[64,1024]{1,0:T(8,128)(2,1)S(1)} %convolution_convert_fusion.4), channel_id=1, source_target_pairs={{0,1},{1,0},{2,3},{3,2},{4,5},{5,4},{6,7},{7,6},{8,9},{9,8},{10,11... | collective-permute-start | bytes 393224 | tf_op jit(solution)/shard_map/ppermute | solution.py:27
  5.6 12.6 %collective-permute-start.2 = (bf16[64,1024]{1,0:T(8,128)(2,1)S(1)}, bf16[64,1024]{1,0:T(8,128)(2,1)}, u32[]{:S(2)}, u32[]{:S(2)}) collective-permute-start(bf16[64,1024]{1,0:T(8,128)(2,1)S(1)} %convolution_convert_fusion.4), channel_id=1, source_target_pairs={{0,2},{1,3},{2,0},{3,1},{4,6},{5,7},{6,4},{7,5},{8,10},{9,11},{10,... | collective-permute-start | bytes 393224 | tf_op jit(solution)/shard_map/ppermute | solution.py:27
  7.2 12.9 %collective-permute-start.3 = (bf16[64,1024]{1,0:T(8,128)(2,1)S(1)}, bf16[64,1024]{1,0:T(8,128)(2,1)}, u32[]{:S(2)}, u32[]{:S(2)}) collective-permute-start(bf16[64,1024]{1,0:T(8,128)(2,1)S(1)} %convolution_convert_fusion.4), channel_id=1, source_target_pairs={{0,3},{1,2},{2,1},{3,0},{4,7},{5,6},{6,5},{7,4},{8,11},{9,10},{10,... | collective-permute-start | bytes 393224 | tf_op jit(solution)/shard_map/ppermute | solution.py:27
  8.3 19.7 %collective-permute-start = (bf16[128,1024]{1,0:T(8,128)(2,1)S(1)}, bf16[128,1024]{1,0:T(8,128)(2,1)S(1)}, u32[]{:S(2)}, u32[]{:S(2)}) collective-permute-start(bf16[128,1024]{1,0:T(8,128)(2,1)S(1)} %dynamic-slice_bitcast_fusion), channel_id=1, source_target_pairs={{0,227},{1,226},{2,225},{3,224},{32,195},{33,194},{34,193},{35,192... | collective-permute-start | bytes 786440 | tf_op jit(solution)/shard_map/ppermute | solution.py:33
  21.5 23.6 %copy-start.7 = (bf16[64,4096]{1,0:T(8,128)(2,1)}, bf16[64,4096]{1,0:T(8,128)(2,1)S(1)}, u32[]{:S(2)}) copy-start(bf16[64,4096]{1,0:T(8,128)(2,1)S(1)} %pad_maximum_fusion.6.refs_0_) | copy-start | bytes 1572868
  21.5 22.5 %collective-permute-start.10 = (bf16[64,4096]{1,0:T(8,128)(2,1)S(1)}, bf16[64,4096]{1,0:T(8,128)(2,1)S(1)}, u32[]{:S(2)}, u32[]{:S(2)}) collective-permute-start(bf16[64,4096]{1,0:T(8,128)(2,1)S(1)} %pad_maximum_fusion.6.refs_0_), channel_id=1, source_target_pairs={{0,24},{4,28},{8,0},{12,4},{16,8},{20,12},{24,16},{28,20},{1,25},{... | collective-permute-start | bytes 1572872 | tf_op jit(solution)/shard_map/ppermute | solution.py:17
  24.5 19.4 %collective-permute-start.9 = (bf16[64,4096]{1,0:T(8,128)(2,1)S(1)}, bf16[64,4096]{1,0:T(8,128)(2,1)S(1)}, u32[]{:S(2)}, u32[]{:S(2)}) collective-permute-start(bf16[64,4096]{1,0:T(8,128)(2,1)S(1)} %pad_maximum_fusion.6.refs_0_), channel_id=1, source_target_pairs={{0,8},{4,12},{8,16},{12,20},{16,24},{20,28},{24,0},{28,4},{1,9},{5... | collective-permute-start | bytes 1572872 | tf_op jit(solution)/shard_map/ppermute | solution.py:17
  24.6 6.4 %collective-permute-start.5 = (bf16[64,1024]{1,0:T(8,128)(2,1)S(1)}, bf16[64,1024]{1,0:T(8,128)(2,1)S(1)}, u32[]{:S(2)}, u32[]{:S(2)}) collective-permute-start(bf16[64,1024]{1,0:T(8,128)(2,1)S(1)} %convolution_convert_fusion.2), channel_id=1, source_target_pairs={{0,1},{1,0},{2,3},{3,2},{4,5},{5,4},{6,7},{7,6},{8,9},{9,8},{10,11... | collective-permute-start | bytes 393224 | tf_op jit(solution)/shard_map/ppermute | solution.py:27
  24.6 11.6 %collective-permute-start.6 = (bf16[64,1024]{1,0:T(8,128)(2,1)S(1)}, bf16[64,1024]{1,0:T(8,128)(2,1)S(1)}, u32[]{:S(2)}, u32[]{:S(2)}) collective-permute-start(bf16[64,1024]{1,0:T(8,128)(2,1)S(1)} %convolution_convert_fusion.2), channel_id=1, source_target_pairs={{0,2},{1,3},{2,0},{3,1},{4,6},{5,7},{6,4},{7,5},{8,10},{9,11},{10,... | collective-permute-start | bytes 393224 | tf_op jit(solution)/shard_map/ppermute | solution.py:27
  28.0 11.0 %collective-permute-start.7 = (bf16[64,1024]{1,0:T(8,128)(2,1)S(1)}, bf16[64,1024]{1,0:T(8,128)(2,1)S(1)}, u32[]{:S(2)}, u32[]{:S(2)}) collective-permute-start(bf16[64,1024]{1,0:T(8,128)(2,1)S(1)} %convolution_convert_fusion.2), channel_id=1, source_target_pairs={{0,3},{1,2},{2,1},{3,0},{4,7},{5,6},{6,5},{7,4},{8,11},{9,10},{10,... | collective-permute-start | bytes 393224 | tf_op jit(solution)/shard_map/ppermute | solution.py:27
  39.0 5.0 %collective-permute-start.8 = (bf16[64,1024]{1,0:T(8,128)(2,1)S(1)}, bf16[64,1024]{1,0:T(8,128)(2,1)S(1)}, u32[]{:S(2)}, u32[]{:S(2)}) collective-permute-start(bf16[64,1024]{1,0:T(8,128)(2,1)S(1)} %convolution_convert_fusion.3), channel_id=1, source_target_pairs={{0,1},{1,0},{2,3},{3,2},{4,5},{5,4},{6,7},{7,6},{8,9},{9,8},{10,11... | collective-permute-start | bytes 393224 | tf_op jit(solution)/shard_map/ppermute | solution.py:27
  39.0 12.2 %collective-permute-start.15 = (bf16[224,4096]{1,0:T(8,128)(2,1)}, bf16[224,4096]{1,0:T(8,128)(2,1)}, u32[]{:S(2)}, u32[]{:S(2)}) collective-permute-start(bf16[224,4096]{1,0:T(8,128)(2,1)} %bitcast.8.refs_6_.refs_7_), channel_id=1, source_target_pairs={{0,4},{4,0},{8,12},{12,8},{16,20},{20,16},{24,28},{28,24},{1,5},{5... | collective-permute-start | bytes 5505032 | tf_op jit(solution)/shard_map/ppermute | solution.py:22
  45.1 20.1 %copy-start.1 = (bf16[1,224,4096]{2,1,0:T(8,128)(2,1)S(1)}, bf16[1,224,4096]{2,1,0:T(8,128)(2,1)}, u32[]{:S(2)}) copy-start(bf16[1,224,4096]{2,1,0:T(8,128)(2,1)} %param.23) | copy-start | bytes 5505028
  46.4 18.7 %collective-permute-start.11 = (bf16[96,4096]{1,0:T(8,128)(2,1)}, bf16[96,4096]{1,0:T(8,128)(2,1)S(1)}, u32[]{:S(2)}, u32[]{:S(2)}) collective-permute-start(bf16[96,4096]{1,0:T(8,128)(2,1)} %get-tuple-element.194.refs_0_), channel_id=1, source_target_pairs={{0,8},{4,12},{8,16},{12,20},{16,24},{20,28},{24,0},{28,4},{1,9},{5... | collective-permute-start | bytes 2359304 | tf_op jit(solution)/shard_map/ppermute | solution.py:17
  46.8 18.3 %collective-permute-start.12 = (bf16[96,4096]{1,0:T(8,128)(2,1)}, bf16[96,4096]{1,0:T(8,128)(2,1)}, u32[]{:S(2)}, u32[]{:S(2)}) collective-permute-start(bf16[96,4096]{1,0:T(8,128)(2,1)} %get-tuple-element.193), channel_id=1, source_target_pairs={{0,24},{4,28},{8,0},{12,4},{16,8},{20,12},{24,16},{28,20},{1,25},{... | collective-permute-start | bytes 2359304 | tf_op jit(solution)/shard_map/ppermute | solution.py:17
  49.6 8.6 %collective-permute-start.13 = (bf16[64,1024]{1,0:T(8,128)(2,1)S(1)}, bf16[64,1024]{1,0:T(8,128)(2,1)S(1)}, u32[]{:S(2)}, u32[]{:S(2)}) collective-permute-start(bf16[64,1024]{1,0:T(8,128)(2,1)S(1)} %convolution_convert_fusion.3), channel_id=1, source_target_pairs={{0,2},{1,3},{2,0},{3,1},{4,6},{5,7},{6,4},{7,5},{8,10},{9,11},{10,... | collective-permute-start | bytes 393224 | tf_op jit(solution)/shard_map/ppermute | solution.py:27
  50.6 10.2 %collective-permute-start.14 = (bf16[64,1024]{1,0:T(8,128)(2,1)S(1)}, bf16[64,1024]{1,0:T(8,128)(2,1)}, u32[]{:S(2)}, u32[]{:S(2)}) collective-permute-start(bf16[64,1024]{1,0:T(8,128)(2,1)S(1)} %convolution_convert_fusion.3), channel_id=1, source_target_pairs={{0,3},{1,2},{2,1},{3,0},{4,7},{5,6},{6,5},{7,4},{8,11},{9,10},{10,... | collective-permute-start | bytes 393224 | tf_op jit(solution)/shard_map/ppermute | solution.py:27
  65.1 6.0 %collective-permute-start.18 = (bf16[224,4096]{1,0:T(8,128)(2,1)S(1)}, bf16[224,4096]{1,0:T(8,128)(2,1)S(1)}, u32[]{:S(2)}, u32[]{:S(2)}) collective-permute-start(bf16[224,4096]{1,0:T(8,128)(2,1)S(1)} %bitcast.35), channel_id=1, source_target_pairs={{0,4},{4,0},{8,12},{12,8},{16,20},{20,16},{24,28},{28,24},{1,5},{5... | collective-permute-start | bytes 5505032 | tf_op jit(solution)/shard_map/ppermute | solution.py:22
  67.6 21.5 %collective-permute-start.16 = (bf16[96,4096]{1,0:T(8,128)(2,1)S(1)}, bf16[96,4096]{1,0:T(8,128)(2,1)S(1)}, u32[]{:S(2)}, u32[]{:S(2)}) collective-permute-start(bf16[96,4096]{1,0:T(8,128)(2,1)S(1)} %get-tuple-element.190.refs_0_), channel_id=1, source_target_pairs={{0,8},{4,12},{8,16},{12,20},{16,24},{20,28},{24,0},{28,4},{1,9},{5... | collective-permute-start | bytes 2359304 | tf_op jit(solution)/shard_map/ppermute | solution.py:17
  69.4 19.7 %collective-permute-start.17 = (bf16[96,4096]{1,0:T(8,128)(2,1)S(1)}, bf16[96,4096]{1,0:T(8,128)(2,1)S(1)}, u32[]{:S(2)}, u32[]{:S(2)}) collective-permute-start(bf16[96,4096]{1,0:T(8,128)(2,1)S(1)} %get-tuple-element.189), channel_id=1, source_target_pairs={{0,24},{4,28},{8,0},{12,4},{16,8},{20,12},{24,16},{28,20},{1,25},{... | collective-permute-start | bytes 2359304 | tf_op jit(solution)/shard_map/ppermute | solution.py:17
  77.7 14.6 %copy-start.16 = (f32[64,4096]{1,0:T(8,128)}, f32[64,4096]{1,0:T(8,128)S(1)}, u32[]{:S(2)}) copy-start(f32[64,4096]{1,0:T(8,128)S(1)} %get-tuple-element.148) | copy-start | bytes 3145732
  89.2 14.1 %collective-permute-start.20 = (bf16[64,4096]{1,0:T(8,128)(2,1)S(1)}, bf16[64,4096]{1,0:T(8,128)(2,1)S(1)}, u32[]{:S(2)}, u32[]{:S(2)}) collective-permute-start(bf16[64,4096]{1,0:T(8,128)(2,1)S(1)} %pad_maximum_fusion.8), channel_id=1, source_target_pairs={{0,24},{4,28},{8,0},{12,4},{16,8},{20,12},{24,16},{28,20},{1,25},{... | collective-permute-start | bytes 1572872 | tf_op jit(solution)/shard_map/ppermute | solution.py:17
  92.4 14.5 %collective-permute-start.19 = (bf16[64,4096]{1,0:T(8,128)(2,1)S(1)}, bf16[64,4096]{1,0:T(8,128)(2,1)S(1)}, u32[]{:S(2)}, u32[]{:S(2)}) collective-permute-start(bf16[64,4096]{1,0:T(8,128)(2,1)S(1)} %pad_maximum_fusion.7), channel_id=1, source_target_pairs={{0,8},{4,12},{8,16},{12,20},{16,24},{20,28},{24,0},{28,4},{1,9},{5... | collective-permute-start | bytes 1572872 | tf_op jit(solution)/shard_map/ppermute | solution.py:17
  95.1 13.1 %copy-start.9 = (bf16[256,4096]{1,0:T(8,128)(2,1)}, bf16[256,4096]{1,0:T(8,128)(2,1)S(1)}, u32[]{:S(2)}) copy-start(bf16[256,4096]{1,0:T(8,128)(2,1)S(1)} %get-tuple-element.133.rows_ref) | copy-start | bytes 6291460
  95.1 13.1 %copy-start.17 = (f32[448,256]{1,0:T(8,128)}, f32[448,256]{1,0:T(8,128)S(1)}, u32[]{:S(2)}) copy-start(f32[448,256]{1,0:T(8,128)S(1)} %get-tuple-element.134.refs_5_) | copy-start | bytes 1376260
  106.9 17.2 %collective-permute-start.23 = (bf16[256,4096]{1,0:T(8,128)(2,1)S(1)}, bf16[256,4096]{1,0:T(8,128)(2,1)S(1)}, u32[]{:S(2)}, u32[]{:S(2)}) collective-permute-start(bf16[256,4096]{1,0:T(8,128)(2,1)S(1)} %get-tuple-element.133.rows_ref), channel_id=1, source_target_pairs={{0,4},{4,0},{8,12},{12,8},{16,20},{20,16},{24,28},{28,24},{1,5},{5... | collective-permute-start | bytes 6291464 | tf_op jit(solution)/shard_map/ppermute | solution.py:22
  107.1 14.4 %collective-permute-start.22 = (bf16[64,4096]{1,0:T(8,128)(2,1)S(1)}, bf16[64,4096]{1,0:T(8,128)(2,1)S(1)}, u32[]{:S(2)}, u32[]{:S(2)}) collective-permute-start(bf16[64,4096]{1,0:T(8,128)(2,1)S(1)} %add_convert_fusion.2), channel_id=1, source_target_pairs={{0,24},{4,28},{8,0},{12,4},{16,8},{20,12},{24,16},{28,20},{1,25},{... | collective-permute-start | bytes 1572872 | tf_op jit(solution)/shard_map/ppermute | solution.py:17
  108.2 15.9 %collective-permute-start.21 = (bf16[64,4096]{1,0:T(8,128)(2,1)}, bf16[64,4096]{1,0:T(8,128)(2,1)S(1)}, u32[]{:S(2)}, u32[]{:S(2)}) collective-permute-start(bf16[64,4096]{1,0:T(8,128)(2,1)} %add_convert_fusion.3), channel_id=1, source_target_pairs={{0,8},{4,12},{8,16},{12,20},{16,24},{20,28},{24,0},{28,4},{1,9},{5... | collective-permute-start | bytes 1572872 | tf_op jit(solution)/shard_map/ppermute | solution.py:17
  124.9 10.2 %collective-permute-start.27 = (bf16[256,4096]{1,0:T(8,128)(2,1)}, bf16[256,4096]{1,0:T(8,128)(2,1)}, u32[]{:S(2)}, u32[]{:S(2)}) collective-permute-start(bf16[256,4096]{1,0:T(8,128)(2,1)} %get-tuple-element.147.rows_ref), channel_id=1, source_target_pairs={{0,4},{4,0},{8,12},{12,8},{16,20},{20,16},{24,28},{28,24},{1,5},{5... | collective-permute-start | bytes 6291464 | tf_op jit(solution)/shard_map/ppermute | solution.py:22
  124.9 10.1 %collective-permute-start.26 = (bf16[672,256]{1,0:T(8,128)(2,1)}, bf16[672,256]{1,0:T(8,128)(2,1)S(1)}, u32[]{:S(2)}, u32[]{:S(2)}) collective-permute-start(bf16[672,256]{1,0:T(8,128)(2,1)} %get-tuple-element.146), channel_id=1, source_target_pairs={{0,4},{4,0},{8,12},{12,8},{16,20},{20,16},{24,28},{28,24},{1,5},{5... | collective-permute-start | bytes 1032200 | tf_op jit(solution)/shard_map/ppermute | solution.py:22
  125.4 9.6 %collective-permute-start.24 = (bf16[32,4096]{1,0:T(8,128)(2,1)}, bf16[32,4096]{1,0:T(8,128)(2,1)S(1)}, u32[]{:S(2)}, u32[]{:S(2)}) collective-permute-start(bf16[32,4096]{1,0:T(8,128)(2,1)} %get-tuple-element.144), channel_id=1, source_target_pairs={{0,8},{4,12},{8,16},{12,20},{16,24},{20,28},{24,0},{28,4},{1,9},{5... | collective-permute-start | bytes 786440 | tf_op jit(solution)/shard_map/ppermute | solution.py:17
  125.9 9.1 %collective-permute-start.25 = (bf16[32,4096]{1,0:T(8,128)(2,1)}, bf16[32,4096]{1,0:T(8,128)(2,1)S(1)}, u32[]{:S(2)}, u32[]{:S(2)}) collective-permute-start(bf16[32,4096]{1,0:T(8,128)(2,1)} %get-tuple-element.145), channel_id=1, source_target_pairs={{0,24},{4,28},{8,0},{12,4},{16,8},{20,12},{24,16},{28,20},{1,25},{... | collective-permute-start | bytes 786440 | tf_op jit(solution)/shard_map/ppermute | solution.py:17
  130.2 11.7 %copy-start.28 = (s32[1,128,2]{1,2,0:T(2,128)S(1)}, s32[1,128,2]{1,2,0:T(2,128)}, u32[]{:S(2)}) copy-start(s32[1,128,2]{1,2,0:T(2,128)} %param.13) | copy-start | bytes 3076
  130.3 11.7 %copy-start.29 = (f32[1,128,2]{1,2,0:T(2,128)S(1)}, f32[1,128,2]{1,2,0:T(2,128)}, u32[]{:S(2)}) copy-start(f32[1,128,2]{1,2,0:T(2,128)} %param.14) | copy-start | bytes 3076
  130.3 11.8 %copy-start.10 = (bf16[256,4096]{1,0:T(8,128)(2,1)S(1)}, bf16[256,4096]{1,0:T(8,128)(2,1)}, u32[]{:S(2)}) copy-start(bf16[256,4096]{1,0:T(8,128)(2,1)} %copy-done.9) | copy-start | bytes 6291460
  130.3 11.8 %copy-start.19 = (bf16[224,256]{1,0:T(8,128)(2,1)S(1)}, bf16[224,256]{1,0:T(8,128)(2,1)}, u32[]{:S(2)}) copy-start(bf16[224,256]{1,0:T(8,128)(2,1)} %get-tuple-element.159.hidden_ref) | copy-start | bytes 344068
  135.1 16.9 %collective-permute-start.29 = (bf16[64,4096]{1,0:T(8,128)(2,1)S(1)}, bf16[64,4096]{1,0:T(8,128)(2,1)S(1)}, u32[]{:S(2)}, u32[]{:S(2)}) collective-permute-start(bf16[64,4096]{1,0:T(8,128)(2,1)S(1)} %add_convert_fusion), channel_id=1, source_target_pairs={{0,24},{4,28},{8,0},{12,4},{16,8},{20,12},{24,16},{28,20},{1,25},{... | collective-permute-start | bytes 1572872 | tf_op jit(solution)/shard_map/ppermute | solution.py:17
  138.2 13.8 %collective-permute-start.28 = (bf16[64,4096]{1,0:T(8,128)(2,1)S(1)}, bf16[64,4096]{1,0:T(8,128)(2,1)S(1)}, u32[]{:S(2)}, u32[]{:S(2)}) collective-permute-start(bf16[64,4096]{1,0:T(8,128)(2,1)S(1)} %add_convert_fusion.1), channel_id=1, source_target_pairs={{0,8},{4,12},{8,16},{12,20},{16,24},{20,28},{24,0},{28,4},{1,9},{5... | collective-permute-start | bytes 1572872 | tf_op jit(solution)/shard_map/ppermute | solution.py:17
  138.3 6.8 %collective-permute-start.30 = (bf16[64,1024]{1,0:T(8,128)(2,1)S(1)}, bf16[64,1024]{1,0:T(8,128)(2,1)S(1)}, u32[]{:S(2)}, u32[]{:S(2)}) collective-permute-start(bf16[64,1024]{1,0:T(8,128)(2,1)S(1)} %get-tuple-element.156), channel_id=1, source_target_pairs={{0,1},{1,0},{2,3},{3,2},{4,5},{5,4},{6,7},{7,6},{8,9},{9,8},{10,11... | collective-permute-start | bytes 393224 | tf_op jit(solution)/shard_map/ppermute | solution.py:27
  138.5 10.8 %collective-permute-start.31 = (bf16[64,1024]{1,0:T(8,128)(2,1)S(1)}, bf16[64,1024]{1,0:T(8,128)(2,1)S(1)}, u32[]{:S(2)}, u32[]{:S(2)}) collective-permute-start(bf16[64,1024]{1,0:T(8,128)(2,1)S(1)} %get-tuple-element.157), channel_id=1, source_target_pairs={{0,2},{1,3},{2,0},{3,1},{4,6},{5,7},{6,4},{7,5},{8,10},{9,11},{10,... | collective-permute-start | bytes 393224 | tf_op jit(solution)/shard_map/ppermute | solution.py:27
  141.6 10.4 %collective-permute-start.32 = (bf16[64,1024]{1,0:T(8,128)(2,1)S(1)}, bf16[64,1024]{1,0:T(8,128)(2,1)S(1)}, u32[]{:S(2)}, u32[]{:S(2)}) collective-permute-start(bf16[64,1024]{1,0:T(8,128)(2,1)S(1)} %get-tuple-element.158), channel_id=1, source_target_pairs={{0,3},{1,2},{2,1},{3,0},{4,7},{5,6},{6,5},{7,4},{8,11},{9,10},{10,... | collective-permute-start | bytes 393224 | tf_op jit(solution)/shard_map/ppermute | solution.py:27
  145.1 10.7 %copy-start.11 = (bf16[256,4096]{1,0:T(8,128)(2,1)S(1)}, bf16[256,4096]{1,0:T(8,128)(2,1)}, u32[]{:S(2)}) copy-start(bf16[256,4096]{1,0:T(8,128)(2,1)} %get-tuple-element.147.rows_ref) | copy-start | bytes 6291460
  145.1 10.7 %copy-start.18 = (bf16[448,256]{1,0:T(8,128)(2,1)S(1)}, bf16[448,256]{1,0:T(8,128)(2,1)}, u32[]{:S(2)}) copy-start(bf16[448,256]{1,0:T(8,128)(2,1)} %get-tuple-element.169.hidden_ref) | copy-start | bytes 688132
  152.3 9.7 %collective-permute-start.33 = (bf16[64,1024]{1,0:T(8,128)(2,1)S(1)}, bf16[64,1024]{1,0:T(8,128)(2,1)S(1)}, u32[]{:S(2)}, u32[]{:S(2)}) collective-permute-start(bf16[64,1024]{1,0:T(8,128)(2,1)S(1)} %get-tuple-element.185), channel_id=1, source_target_pairs={{0,1},{1,0},{2,3},{3,2},{4,5},{5,4},{6,7},{7,6},{8,9},{9,8},{10,11... | collective-permute-start | bytes 393224 | tf_op jit(solution)/shard_map/ppermute | solution.py:27
  152.4 11.3 %collective-permute-start.34 = (bf16[64,1024]{1,0:T(8,128)(2,1)S(1)}, bf16[64,1024]{1,0:T(8,128)(2,1)S(1)}, u32[]{:S(2)}, u32[]{:S(2)}) collective-permute-start(bf16[64,1024]{1,0:T(8,128)(2,1)S(1)} %get-tuple-element.184), channel_id=1, source_target_pairs={{0,2},{1,3},{2,0},{3,1},{4,6},{5,7},{6,4},{7,5},{8,10},{9,11},{10,... | collective-permute-start | bytes 393224 | tf_op jit(solution)/shard_map/ppermute | solution.py:27
  155.5 11.0 %collective-permute-start.35 = (bf16[64,1024]{1,0:T(8,128)(2,1)S(1)}, bf16[64,1024]{1,0:T(8,128)(2,1)S(1)}, u32[]{:S(2)}, u32[]{:S(2)}) collective-permute-start(bf16[64,1024]{1,0:T(8,128)(2,1)S(1)} %get-tuple-element.183), channel_id=1, source_target_pairs={{0,3},{1,2},{2,1},{3,0},{4,7},{5,6},{6,5},{7,4},{8,11},{9,10},{10,... | collective-permute-start | bytes 393224 | tf_op jit(solution)/shard_map/ppermute | solution.py:27
  (18 other events, 81.8 us)

commit v4 on v3

--- a/solution.py
+++ b/solution.py
@@ -72,13 +72,14 @@
 
 
 def widen(block, others, place):
-    one, two, three = others
+    three, two, one = others
     odd, high = (place & 1) == 1, (place & 2) == 2
     return beside(high, beside(odd, block, one), beside(odd, two, three))
 
 
 def ask_mp(block):
-    return tuple(along_mp(block, flip) for flip in (1, 2, 3))
+    three, two, one = (along_mp(block, flip) for flip in (3, 2, 1))
+    return (three, two, one)
 
 
 def both_ways(to_ahead, to_behind):
@@ -291,7 +292,7 @@
 HBM = pl.BlockSpec(memory_space=pltpu.HBM)
 VMEM = pl.BlockSpec(memory_space=pltpu.VMEM)
 CHUNKS = 4
-PARAMS = pltpu.CompilerParams(vmem_limit_bytes=30 * 2**20)
+PARAMS = pltpu.CompilerParams(vmem_limit_bytes=22 * 2**20)
 SMALL = pl.CostEstimate(flops=1, bytes_accessed=1, transcendentals=0)
 
 
@@ -415,7 +416,8 @@
 
 
 def send_mp(blocks):
-    return tuple(along_mp(block, flip) for flip, block in zip((1, 2, 3), blocks))
+    three, two, one = (along_mp(blocks[flip - 1], flip) for flip in (3, 2, 1))
+    return (three, two, one)
 
 
 def per_device(
@@ -448,32 +450,32 @@
     back_pick = picker_of(back_slot)
     grad_tokens = (back_gate[:, None] * upstream[0].astype(jnp.float32)).astype(jnp.bfloat16)
     held_rows = mirrored(held_rows)
-    one, two, three, gate_x, grad_buf = together(
+    three, two, one, gate_x, grad_buf = together(
         *ask_mp(fwd_buf), other_core(gate_w), pack(back_pick, grad_tokens)
     )
 
-    fwd_wide = widen(fwd_buf, (one, two, three), place)
-    back_buf, one, two, three = together(pack(back_pick, held_rows), *ask_mp(grad_buf))
-    back_one, fwd_behind, fwd_ahead, one, two, three, back_buf = together(
-        along_mp(back_buf, 1), *both_ways(fwd_wide, fwd_wide), one, two, three, back_buf
-    )
-
-    grad_wide = widen(grad_buf, (one, two, three), place)
+    fwd_wide = widen(fwd_buf, (three, two, one), place)
+    three, two, one = ask_mp(grad_buf)
+    back_buf, three = together(pack(back_pick, held_rows), three)
+    fwd_behind, fwd_ahead, three, two, one, back_one, back_buf = together(
+        *both_ways(fwd_wide, fwd_wide), three, two, one, along_mp(back_buf, 1), back_buf
+    )
+
+    grad_wide = widen(grad_buf, (three, two, one), place)
     grad_sent = stacked(fwd_behind[:half], grad_wide)
-    cw, ccw, two, three, up_x, down_w = together(
+    cw, ccw, three, two, up_x, down_w = together(
         *both_ways(grad_sent, stacked(fwd_ahead[half:], grad_wide)),
-        *(along_mp(back_buf, flip) for flip in (2, 3)),
+        *(along_mp(back_buf, flip) for flip in (3, 2)),
         other_core(up_w),
         down_w,
     )
-    one = back_one
 
     down_x = other_core(down_w)
     fwd_terms = run_fwd(
         (fwd_wide, fwd_behind, fwd_ahead, cw, ccw), (gate_w, up_w, down_w, gate_x, up_x, down_x)
     )
     grad_pieces = (grad_sent, cw, ccw)
-    back_wide = widen(back_buf, (one, two, three), place ^ 3)
+    back_wide = widen(back_buf, (three, two, back_one), place ^ 3)
     back_sent = stacked(cw[half:CAP], back_wide)
     cw, ccw, down_x, *fwd_terms = together(
         *both_ways(back_sent, stacked(ccw[CAP:], back_wide)),

time: 168 us -> 166 us (0.988)
  waiting for transfers between devices: 74.2 us -> 69.1 us
    ppermute x15, waiting for transfers between devices: 37.7 us -> 23.1 us  [along_mp(): return lax.ppermute(array, 'mp', [(i, i ^ flip) for i in range(n)])]
    ppermute x1, waiting for transfers between devices: 0.39 us -> 5.78 us  [mirrored(): lax.ppermute(array, ('section', 'mp'), [(i, last - i) for i in range(last...]
    ppermute x14, waiting for transfers between devices: 36.1 us -> 40.2 us  [along_y(): lax.ppermute(array, 'expert', [(i, (i + 2 * step) % n) for i in range(n)])]
where the time goes in v4:
time: 166 us; the launch traced here: 164 us
  waiting for transfers between devices  69.1 us (42%)
  starting transfers between devices  47.7 us (29%)
  Pallas kernels  27 us (16%)
  other arithmetic  9.82 us (6%)
  local copies, waits for them, and re-layouts  4.03 us (2%)
  matrix products  3.53 us (2%)
  between operations  2.68 us (2%)
    ppermute x14, waiting for transfers between devices, along_y(): lax.ppermute(array, 'expert', [(i, (i + 2 * step) % n) for i in range(n)])  40.2 us
    ppermute x15, waiting for transfers between devices, along_mp(): return lax.ppermute(array, 'mp', [(i, i ^ flip) for i in range(n)])  23.1 us
    ppermute x14, starting transfers between devices, along_y(): lax.ppermute(array, 'expert', [(i, (i + 2 * step) % n) for i in range(n)])  21.9 us
    ppermute x15, starting transfers between devices, along_mp(): return lax.ppermute(array, 'mp', [(i, i ^ flip) for i in range(n)])  18.2 us
    pallas_call x1, Pallas kernels, run_back(): pl.pallas_call(back_kernel, out_shape=block_shapes(width) + (hidden(1), h...  9.7 us
    pallas_call x2, Pallas kernels, run_weights(): pl.pallas_call(weight_kernel, grid=(width // step,), out_shape=(jax.Shape...  8.12 us
    ppermute x1, starting transfers between devices, mirrored(): lax.ppermute(array, ('section', 'mp'), [(i, last - i) for i in range(last...  6.88 us
    pallas_call x1, Pallas kernels, run_fwd(): pl.pallas_call(fwd_kernel, out_shape=block_shapes(width), in_specs=[HBM]...  6.61 us
  transfers between devices with their start and end apart: 36, of which 19 were waited for; matrix products, arithmetic and copies ran while one was open for 8% of the time, Pallas kernels for 16%

profile of v4, /device:TPU:32, one launch (start us, length us, event | category | flops | bytes accessed | tf_op | source)
XLA Modules:
  0.0 163.8 jit_solution(10379874725884371342)
XLA Ops:
  2.6 1.1 convolution_convert_fusion.4
  3.7 2.0 %collective-permute-start = (bf16[64,1024]{1,0:T(8,128)(2,1)S(1)}, bf16[64,1024]{1,0:T(8,128)(2,1)S(1)}, u32[]{:S(2)}, u32[]{:S(2)}) collective-permute-start(bf16[64,1024]{1,0:T(8,128)(2,1)S(1)} %convolution_convert_fusion.4), channel_id=1, source_target_pairs={{0,3},{1,2},{2,1},{3,0},{4,7},{5,6},{6,5},{7,4},{8,11},{9,10},{10,... | collective-permute-start | bytes 393224 | tf_op jit(solution)/shard_map/ppermute | solution.py:27
  5.7 2.3 %collective-permute-start.1 = (bf16[64,1024]{1,0:T(8,128)(2,1)S(1)}, bf16[64,1024]{1,0:T(8,128)(2,1)}, u32[]{:S(2)}, u32[]{:S(2)}) collective-permute-start(bf16[64,1024]{1,0:T(8,128)(2,1)S(1)} %convolution_convert_fusion.4), channel_id=1, source_target_pairs={{0,2},{1,3},{2,0},{3,1},{4,6},{5,7},{6,4},{7,5},{8,10},{9,11},{10,... | collective-permute-start | bytes 393224 | tf_op jit(solution)/shard_map/ppermute | solution.py:27
  9.2 6.9 %collective-permute-start.6 = (bf16[128,1024]{1,0:T(8,128)(2,1)S(1)}, bf16[128,1024]{1,0:T(8,128)(2,1)S(1)}, u32[]{:S(2)}, u32[]{:S(2)}) collective-permute-start(bf16[128,1024]{1,0:T(8,128)(2,1)S(1)} %dynamic-slice_bitcast_fusion), channel_id=1, source_target_pairs={{0,227},{1,226},{2,225},{3,224},{32,195},{33,194},{34,193},{35,192... | collective-permute-start | bytes 786440 | tf_op jit(solution)/shard_map/ppermute | solution.py:33
  18.3 1.3 broadcast_select_fusion.15
  19.8 1.7 %collective-permute-start.4 = (bf16[64,4096]{1,0:T(8,128)(2,1)S(1)}, bf16[64,4096]{1,0:T(8,128)(2,1)S(1)}, u32[]{:S(2)}, u32[]{:S(2)}) collective-permute-start(bf16[64,4096]{1,0:T(8,128)(2,1)S(1)} %pad_maximum_fusion.6.refs_0_), channel_id=1, source_target_pairs={{0,8},{4,12},{8,16},{12,20},{16,24},{20,28},{24,0},{28,4},{1,9},{5... | collective-permute-start | bytes 1572872 | tf_op jit(solution)/shard_map/ppermute | solution.py:17
  21.4 1.7 %collective-permute-start.5 = (bf16[64,4096]{1,0:T(8,128)(2,1)S(1)}, bf16[64,4096]{1,0:T(8,128)(2,1)S(1)}, u32[]{:S(2)}, u32[]{:S(2)}) collective-permute-start(bf16[64,4096]{1,0:T(8,128)(2,1)S(1)} %pad_maximum_fusion.6.refs_0_), channel_id=1, source_target_pairs={{0,24},{4,28},{8,0},{12,4},{16,8},{20,12},{24,16},{28,20},{1,25},{... | collective-permute-start | bytes 1572872 | tf_op jit(solution)/shard_map/ppermute | solution.py:17
  23.1 1.0 collective-permute-start.7
  24.1 5.8 %collective-permute-done.6 = bf16[128,1024]{1,0:T(8,128)(2,1)S(1)} collective-permute-done((bf16[128,1024]{1,0:T(8,128)(2,1)S(1)}, bf16[128,1024]{1,0:T(8,128)(2,1)S(1)}, u32[]{:S(2)}, u32[]{:S(2)}) %collective-permute-start.6) | collective-permute-done | bytes 262176 | tf_op jit(solution)/shard_map/ppermute | solution.py:33
  30.1 2.5 %collective-permute-start.9 = (bf16[64,1024]{1,0:T(8,128)(2,1)S(1)}, bf16[64,1024]{1,0:T(8,128)(2,1)S(1)}, u32[]{:S(2)}, u32[]{:S(2)}) collective-permute-start(bf16[64,1024]{1,0:T(8,128)(2,1)S(1)} %convolution_convert_fusion.3), channel_id=1, source_target_pairs={{0,1},{1,0},{2,3},{3,2},{4,5},{5,4},{6,7},{7,6},{8,9},{9,8},{10,11... | collective-permute-start | bytes 393224 | tf_op jit(solution)/shard_map/ppermute | solution.py:27
  32.7 4.7 %collective-permute-done.8 = bf16[64,1024]{1,0:T(8,128)(2,1)S(1)} collective-permute-done((bf16[64,1024]{1,0:T(8,128)(2,1)S(1)}, bf16[64,1024]{1,0:T(8,128)(2,1)S(1)}, u32[]{:S(2)}, u32[]{:S(2)}) %collective-permute-start.8) | collective-permute-done | bytes 131104 | tf_op jit(solution)/shard_map/ppermute | solution.py:27
  37.4 2.4 %collective-permute-done.9 = bf16[64,1024]{1,0:T(8,128)(2,1)S(1)} collective-permute-done((bf16[64,1024]{1,0:T(8,128)(2,1)S(1)}, bf16[64,1024]{1,0:T(8,128)(2,1)S(1)}, u32[]{:S(2)}, u32[]{:S(2)}) %collective-permute-start.9) | collective-permute-done | bytes 131104 | tf_op jit(solution)/shard_map/ppermute | solution.py:27
  39.8 1.8 %collective-permute-done.10 = bf16[64,1024]{1,0:T(8,128)(2,1)S(1)} collective-permute-done((bf16[64,1024]{1,0:T(8,128)(2,1)S(1)}, bf16[64,1024]{1,0:T(8,128)(2,1)S(1)}, u32[]{:S(2)}, u32[]{:S(2)}) %collective-permute-start.10) | collective-permute-done | bytes 131104 | tf_op jit(solution)/shard_map/ppermute | solution.py:27
  43.4 1.3 pad_maximum_fusion.2
  44.7 1.6 collective-permute-start.11
  46.3 1.7 %collective-permute-start.12 = (bf16[96,4096]{1,0:T(8,128)(2,1)}, bf16[96,4096]{1,0:T(8,128)(2,1)}, u32[]{:S(2)}, u32[]{:S(2)}) collective-permute-start(bf16[96,4096]{1,0:T(8,128)(2,1)} %get-tuple-element.189), channel_id=1, source_target_pairs={{0,24},{4,28},{8,0},{12,4},{16,8},{20,12},{24,16},{28,20},{1,25},{... | collective-permute-start | bytes 2359304 | tf_op jit(solution)/shard_map/ppermute | solution.py:17
  48.0 1.0 collective-permute-start.13
  49.0 1.6 collective-permute-start.14
  50.6 7.7 %collective-permute-done.13 = bf16[64,1024]{1,0:T(8,128)(2,1)S(1)} collective-permute-done((bf16[64,1024]{1,0:T(8,128)(2,1)S(1)}, bf16[64,1024]{1,0:T(8,128)(2,1)S(1)}, u32[]{:S(2)}, u32[]{:S(2)}) %collective-permute-start.13) | collective-permute-done | bytes 131104 | tf_op jit(solution)/shard_map/ppermute | solution.py:27
  58.9 5.8 %collective-permute-done.11.refs_3_.refs_1_ = bf16[96,4096]{1,0:T(8,128)(2,1)S(1)} collective-permute-done((bf16[96,4096]{1,0:T(8,128)(2,1)}, bf16[96,4096]{1,0:T(8,128)(2,1)S(1)}, u32[]{:S(2)}, u32[]{:S(2)}) %collective-permute-start.11) | collective-permute-done | bytes 786464 | tf_op jit(solution)/shard_map/ppermute | solution.py:17
  65.0 1.0 slice.33
  66.0 1.0 broadcast_select_fusion.9
  67.3 1.8 %collective-permute-start.16 = (bf16[96,4096]{1,0:T(8,128)(2,1)S(1)}, bf16[96,4096]{1,0:T(8,128)(2,1)S(1)}, u32[]{:S(2)}, u32[]{:S(2)}) collective-permute-start(bf16[96,4096]{1,0:T(8,128)(2,1)S(1)} %get-tuple-element.186.refs_0_), channel_id=1, source_target_pairs={{0,8},{4,12},{8,16},{12,20},{16,24},{20,28},{24,0},{28,4},{1,9},{5... | collective-permute-start | bytes 2359304 | tf_op jit(solution)/shard_map/ppermute | solution.py:17
  69.2 1.7 %collective-permute-start.17 = (bf16[96,4096]{1,0:T(8,128)(2,1)S(1)}, bf16[96,4096]{1,0:T(8,128)(2,1)S(1)}, u32[]{:S(2)}, u32[]{:S(2)}) collective-permute-start(bf16[96,4096]{1,0:T(8,128)(2,1)S(1)} %get-tuple-element.185), channel_id=1, source_target_pairs={{0,24},{4,28},{8,0},{12,4},{16,8},{20,12},{24,16},{28,20},{1,25},{... | collective-permute-start | bytes 2359304 | tf_op jit(solution)/shard_map/ppermute | solution.py:17
  70.9 6.6 %shard_map.155 = (f32[64,4096]{1,0:T(8,128)S(1)}, bf16[64,4096]{1,0:T(8,128)(2,1)S(1)}, bf16[64,4096]{1,0:T(8,128)(2,1)S(1)}, bf16[32,4096]{1,0:T(8,128)(2,1)S(1)}, bf16[32,4096]{1,0:T(8,128)(2,1)S(1)}) custom-call(bf16[64,4096]{1,0:T(8,128)(2,1)S(1)} %copy-done.8, bf16[64,4096]{1,0:T(8,128)(2,1)S(1)} %copy-done.13, bf16[64,4096]{1,0:T(8,128)(2,1)S(1)} %copy-done.15, ...), custom_call_target="tpu_custom_call" | custom-call | flops 1 | bytes 1 | tf_op jit(solution)/shard_map/pallas_call | solution.py:320
  77.5 11.2 %collective-permute-done.16.refs_3_.refs_1_ = bf16[96,4096]{1,0:T(8,128)(2,1)S(1)} collective-permute-done((bf16[96,4096]{1,0:T(8,128)(2,1)S(1)}, bf16[96,4096]{1,0:T(8,128)(2,1)S(1)}, u32[]{:S(2)}, u32[]{:S(2)}) %collective-permute-start.16) | collective-permute-done | bytes 786464 | tf_op jit(solution)/shard_map/ppermute | solution.py:17
  88.9 3.0 %collective-permute-start.20 = (bf16[64,4096]{1,0:T(8,128)(2,1)S(1)}, bf16[64,4096]{1,0:T(8,128)(2,1)S(1)}, u32[]{:S(2)}, u32[]{:S(2)}) collective-permute-start(bf16[64,4096]{1,0:T(8,128)(2,1)S(1)} %pad_maximum_fusion.8), channel_id=1, source_target_pairs={{0,24},{4,28},{8,0},{12,4},{16,8},{20,12},{24,16},{28,20},{1,25},{... | collective-permute-start | bytes 1572872 | tf_op jit(solution)/shard_map/ppermute | solution.py:17
  92.1 2.6 %shard_map.156 = (f32[448,256]{1,0:T(8,128)S(1)}, bf16[256,4096]{1,0:T(8,128)(2,1)S(1)}) custom-call(bf16[96,4096]{1,0:T(8,128)(2,1)} %get-tuple-element.190.refs_0_, bf16[96,4096]{1,0:T(8,128)(2,1)S(1)} %collective-permute-done.11.refs_3_.refs_1_, bf16[96,4096]{1,0:T(8,128)(2,1)} %collective-permute-done.12.refs_4_.refs_2_, ...), custom_call_target="tpu_custom_call" | custom-call | flops 1 | bytes 1 | tf_op jit(solution)/shard_map/pallas_call | solution.py:333
  94.7 8.0 %collective-permute-done.20.refs_4_ = bf16[64,4096]{1,0:T(8,128)(2,1)S(1)} collective-permute-done((bf16[64,4096]{1,0:T(8,128)(2,1)S(1)}, bf16[64,4096]{1,0:T(8,128)(2,1)S(1)}, u32[]{:S(2)}, u32[]{:S(2)}) %collective-permute-start.20) | collective-permute-done | bytes 524320 | tf_op jit(solution)/shard_map/ppermute | solution.py:17
  102.8 3.6 %collective-permute-done.19.refs_3_ = bf16[64,4096]{1,0:T(8,128)(2,1)S(1)} collective-permute-done((bf16[64,4096]{1,0:T(8,128)(2,1)S(1)}, bf16[64,4096]{1,0:T(8,128)(2,1)S(1)}, u32[]{:S(2)}, u32[]{:S(2)}) %collective-permute-start.19) | collective-permute-done | bytes 524320 | tf_op jit(solution)/shard_map/ppermute | solution.py:17
  107.6 2.2 %collective-permute-start.21 = (bf16[64,4096]{1,0:T(8,128)(2,1)}, bf16[64,4096]{1,0:T(8,128)(2,1)S(1)}, u32[]{:S(2)}, u32[]{:S(2)}) collective-permute-start(bf16[64,4096]{1,0:T(8,128)(2,1)} %add_convert_fusion.3), channel_id=1, source_target_pairs={{0,8},{4,12},{8,16},{12,20},{16,24},{20,28},{24,0},{28,4},{1,9},{5... | collective-permute-start | bytes 1572872 | tf_op jit(solution)/shard_map/ppermute | solution.py:17
  109.8 9.7 %shard_map.157 = (f32[64,4096]{1,0:T(8,128)}, bf16[64,4096]{1,0:T(8,128)(2,1)}, bf16[64,4096]{1,0:T(8,128)(2,1)}, bf16[32,4096]{1,0:T(8,128)(2,1)}, bf16[32,4096...) custom-call(bf16[96,4096]{1,0:T(8,128)(2,1)} %copy-done.20, ...), custom_call_target="tpu_custom_call" | custom-call | flops 1 | bytes 1 | tf_op jit(solution)/shard_map/pallas_call | solution.py:353
  119.5 1.4 collective-permute-done.22
  120.9 2.7 %collective-permute-done.21 = bf16[64,4096]{1,0:T(8,128)(2,1)S(1)} collective-permute-done((bf16[64,4096]{1,0:T(8,128)(2,1)}, bf16[64,4096]{1,0:T(8,128)(2,1)S(1)}, u32[]{:S(2)}, u32[]{:S(2)}) %collective-permute-start.21) | collective-permute-done | bytes 524320 | tf_op jit(solution)/shard_map/ppermute | solution.py:17
  125.4 2.7 %collective-permute-start.25 = (bf16[32,4096]{1,0:T(8,128)(2,1)}, bf16[32,4096]{1,0:T(8,128)(2,1)S(1)}, u32[]{:S(2)}, u32[]{:S(2)}) collective-permute-start(bf16[32,4096]{1,0:T(8,128)(2,1)} %get-tuple-element.141), channel_id=1, source_target_pairs={{0,24},{4,28},{8,0},{12,4},{16,8},{20,12},{24,16},{28,20},{1,25},{... | collective-permute-start | bytes 786440 | tf_op jit(solution)/shard_map/ppermute | solution.py:17
  128.1 1.5 fusion.19
  129.8 4.7 %collective-permute-done.24 = bf16[32,4096]{1,0:T(8,128)(2,1)S(1)} collective-permute-done((bf16[32,4096]{1,0:T(8,128)(2,1)}, bf16[32,4096]{1,0:T(8,128)(2,1)S(1)}, u32[]{:S(2)}, u32[]{:S(2)}) %collective-permute-start.24) | collective-permute-done | bytes 262176 | tf_op jit(solution)/shard_map/ppermute | solution.py:17
  134.6 3.0 %collective-permute-start.29 = (bf16[64,4096]{1,0:T(8,128)(2,1)S(1)}, bf16[64,4096]{1,0:T(8,128)(2,1)S(1)}, u32[]{:S(2)}, u32[]{:S(2)}) collective-permute-start(bf16[64,4096]{1,0:T(8,128)(2,1)S(1)} %add_convert_fusion), channel_id=1, source_target_pairs={{0,24},{4,28},{8,0},{12,4},{16,8},{20,12},{24,16},{28,20},{1,25},{... | collective-permute-start | bytes 1572872 | tf_op jit(solution)/shard_map/ppermute | solution.py:17
  137.8 1.1 collective-permute-start.30
  138.9 1.5 collective-permute-start.31
  141.5 3.0 %shard_map.158 = bf16[224,4096]{1,0:T(8,128)(2,1)} custom-call(bf16[224,256]{1,0:T(8,128)(2,1)S(1)} %copy-done.19, bf16[224,256]{1,0:T(8,128)(2,1)S(1)} %slice.38.hidden_x_ref, bf16[256,4096]{1,0:T(8,128)(2,1)S(1)} %copy-done.10, bf16[256,4096]{1,0:T(8,128)(2,1)S(1)} %collective-permute-done.23.rows_x_ref), custom_call_target="tpu_custom_call" | custom-call | flops 1 | bytes 1 | tf_op jit(solution)/shard_map/pallas_call | solution.py:380
  144.6 3.5 %collective-permute-done.30 = bf16[64,1024]{1,0:T(8,128)(2,1)S(1)} collective-permute-done((bf16[64,1024]{1,0:T(8,128)(2,1)S(1)}, bf16[64,1024]{1,0:T(8,128)(2,1)S(1)}, u32[]{:S(2)}, u32[]{:S(2)}) %collective-permute-start.30) | collective-permute-done | bytes 131104 | tf_op jit(solution)/shard_map/ppermute | solution.py:27
  148.8 2.6 %collective-permute-done.28 = bf16[64,4096]{1,0:T(8,128)(2,1)S(1)} collective-permute-done((bf16[64,4096]{1,0:T(8,128)(2,1)S(1)}, bf16[64,4096]{1,0:T(8,128)(2,1)S(1)}, u32[]{:S(2)}, u32[]{:S(2)}) %collective-permute-start.28) | collective-permute-done | bytes 524320 | tf_op jit(solution)/shard_map/ppermute | solution.py:17
  151.6 1.1 collective-permute-start.33
  152.7 1.7 %collective-permute-start.34 = (bf16[64,1024]{1,0:T(8,128)(2,1)S(1)}, bf16[64,1024]{1,0:T(8,128)(2,1)S(1)}, u32[]{:S(2)}, u32[]{:S(2)}) collective-permute-start(bf16[64,1024]{1,0:T(8,128)(2,1)S(1)} %get-tuple-element.180), channel_id=1, source_target_pairs={{0,2},{1,3},{2,0},{3,1},{4,6},{5,7},{6,4},{7,5},{8,10},{9,11},{10,... | collective-permute-start | bytes 393224 | tf_op jit(solution)/shard_map/ppermute | solution.py:27
  155.2 5.1 %shard_map.159 = (bf16[224,4096]{1,0:T(8,128)(2,1)}, bf16[224,4096]{1,0:T(8,128)(2,1)}) custom-call(bf16[448,256]{1,0:T(8,128)(2,1)S(1)} %copy-done.18, bf16[448,256]{1,0:T(8,128)(2,1)S(1)} %slice.39.hidden_x_ref, bf16[256,4096]{1,0:T(8,128)(2,1)S(1)} %copy-done.11, bf16[256,4096]{1,0:T(8,128)(2,1)} %collective-permute-done.27.rows_x_ref), custom_call_target="tpu_custom_call" | custom-call | flops 1 | bytes 1 | tf_op jit(solution)/shard_map/pallas_call | solution.py:380
  160.3 1.0 fusion
  161.3 1.6 collective-permute-done.33
  (142 shorter events, 14.7 us)
Async XLA Ops:
  0.6 17.3 %copy-start.27 = (bf16[1,128,1024]{2,1,0:T(8,128)(2,1)S(1)}, bf16[1,128,1024]{2,1,0:T(8,128)(2,1)}, u32[]{:S(2)}) copy-start(bf16[1,128,1024]{2,1,0:T(8,128)(2,1)} %param.19) | copy-start | bytes 786436
  0.7 17.6 %collective-permute-start.3 = (bf16[224,4096]{1,0:T(8,128)(2,1)}, bf16[224,4096]{1,0:T(8,128)(2,1)S(1)}, u32[]{:S(2)}, u32[]{:S(2)}) collective-permute-start(bf16[224,4096]{1,0:T(8,128)(2,1)} %bitcast.38), channel_id=1, source_target_pairs={{0,4},{4,0},{8,12},{12,8},{16,20},{20,16},{24,28},{28,24},{1,5},{5... | collective-permute-start | bytes 5505032 | tf_op jit(solution)/shard_map/ppermute | solution.py:22
  3.7 14.5 %collective-permute-start = (bf16[64,1024]{1,0:T(8,128)(2,1)S(1)}, bf16[64,1024]{1,0:T(8,128)(2,1)S(1)}, u32[]{:S(2)}, u32[]{:S(2)}) collective-permute-start(bf16[64,1024]{1,0:T(8,128)(2,1)S(1)} %convolution_convert_fusion.4), channel_id=1, source_target_pairs={{0,3},{1,2},{2,1},{3,0},{4,7},{5,6},{6,5},{7,4},{8,11},{9,10},{10,... | collective-permute-start | bytes 393224 | tf_op jit(solution)/shard_map/ppermute | solution.py:27
  5.7 12.5 %collective-permute-start.1 = (bf16[64,1024]{1,0:T(8,128)(2,1)S(1)}, bf16[64,1024]{1,0:T(8,128)(2,1)}, u32[]{:S(2)}, u32[]{:S(2)}) collective-permute-start(bf16[64,1024]{1,0:T(8,128)(2,1)S(1)} %convolution_convert_fusion.4), channel_id=1, source_target_pairs={{0,2},{1,3},{2,0},{3,1},{4,6},{5,7},{6,4},{7,5},{8,10},{9,11},{10,... | collective-permute-start | bytes 393224 | tf_op jit(solution)/shard_map/ppermute | solution.py:27
  8.0 10.2 %collective-permute-start.2 = (bf16[64,1024]{1,0:T(8,128)(2,1)S(1)}, bf16[64,1024]{1,0:T(8,128)(2,1)}, u32[]{:S(2)}, u32[]{:S(2)}) collective-permute-start(bf16[64,1024]{1,0:T(8,128)(2,1)S(1)} %convolution_convert_fusion.4), channel_id=1, source_target_pairs={{0,1},{1,0},{2,3},{3,2},{4,5},{5,4},{6,7},{7,6},{8,9},{9,8},{10,11... | collective-permute-start | bytes 393224 | tf_op jit(solution)/shard_map/ppermute | solution.py:27
  9.2 20.6 %collective-permute-start.6 = (bf16[128,1024]{1,0:T(8,128)(2,1)S(1)}, bf16[128,1024]{1,0:T(8,128)(2,1)S(1)}, u32[]{:S(2)}, u32[]{:S(2)}) collective-permute-start(bf16[128,1024]{1,0:T(8,128)(2,1)S(1)} %dynamic-slice_bitcast_fusion), channel_id=1, source_target_pairs={{0,227},{1,226},{2,225},{3,224},{32,195},{33,194},{34,193},{35,192... | collective-permute-start | bytes 786440 | tf_op jit(solution)/shard_map/ppermute | solution.py:33
  19.7 23.6 %copy-start.7 = (bf16[64,4096]{1,0:T(8,128)(2,1)}, bf16[64,4096]{1,0:T(8,128)(2,1)S(1)}, u32[]{:S(2)}) copy-start(bf16[64,4096]{1,0:T(8,128)(2,1)S(1)} %pad_maximum_fusion.6.refs_0_) | copy-start | bytes 1572868
  19.8 21.9 %collective-permute-start.4 = (bf16[64,4096]{1,0:T(8,128)(2,1)S(1)}, bf16[64,4096]{1,0:T(8,128)(2,1)S(1)}, u32[]{:S(2)}, u32[]{:S(2)}) collective-permute-start(bf16[64,4096]{1,0:T(8,128)(2,1)S(1)} %pad_maximum_fusion.6.refs_0_), channel_id=1, source_target_pairs={{0,8},{4,12},{8,16},{12,20},{16,24},{20,28},{24,0},{28,4},{1,9},{5... | collective-permute-start | bytes 1572872 | tf_op jit(solution)/shard_map/ppermute | solution.py:17
  21.4 20.2 %collective-permute-start.5 = (bf16[64,4096]{1,0:T(8,128)(2,1)S(1)}, bf16[64,4096]{1,0:T(8,128)(2,1)S(1)}, u32[]{:S(2)}, u32[]{:S(2)}) collective-permute-start(bf16[64,4096]{1,0:T(8,128)(2,1)S(1)} %pad_maximum_fusion.6.refs_0_), channel_id=1, source_target_pairs={{0,24},{4,28},{8,0},{12,4},{16,8},{20,12},{24,16},{28,20},{1,25},{... | collective-permute-start | bytes 1572872 | tf_op jit(solution)/shard_map/ppermute | solution.py:17
  23.1 9.6 %collective-permute-start.7 = (bf16[64,1024]{1,0:T(8,128)(2,1)S(1)}, bf16[64,1024]{1,0:T(8,128)(2,1)S(1)}, u32[]{:S(2)}, u32[]{:S(2)}) collective-permute-start(bf16[64,1024]{1,0:T(8,128)(2,1)S(1)} %convolution_convert_fusion.3), channel_id=1, source_target_pairs={{0,3},{1,2},{2,1},{3,0},{4,7},{5,6},{6,5},{7,4},{8,11},{9,10},{10,... | collective-permute-start | bytes 393224 | tf_op jit(solution)/shard_map/ppermute | solution.py:27
  30.0 7.4 %collective-permute-start.8 = (bf16[64,1024]{1,0:T(8,128)(2,1)S(1)}, bf16[64,1024]{1,0:T(8,128)(2,1)S(1)}, u32[]{:S(2)}, u32[]{:S(2)}) collective-permute-start(bf16[64,1024]{1,0:T(8,128)(2,1)S(1)} %convolution_convert_fusion.3), channel_id=1, source_target_pairs={{0,2},{1,3},{2,0},{3,1},{4,6},{5,7},{6,4},{7,5},{8,10},{9,11},{10,... | collective-permute-start | bytes 393224 | tf_op jit(solution)/shard_map/ppermute | solution.py:27
  30.1 9.7 %collective-permute-start.9 = (bf16[64,1024]{1,0:T(8,128)(2,1)S(1)}, bf16[64,1024]{1,0:T(8,128)(2,1)S(1)}, u32[]{:S(2)}, u32[]{:S(2)}) collective-permute-start(bf16[64,1024]{1,0:T(8,128)(2,1)S(1)} %convolution_convert_fusion.3), channel_id=1, source_target_pairs={{0,1},{1,0},{2,3},{3,2},{4,5},{5,4},{6,7},{7,6},{8,9},{9,8},{10,11... | collective-permute-start | bytes 393224 | tf_op jit(solution)/shard_map/ppermute | solution.py:27
  32.6 9.0 %collective-permute-start.10 = (bf16[64,1024]{1,0:T(8,128)(2,1)S(1)}, bf16[64,1024]{1,0:T(8,128)(2,1)S(1)}, u32[]{:S(2)}, u32[]{:S(2)}) collective-permute-start(bf16[64,1024]{1,0:T(8,128)(2,1)S(1)} %convolution_convert_fusion.2), channel_id=1, source_target_pairs={{0,1},{1,0},{2,3},{3,2},{4,5},{5,4},{6,7},{7,6},{8,9},{9,8},{10,11... | collective-permute-start | bytes 393224 | tf_op jit(solution)/shard_map/ppermute | solution.py:27
  37.4 13.1 %collective-permute-start.15 = (bf16[224,4096]{1,0:T(8,128)(2,1)}, bf16[224,4096]{1,0:T(8,128)(2,1)}, u32[]{:S(2)}, u32[]{:S(2)}) collective-permute-start(bf16[224,4096]{1,0:T(8,128)(2,1)} %bitcast.8.refs_6_.refs_7_), channel_id=1, source_target_pairs={{0,4},{4,0},{8,12},{12,8},{16,20},{20,16},{24,28},{28,24},{1,5},{5... | collective-permute-start | bytes 5505032 | tf_op jit(solution)/shard_map/ppermute | solution.py:22
  43.4 21.5 %copy-start.1 = (bf16[1,224,4096]{2,1,0:T(8,128)(2,1)S(1)}, bf16[1,224,4096]{2,1,0:T(8,128)(2,1)}, u32[]{:S(2)}) copy-start(bf16[1,224,4096]{2,1,0:T(8,128)(2,1)} %param.23) | copy-start | bytes 5505028
  44.7 20.0 %collective-permute-start.11 = (bf16[96,4096]{1,0:T(8,128)(2,1)}, bf16[96,4096]{1,0:T(8,128)(2,1)S(1)}, u32[]{:S(2)}, u32[]{:S(2)}) collective-permute-start(bf16[96,4096]{1,0:T(8,128)(2,1)} %get-tuple-element.190.refs_0_), channel_id=1, source_target_pairs={{0,8},{4,12},{8,16},{12,20},{16,24},{20,28},{24,0},{28,4},{1,9},{5... | collective-permute-start | bytes 2359304 | tf_op jit(solution)/shard_map/ppermute | solution.py:17
  46.3 18.6 %collective-permute-start.12 = (bf16[96,4096]{1,0:T(8,128)(2,1)}, bf16[96,4096]{1,0:T(8,128)(2,1)}, u32[]{:S(2)}, u32[]{:S(2)}) collective-permute-start(bf16[96,4096]{1,0:T(8,128)(2,1)} %get-tuple-element.189), channel_id=1, source_target_pairs={{0,24},{4,28},{8,0},{12,4},{16,8},{20,12},{24,16},{28,20},{1,25},{... | collective-permute-start | bytes 2359304 | tf_op jit(solution)/shard_map/ppermute | solution.py:17
  48.0 10.3 %collective-permute-start.13 = (bf16[64,1024]{1,0:T(8,128)(2,1)S(1)}, bf16[64,1024]{1,0:T(8,128)(2,1)S(1)}, u32[]{:S(2)}, u32[]{:S(2)}) collective-permute-start(bf16[64,1024]{1,0:T(8,128)(2,1)S(1)} %convolution_convert_fusion.2), channel_id=1, source_target_pairs={{0,3},{1,2},{2,1},{3,0},{4,7},{5,6},{6,5},{7,4},{8,11},{9,10},{10,... | collective-permute-start | bytes 393224 | tf_op jit(solution)/shard_map/ppermute | solution.py:27
  49.0 10.0 %collective-permute-start.14 = (bf16[64,1024]{1,0:T(8,128)(2,1)S(1)}, bf16[64,1024]{1,0:T(8,128)(2,1)}, u32[]{:S(2)}, u32[]{:S(2)}) collective-permute-start(bf16[64,1024]{1,0:T(8,128)(2,1)S(1)} %convolution_convert_fusion.2), channel_id=1, source_target_pairs={{0,2},{1,3},{2,0},{3,1},{4,6},{5,7},{6,4},{7,5},{8,10},{9,11},{10,... | collective-permute-start | bytes 393224 | tf_op jit(solution)/shard_map/ppermute | solution.py:27
  64.9 5.9 %collective-permute-start.18 = (bf16[224,4096]{1,0:T(8,128)(2,1)S(1)}, bf16[224,4096]{1,0:T(8,128)(2,1)S(1)}, u32[]{:S(2)}, u32[]{:S(2)}) collective-permute-start(bf16[224,4096]{1,0:T(8,128)(2,1)S(1)} %bitcast.35), channel_id=1, source_target_pairs={{0,4},{4,0},{8,12},{12,8},{16,20},{20,16},{24,28},{28,24},{1,5},{5... | collective-permute-start | bytes 5505032 | tf_op jit(solution)/shard_map/ppermute | solution.py:22
  67.3 21.4 %collective-permute-start.16 = (bf16[96,4096]{1,0:T(8,128)(2,1)S(1)}, bf16[96,4096]{1,0:T(8,128)(2,1)S(1)}, u32[]{:S(2)}, u32[]{:S(2)}) collective-permute-start(bf16[96,4096]{1,0:T(8,128)(2,1)S(1)} %get-tuple-element.186.refs_0_), channel_id=1, source_target_pairs={{0,8},{4,12},{8,16},{12,20},{16,24},{20,28},{24,0},{28,4},{1,9},{5... | collective-permute-start | bytes 2359304 | tf_op jit(solution)/shard_map/ppermute | solution.py:17
  69.2 19.7 %collective-permute-start.17 = (bf16[96,4096]{1,0:T(8,128)(2,1)S(1)}, bf16[96,4096]{1,0:T(8,128)(2,1)S(1)}, u32[]{:S(2)}, u32[]{:S(2)}) collective-permute-start(bf16[96,4096]{1,0:T(8,128)(2,1)S(1)} %get-tuple-element.185), channel_id=1, source_target_pairs={{0,24},{4,28},{8,0},{12,4},{16,8},{20,12},{24,16},{28,20},{1,25},{... | collective-permute-start | bytes 2359304 | tf_op jit(solution)/shard_map/ppermute | solution.py:17
  77.5 14.5 %copy-start.16 = (f32[64,4096]{1,0:T(8,128)}, f32[64,4096]{1,0:T(8,128)S(1)}, u32[]{:S(2)}) copy-start(f32[64,4096]{1,0:T(8,128)S(1)} %get-tuple-element.144) | copy-start | bytes 3145732
  88.9 13.8 %collective-permute-start.20 = (bf16[64,4096]{1,0:T(8,128)(2,1)S(1)}, bf16[64,4096]{1,0:T(8,128)(2,1)S(1)}, u32[]{:S(2)}, u32[]{:S(2)}) collective-permute-start(bf16[64,4096]{1,0:T(8,128)(2,1)S(1)} %pad_maximum_fusion.8), channel_id=1, source_target_pairs={{0,24},{4,28},{8,0},{12,4},{16,8},{20,12},{24,16},{28,20},{1,25},{... | collective-permute-start | bytes 1572872 | tf_op jit(solution)/shard_map/ppermute | solution.py:17
  92.0 14.3 %collective-permute-start.19 = (bf16[64,4096]{1,0:T(8,128)(2,1)S(1)}, bf16[64,4096]{1,0:T(8,128)(2,1)S(1)}, u32[]{:S(2)}, u32[]{:S(2)}) collective-permute-start(bf16[64,4096]{1,0:T(8,128)(2,1)S(1)} %pad_maximum_fusion.7), channel_id=1, source_target_pairs={{0,8},{4,12},{8,16},{12,20},{16,24},{20,28},{24,0},{28,4},{1,9},{5... | collective-permute-start | bytes 1572872 | tf_op jit(solution)/shard_map/ppermute | solution.py:17
  94.7 12.9 %copy-start.9 = (bf16[256,4096]{1,0:T(8,128)(2,1)}, bf16[256,4096]{1,0:T(8,128)(2,1)S(1)}, u32[]{:S(2)}) copy-start(bf16[256,4096]{1,0:T(8,128)(2,1)S(1)} %get-tuple-element.129.rows_ref) | copy-start | bytes 6291460
  94.7 12.9 %copy-start.17 = (f32[448,256]{1,0:T(8,128)}, f32[448,256]{1,0:T(8,128)S(1)}, u32[]{:S(2)}) copy-start(f32[448,256]{1,0:T(8,128)S(1)} %get-tuple-element.130.refs_5_) | copy-start | bytes 1376260
  106.3 17.2 %collective-permute-start.23 = (bf16[256,4096]{1,0:T(8,128)(2,1)S(1)}, bf16[256,4096]{1,0:T(8,128)(2,1)S(1)}, u32[]{:S(2)}, u32[]{:S(2)}) collective-permute-start(bf16[256,4096]{1,0:T(8,128)(2,1)S(1)} %get-tuple-element.129.rows_ref), channel_id=1, source_target_pairs={{0,4},{4,0},{8,12},{12,8},{16,20},{20,16},{24,28},{28,24},{1,5},{5... | collective-permute-start | bytes 6291464 | tf_op jit(solution)/shard_map/ppermute | solution.py:22
  106.5 14.4 %collective-permute-start.22 = (bf16[64,4096]{1,0:T(8,128)(2,1)S(1)}, bf16[64,4096]{1,0:T(8,128)(2,1)S(1)}, u32[]{:S(2)}, u32[]{:S(2)}) collective-permute-start(bf16[64,4096]{1,0:T(8,128)(2,1)S(1)} %add_convert_fusion.2), channel_id=1, source_target_pairs={{0,24},{4,28},{8,0},{12,4},{16,8},{20,12},{24,16},{28,20},{1,25},{... | collective-permute-start | bytes 1572872 | tf_op jit(solution)/shard_map/ppermute | solution.py:17
  107.6 15.9 %collective-permute-start.21 = (bf16[64,4096]{1,0:T(8,128)(2,1)}, bf16[64,4096]{1,0:T(8,128)(2,1)S(1)}, u32[]{:S(2)}, u32[]{:S(2)}) collective-permute-start(bf16[64,4096]{1,0:T(8,128)(2,1)} %add_convert_fusion.3), channel_id=1, source_target_pairs={{0,8},{4,12},{8,16},{12,20},{16,24},{20,28},{24,0},{28,4},{1,9},{5... | collective-permute-start | bytes 1572872 | tf_op jit(solution)/shard_map/ppermute | solution.py:17
  124.4 10.2 %collective-permute-start.27 = (bf16[256,4096]{1,0:T(8,128)(2,1)}, bf16[256,4096]{1,0:T(8,128)(2,1)}, u32[]{:S(2)}, u32[]{:S(2)}) collective-permute-start(bf16[256,4096]{1,0:T(8,128)(2,1)} %get-tuple-element.143.rows_ref), channel_id=1, source_target_pairs={{0,4},{4,0},{8,12},{12,8},{16,20},{20,16},{24,28},{28,24},{1,5},{5... | collective-permute-start | bytes 6291464 | tf_op jit(solution)/shard_map/ppermute | solution.py:22
  124.4 10.1 %collective-permute-start.26 = (bf16[672,256]{1,0:T(8,128)(2,1)}, bf16[672,256]{1,0:T(8,128)(2,1)S(1)}, u32[]{:S(2)}, u32[]{:S(2)}) collective-permute-start(bf16[672,256]{1,0:T(8,128)(2,1)} %get-tuple-element.142), channel_id=1, source_target_pairs={{0,4},{4,0},{8,12},{12,8},{16,20},{20,16},{24,28},{28,24},{1,5},{5... | collective-permute-start | bytes 1032200 | tf_op jit(solution)/shard_map/ppermute | solution.py:22
  124.9 9.6 %collective-permute-start.24 = (bf16[32,4096]{1,0:T(8,128)(2,1)}, bf16[32,4096]{1,0:T(8,128)(2,1)S(1)}, u32[]{:S(2)}, u32[]{:S(2)}) collective-permute-start(bf16[32,4096]{1,0:T(8,128)(2,1)} %get-tuple-element.140), channel_id=1, source_target_pairs={{0,8},{4,12},{8,16},{12,20},{16,24},{20,28},{24,0},{28,4},{1,9},{5... | collective-permute-start | bytes 786440 | tf_op jit(solution)/shard_map/ppermute | solution.py:17
  125.4 9.1 %collective-permute-start.25 = (bf16[32,4096]{1,0:T(8,128)(2,1)}, bf16[32,4096]{1,0:T(8,128)(2,1)S(1)}, u32[]{:S(2)}, u32[]{:S(2)}) collective-permute-start(bf16[32,4096]{1,0:T(8,128)(2,1)} %get-tuple-element.141), channel_id=1, source_target_pairs={{0,24},{4,28},{8,0},{12,4},{16,8},{20,12},{24,16},{28,20},{1,25},{... | collective-permute-start | bytes 786440 | tf_op jit(solution)/shard_map/ppermute | solution.py:17
  129.7 11.7 %copy-start.28 = (s32[1,128,2]{1,2,0:T(2,128)S(1)}, s32[1,128,2]{1,2,0:T(2,128)}, u32[]{:S(2)}) copy-start(s32[1,128,2]{1,2,0:T(2,128)} %param.13) | copy-start | bytes 3076
  129.7 11.7 %copy-start.29 = (f32[1,128,2]{1,2,0:T(2,128)S(1)}, f32[1,128,2]{1,2,0:T(2,128)}, u32[]{:S(2)}) copy-start(f32[1,128,2]{1,2,0:T(2,128)} %param.14) | copy-start | bytes 3076
  129.8 11.8 %copy-start.10 = (bf16[256,4096]{1,0:T(8,128)(2,1)S(1)}, bf16[256,4096]{1,0:T(8,128)(2,1)}, u32[]{:S(2)}) copy-start(bf16[256,4096]{1,0:T(8,128)(2,1)} %copy-done.9) | copy-start | bytes 6291460
  129.8 11.8 %copy-start.19 = (bf16[224,256]{1,0:T(8,128)(2,1)S(1)}, bf16[224,256]{1,0:T(8,128)(2,1)}, u32[]{:S(2)}) copy-start(bf16[224,256]{1,0:T(8,128)(2,1)} %get-tuple-element.155.hidden_ref) | copy-start | bytes 344068
  134.6 14.2 %collective-permute-start.29 = (bf16[64,4096]{1,0:T(8,128)(2,1)S(1)}, bf16[64,4096]{1,0:T(8,128)(2,1)S(1)}, u32[]{:S(2)}, u32[]{:S(2)}) collective-permute-start(bf16[64,4096]{1,0:T(8,128)(2,1)S(1)} %add_convert_fusion), channel_id=1, source_target_pairs={{0,24},{4,28},{8,0},{12,4},{16,8},{20,12},{24,16},{28,20},{1,25},{... | collective-permute-start | bytes 1572872 | tf_op jit(solution)/shard_map/ppermute | solution.py:17
  137.7 13.7 %collective-permute-start.28 = (bf16[64,4096]{1,0:T(8,128)(2,1)S(1)}, bf16[64,4096]{1,0:T(8,128)(2,1)S(1)}, u32[]{:S(2)}, u32[]{:S(2)}) collective-permute-start(bf16[64,4096]{1,0:T(8,128)(2,1)S(1)} %add_convert_fusion.1), channel_id=1, source_target_pairs={{0,8},{4,12},{8,16},{12,20},{16,24},{20,28},{24,0},{28,4},{1,9},{5... | collective-permute-start | bytes 1572872 | tf_op jit(solution)/shard_map/ppermute | solution.py:17
  137.8 10.3 %collective-permute-start.30 = (bf16[64,1024]{1,0:T(8,128)(2,1)S(1)}, bf16[64,1024]{1,0:T(8,128)(2,1)S(1)}, u32[]{:S(2)}, u32[]{:S(2)}) collective-permute-start(bf16[64,1024]{1,0:T(8,128)(2,1)S(1)} %get-tuple-element.152), channel_id=1, source_target_pairs={{0,3},{1,2},{2,1},{3,0},{4,7},{5,6},{6,5},{7,4},{8,11},{9,10},{10,... | collective-permute-start | bytes 393224 | tf_op jit(solution)/shard_map/ppermute | solution.py:27
  138.9 9.9 %collective-permute-start.31 = (bf16[64,1024]{1,0:T(8,128)(2,1)S(1)}, bf16[64,1024]{1,0:T(8,128)(2,1)S(1)}, u32[]{:S(2)}, u32[]{:S(2)}) collective-permute-start(bf16[64,1024]{1,0:T(8,128)(2,1)S(1)} %get-tuple-element.153), channel_id=1, source_target_pairs={{0,2},{1,3},{2,0},{3,1},{4,6},{5,7},{6,4},{7,5},{8,10},{9,11},{10,... | collective-permute-start | bytes 393224 | tf_op jit(solution)/shard_map/ppermute | solution.py:27
  140.4 8.4 %collective-permute-start.32 = (bf16[64,1024]{1,0:T(8,128)(2,1)S(1)}, bf16[64,1024]{1,0:T(8,128)(2,1)S(1)}, u32[]{:S(2)}, u32[]{:S(2)}) collective-permute-start(bf16[64,1024]{1,0:T(8,128)(2,1)S(1)} %get-tuple-element.154), channel_id=1, source_target_pairs={{0,1},{1,0},{2,3},{3,2},{4,5},{5,4},{6,7},{7,6},{8,9},{9,8},{10,11... | collective-permute-start | bytes 393224 | tf_op jit(solution)/shard_map/ppermute | solution.py:27
  144.6 10.6 %copy-start.11 = (bf16[256,4096]{1,0:T(8,128)(2,1)S(1)}, bf16[256,4096]{1,0:T(8,128)(2,1)}, u32[]{:S(2)}) copy-start(bf16[256,4096]{1,0:T(8,128)(2,1)} %get-tuple-element.143.rows_ref) | copy-start | bytes 6291460
  144.6 10.6 %copy-start.18 = (bf16[448,256]{1,0:T(8,128)(2,1)S(1)}, bf16[448,256]{1,0:T(8,128)(2,1)}, u32[]{:S(2)}) copy-start(bf16[448,256]{1,0:T(8,128)(2,1)} %get-tuple-element.165.hidden_ref) | copy-start | bytes 688132
  151.6 11.3 %collective-permute-start.33 = (bf16[64,1024]{1,0:T(8,128)(2,1)S(1)}, bf16[64,1024]{1,0:T(8,128)(2,1)S(1)}, u32[]{:S(2)}, u32[]{:S(2)}) collective-permute-start(bf16[64,1024]{1,0:T(8,128)(2,1)S(1)} %get-tuple-element.181), channel_id=1, source_target_pairs={{0,3},{1,2},{2,1},{3,0},{4,7},{5,6},{6,5},{7,4},{8,11},{9,10},{10,... | collective-permute-start | bytes 393224 | tf_op jit(solution)/shard_map/ppermute | solution.py:27
  152.7 10.1 %collective-permute-start.34 = (bf16[64,1024]{1,0:T(8,128)(2,1)S(1)}, bf16[64,1024]{1,0:T(8,128)(2,1)S(1)}, u32[]{:S(2)}, u32[]{:S(2)}) collective-permute-start(bf16[64,1024]{1,0:T(8,128)(2,1)S(1)} %get-tuple-element.180), channel_id=1, source_target_pairs={{0,2},{1,3},{2,0},{3,1},{4,6},{5,7},{6,4},{7,5},{8,10},{9,11},{10,... | collective-permute-start | bytes 393224 | tf_op jit(solution)/shard_map/ppermute | solution.py:27
  154.4 8.4 %collective-permute-start.35 = (bf16[64,1024]{1,0:T(8,128)(2,1)S(1)}, bf16[64,1024]{1,0:T(8,128)(2,1)S(1)}, u32[]{:S(2)}, u32[]{:S(2)}) collective-permute-start(bf16[64,1024]{1,0:T(8,128)(2,1)S(1)} %get-tuple-element.179), channel_id=1, source_target_pairs={{0,1},{1,0},{2,3},{3,2},{4,5},{5,4},{6,7},{7,6},{8,9},{9,8},{10,11... | collective-permute-start | bytes 393224 | tf_op jit(solution)/shard_map/ppermute | solution.py:27
  (18 other events, 82.3 us)

commit v5 on v4

--- a/solution.py
+++ b/solution.py
@@ -366,7 +366,7 @@
             pltpu.SemaphoreType.DMA((CHUNKS, 5)),
             pltpu.SemaphoreType.DMA((4,)),
         ],
-        compiler_params=pltpu.CompilerParams(vmem_limit_bytes=56 * 2**20),
+        compiler_params=pltpu.CompilerParams(vmem_limit_bytes=30 * 2**20),
         cost_estimate=SMALL,
     )(*pieces, hidden_grad, *weights)
 

time: 166 us -> 165 us (level)
  local copies, waits for them, and re-layouts: 4.03 us -> 7.95 us
  waiting for transfers between devices: 69.1 us -> 65.4 us
    unnamed x60 -> x52, local copies, waits for them, and re-layouts: 2.47 us -> 6.38 us
    ppermute x14, waiting for transfers between devices: 40.2 us -> 36.8 us  [along_y(): lax.ppermute(array, 'expert', [(i, (i + 2 * step) % n) for i in range(n)])]
  transfers between devices with their start and end apart: 36 -> 36, of which waited for: 19 -> 18; matrix products, arithmetic and copies ran while one was open for 8% -> 8% of each run, Pallas kernels for 16% -> 16%
where the time goes in v5:
time: 165 us; the launch traced here: 163 us
  waiting for transfers between devices  65.4 us (40%)
  starting transfers between devices  47.7 us (29%)
  Pallas kernels  26.5 us (16%)
  other arithmetic  9.16 us (6%)
  local copies, waits for them, and re-layouts  7.95 us (5%)
  matrix products  3.53 us (2%)
  between operations  2.63 us (2%)
    ppermute x14, waiting for transfers between devices, along_y(): lax.ppermute(array, 'expert', [(i, (i + 2 * step) % n) for i in range(n)])  36.8 us
    ppermute x15, waiting for transfers between devices, along_mp(): return lax.ppermute(array, 'mp', [(i, i ^ flip) for i in range(n)])  22.8 us
    ppermute x14, starting transfers between devices, along_y(): lax.ppermute(array, 'expert', [(i, (i + 2 * step) % n) for i in range(n)])  21.9 us
    ppermute x15, starting transfers between devices, along_mp(): return lax.ppermute(array, 'mp', [(i, i ^ flip) for i in range(n)])  18.2 us
    pallas_call x1, Pallas kernels, run_back(): pl.pallas_call(back_kernel, out_shape=block_shapes(width) + (hidden(1), h...  8.84 us
    pallas_call x2, Pallas kernels, run_weights(): pl.pallas_call(weight_kernel, grid=(width // step,), out_shape=(jax.Shape...  8.44 us
    ppermute x1, starting transfers between devices, mirrored(): lax.ppermute(array, ('section', 'mp'), [(i, last - i) for i in range(last...  6.88 us
    pallas_call x1, Pallas kernels, run_fwd(): pl.pallas_call(fwd_kernel, out_shape=block_shapes(width), in_specs=[HBM]...  6.61 us
  transfers between devices with their start and end apart: 36, of which 18 were waited for; matrix products, arithmetic and copies ran while one was open for 8% of the time, Pallas kernels for 16%

profile of v5, /device:TPU:32, one launch (start us, length us, event | category | flops | bytes accessed | tf_op | source)
XLA Modules:
  0.0 162.8 jit_solution(572254875127181130)
XLA Ops:
  2.6 1.1 convolution_convert_fusion.4
  3.7 2.0 %collective-permute-start = (bf16[64,1024]{1,0:T(8,128)(2,1)S(1)}, bf16[64,1024]{1,0:T(8,128)(2,1)S(1)}, u32[]{:S(2)}, u32[]{:S(2)}) collective-permute-start(bf16[64,1024]{1,0:T(8,128)(2,1)S(1)} %convolution_convert_fusion.4), channel_id=1, source_target_pairs={{0,3},{1,2},{2,1},{3,0},{4,7},{5,6},{6,5},{7,4},{8,11},{9,10},{10,... | collective-permute-start | bytes 393224 | tf_op jit(solution)/shard_map/ppermute | solution.py:27
  5.7 2.3 %collective-permute-start.1 = (bf16[64,1024]{1,0:T(8,128)(2,1)S(1)}, bf16[64,1024]{1,0:T(8,128)(2,1)}, u32[]{:S(2)}, u32[]{:S(2)}) collective-permute-start(bf16[64,1024]{1,0:T(8,128)(2,1)S(1)} %convolution_convert_fusion.4), channel_id=1, source_target_pairs={{0,2},{1,3},{2,0},{3,1},{4,6},{5,7},{6,4},{7,5},{8,10},{9,11},{10,... | collective-permute-start | bytes 393224 | tf_op jit(solution)/shard_map/ppermute | solution.py:27
  9.2 6.9 %collective-permute-start.6 = (bf16[128,1024]{1,0:T(8,128)(2,1)S(1)}, bf16[128,1024]{1,0:T(8,128)(2,1)S(1)}, u32[]{:S(2)}, u32[]{:S(2)}) collective-permute-start(bf16[128,1024]{1,0:T(8,128)(2,1)S(1)} %dynamic-slice_bitcast_fusion), channel_id=1, source_target_pairs={{0,227},{1,226},{2,225},{3,224},{32,195},{33,194},{34,193},{35,192... | collective-permute-start | bytes 786440 | tf_op jit(solution)/shard_map/ppermute | solution.py:33
  18.3 1.3 broadcast_select_fusion.15
  19.8 1.7 %collective-permute-start.4 = (bf16[64,4096]{1,0:T(8,128)(2,1)S(1)}, bf16[64,4096]{1,0:T(8,128)(2,1)S(1)}, u32[]{:S(2)}, u32[]{:S(2)}) collective-permute-start(bf16[64,4096]{1,0:T(8,128)(2,1)S(1)} %pad_maximum_fusion.6.refs_0_), channel_id=1, source_target_pairs={{0,8},{4,12},{8,16},{12,20},{16,24},{20,28},{24,0},{28,4},{1,9},{5... | collective-permute-start | bytes 1572872 | tf_op jit(solution)/shard_map/ppermute | solution.py:17
  21.4 1.7 %collective-permute-start.5 = (bf16[64,4096]{1,0:T(8,128)(2,1)S(1)}, bf16[64,4096]{1,0:T(8,128)(2,1)S(1)}, u32[]{:S(2)}, u32[]{:S(2)}) collective-permute-start(bf16[64,4096]{1,0:T(8,128)(2,1)S(1)} %pad_maximum_fusion.6.refs_0_), channel_id=1, source_target_pairs={{0,24},{4,28},{8,0},{12,4},{16,8},{20,12},{24,16},{28,20},{1,25},{... | collective-permute-start | bytes 1572872 | tf_op jit(solution)/shard_map/ppermute | solution.py:17
  23.1 1.0 collective-permute-start.7
  24.1 5.8 %collective-permute-done.6 = bf16[128,1024]{1,0:T(8,128)(2,1)S(1)} collective-permute-done((bf16[128,1024]{1,0:T(8,128)(2,1)S(1)}, bf16[128,1024]{1,0:T(8,128)(2,1)S(1)}, u32[]{:S(2)}, u32[]{:S(2)}) %collective-permute-start.6) | collective-permute-done | bytes 262176 | tf_op jit(solution)/shard_map/ppermute | solution.py:33
  30.1 2.5 %collective-permute-start.9 = (bf16[64,1024]{1,0:T(8,128)(2,1)S(1)}, bf16[64,1024]{1,0:T(8,128)(2,1)S(1)}, u32[]{:S(2)}, u32[]{:S(2)}) collective-permute-start(bf16[64,1024]{1,0:T(8,128)(2,1)S(1)} %convolution_convert_fusion.3), channel_id=1, source_target_pairs={{0,1},{1,0},{2,3},{3,2},{4,5},{5,4},{6,7},{7,6},{8,9},{9,8},{10,11... | collective-permute-start | bytes 393224 | tf_op jit(solution)/shard_map/ppermute | solution.py:27
  32.7 4.7 %collective-permute-done.8 = bf16[64,1024]{1,0:T(8,128)(2,1)S(1)} collective-permute-done((bf16[64,1024]{1,0:T(8,128)(2,1)S(1)}, bf16[64,1024]{1,0:T(8,128)(2,1)S(1)}, u32[]{:S(2)}, u32[]{:S(2)}) %collective-permute-start.8) | collective-permute-done | bytes 131104 | tf_op jit(solution)/shard_map/ppermute | solution.py:27
  37.4 2.4 %collective-permute-done.9 = bf16[64,1024]{1,0:T(8,128)(2,1)S(1)} collective-permute-done((bf16[64,1024]{1,0:T(8,128)(2,1)S(1)}, bf16[64,1024]{1,0:T(8,128)(2,1)S(1)}, u32[]{:S(2)}, u32[]{:S(2)}) %collective-permute-start.9) | collective-permute-done | bytes 131104 | tf_op jit(solution)/shard_map/ppermute | solution.py:27
  39.8 1.8 %collective-permute-done.10 = bf16[64,1024]{1,0:T(8,128)(2,1)S(1)} collective-permute-done((bf16[64,1024]{1,0:T(8,128)(2,1)S(1)}, bf16[64,1024]{1,0:T(8,128)(2,1)S(1)}, u32[]{:S(2)}, u32[]{:S(2)}) %collective-permute-start.10) | collective-permute-done | bytes 131104 | tf_op jit(solution)/shard_map/ppermute | solution.py:27
  43.4 1.3 pad_maximum_fusion.2
  44.7 1.6 collective-permute-start.11
  46.3 1.7 %collective-permute-start.12 = (bf16[96,4096]{1,0:T(8,128)(2,1)}, bf16[96,4096]{1,0:T(8,128)(2,1)}, u32[]{:S(2)}, u32[]{:S(2)}) collective-permute-start(bf16[96,4096]{1,0:T(8,128)(2,1)} %get-tuple-element.189), channel_id=1, source_target_pairs={{0,24},{4,28},{8,0},{12,4},{16,8},{20,12},{24,16},{28,20},{1,25},{... | collective-permute-start | bytes 2359304 | tf_op jit(solution)/shard_map/ppermute | solution.py:17
  47.9 1.0 collective-permute-start.13
  49.0 1.6 collective-permute-start.14
  50.5 7.7 %collective-permute-done.13 = bf16[64,1024]{1,0:T(8,128)(2,1)S(1)} collective-permute-done((bf16[64,1024]{1,0:T(8,128)(2,1)S(1)}, bf16[64,1024]{1,0:T(8,128)(2,1)S(1)}, u32[]{:S(2)}, u32[]{:S(2)}) %collective-permute-start.13) | collective-permute-done | bytes 131104 | tf_op jit(solution)/shard_map/ppermute | solution.py:27
  58.9 5.8 %collective-permute-done.11.refs_3_.refs_1_ = bf16[96,4096]{1,0:T(8,128)(2,1)S(1)} collective-permute-done((bf16[96,4096]{1,0:T(8,128)(2,1)}, bf16[96,4096]{1,0:T(8,128)(2,1)S(1)}, u32[]{:S(2)}, u32[]{:S(2)}) %collective-permute-start.11) | collective-permute-done | bytes 786464 | tf_op jit(solution)/shard_map/ppermute | solution.py:17
  65.0 1.0 slice.33
  66.0 1.0 broadcast_select_fusion.9
  67.3 1.8 %collective-permute-start.16 = (bf16[96,4096]{1,0:T(8,128)(2,1)S(1)}, bf16[96,4096]{1,0:T(8,128)(2,1)S(1)}, u32[]{:S(2)}, u32[]{:S(2)}) collective-permute-start(bf16[96,4096]{1,0:T(8,128)(2,1)S(1)} %get-tuple-element.186.refs_0_), channel_id=1, source_target_pairs={{0,8},{4,12},{8,16},{12,20},{16,24},{20,28},{24,0},{28,4},{1,9},{5... | collective-permute-start | bytes 2359304 | tf_op jit(solution)/shard_map/ppermute | solution.py:17
  69.1 1.7 %collective-permute-start.17 = (bf16[96,4096]{1,0:T(8,128)(2,1)S(1)}, bf16[96,4096]{1,0:T(8,128)(2,1)S(1)}, u32[]{:S(2)}, u32[]{:S(2)}) collective-permute-start(bf16[96,4096]{1,0:T(8,128)(2,1)S(1)} %get-tuple-element.185), channel_id=1, source_target_pairs={{0,24},{4,28},{8,0},{12,4},{16,8},{20,12},{24,16},{28,20},{1,25},{... | collective-permute-start | bytes 2359304 | tf_op jit(solution)/shard_map/ppermute | solution.py:17
  70.8 6.6 %shard_map.155 = (f32[64,4096]{1,0:T(8,128)S(1)}, bf16[64,4096]{1,0:T(8,128)(2,1)S(1)}, bf16[64,4096]{1,0:T(8,128)(2,1)S(1)}, bf16[32,4096]{1,0:T(8,128)(2,1)S(1)}, bf16[32,4096]{1,0:T(8,128)(2,1)S(1)}) custom-call(bf16[64,4096]{1,0:T(8,128)(2,1)S(1)} %copy-done.6, bf16[64,4096]{1,0:T(8,128)(2,1)S(1)} %copy-done.10, bf16[64,4096]{1,0:T(8,128)(2,1)S(1)} %copy-done.12, ...), custom_call_target="tpu_custom_call" | custom-call | flops 1 | bytes 1 | tf_op jit(solution)/shard_map/pallas_call | solution.py:320
  77.5 11.3 %collective-permute-done.16.refs_3_.refs_1_ = bf16[96,4096]{1,0:T(8,128)(2,1)S(1)} collective-permute-done((bf16[96,4096]{1,0:T(8,128)(2,1)S(1)}, bf16[96,4096]{1,0:T(8,128)(2,1)S(1)}, u32[]{:S(2)}, u32[]{:S(2)}) %collective-permute-start.16) | collective-permute-done | bytes 786464 | tf_op jit(solution)/shard_map/ppermute | solution.py:17
  88.9 3.0 %collective-permute-start.20 = (bf16[64,4096]{1,0:T(8,128)(2,1)S(1)}, bf16[64,4096]{1,0:T(8,128)(2,1)S(1)}, u32[]{:S(2)}, u32[]{:S(2)}) collective-permute-start(bf16[64,4096]{1,0:T(8,128)(2,1)S(1)} %pad_maximum_fusion.8), channel_id=1, source_target_pairs={{0,24},{4,28},{8,0},{12,4},{16,8},{20,12},{24,16},{28,20},{1,25},{... | collective-permute-start | bytes 1572872 | tf_op jit(solution)/shard_map/ppermute | solution.py:17
  92.1 2.6 %shard_map.156 = (f32[448,256]{1,0:T(8,128)S(1)}, bf16[256,4096]{1,0:T(8,128)(2,1)S(1)}) custom-call(bf16[96,4096]{1,0:T(8,128)(2,1)} %get-tuple-element.190.refs_0_, bf16[96,4096]{1,0:T(8,128)(2,1)S(1)} %collective-permute-done.11.refs_3_.refs_1_, bf16[96,4096]{1,0:T(8,128)(2,1)} %collective-permute-done.12.refs_4_.refs_2_, ...), custom_call_target="tpu_custom_call" | custom-call | flops 1 | bytes 1 | tf_op jit(solution)/shard_map/pallas_call | solution.py:333
  94.7 8.1 %collective-permute-done.20.refs_4_ = bf16[64,4096]{1,0:T(8,128)(2,1)S(1)} collective-permute-done((bf16[64,4096]{1,0:T(8,128)(2,1)S(1)}, bf16[64,4096]{1,0:T(8,128)(2,1)S(1)}, u32[]{:S(2)}, u32[]{:S(2)}) %collective-permute-start.20) | collective-permute-done | bytes 524320 | tf_op jit(solution)/shard_map/ppermute | solution.py:17
  102.7 3.6 %collective-permute-done.19.refs_3_ = bf16[64,4096]{1,0:T(8,128)(2,1)S(1)} collective-permute-done((bf16[64,4096]{1,0:T(8,128)(2,1)S(1)}, bf16[64,4096]{1,0:T(8,128)(2,1)S(1)}, u32[]{:S(2)}, u32[]{:S(2)}) %collective-permute-start.19) | collective-permute-done | bytes 524320 | tf_op jit(solution)/shard_map/ppermute | solution.py:17
  106.8 2.2 %collective-permute-start.21 = (bf16[64,4096]{1,0:T(8,128)(2,1)S(1)}, bf16[64,4096]{1,0:T(8,128)(2,1)S(1)}, u32[]{:S(2)}, u32[]{:S(2)}) collective-permute-start(bf16[64,4096]{1,0:T(8,128)(2,1)S(1)} %add_convert_fusion.3), channel_id=1, source_target_pairs={{0,8},{4,12},{8,16},{12,20},{16,24},{20,28},{24,0},{28,4},{1,9},{5... | collective-permute-start | bytes 1572872 | tf_op jit(solution)/shard_map/ppermute | solution.py:17
  109.0 8.8 %shard_map.157 = (f32[64,4096]{1,0:T(8,128)S(1)}, bf16[64,4096]{1,0:T(8,128)(2,1)S(1)}, bf16[64,4096]{1,0:T(8,128)(2,1)S(1)}, bf16[32,4096]{1,0:T(8,128)(2,1)S(1...) custom-call(bf16[96,4096]{1,0:T(8,128)(2,1)S(1)} %get-tuple-element., ...), custom_call_target="tpu_custom_call" | custom-call | flops 1 | bytes 1 | tf_op jit(solution)/shard_map/pallas_call | solution.py:353
  124.3 2.7 %collective-permute-start.25 = (bf16[32,4096]{1,0:T(8,128)(2,1)}, bf16[32,4096]{1,0:T(8,128)(2,1)S(1)}, u32[]{:S(2)}, u32[]{:S(2)}) collective-permute-start(bf16[32,4096]{1,0:T(8,128)(2,1)} %copy-done.19), channel_id=1, source_target_pairs={{0,24},{4,28},{8,0},{12,4},{16,8},{20,12},{24,16},{28,20},{1,25},{... | collective-permute-start | bytes 786440 | tf_op jit(solution)/shard_map/ppermute | solution.py:17
  127.1 1.7 %fusion.19 = (bf16[64,4096]{1,0:T(8,128)(2,1)S(1)}, f32[64,4096]{1,0:T(8,128)S(1)}) fusion(bf16[64,4096]{1,0:T(8,128)(2,1)} %copy-done.21, f32[64,4096]{1,0:T(8,128)} %copy-done.15, bf16[64,4096]{1,0:T(8,128)(2,1)} %copy-done.22), kind=kLoop, calls=%fused_computation.84 | loop fusion | flops 1310720 | bytes 3670016 | tf_op jit(solution)/shard_map/convert_element_type | solution.py:414
  128.9 4.6 %collective-permute-done.24 = bf16[32,4096]{1,0:T(8,128)(2,1)S(1)} collective-permute-done((bf16[32,4096]{1,0:T(8,128)(2,1)}, bf16[32,4096]{1,0:T(8,128)(2,1)S(1)}, u32[]{:S(2)}, u32[]{:S(2)}) %collective-permute-start.24) | collective-permute-done | bytes 262176 | tf_op jit(solution)/shard_map/ppermute | solution.py:17
  133.6 3.0 %collective-permute-start.29 = (bf16[64,4096]{1,0:T(8,128)(2,1)S(1)}, bf16[64,4096]{1,0:T(8,128)(2,1)S(1)}, u32[]{:S(2)}, u32[]{:S(2)}) collective-permute-start(bf16[64,4096]{1,0:T(8,128)(2,1)S(1)} %add_convert_fusion), channel_id=1, source_target_pairs={{0,24},{4,28},{8,0},{12,4},{16,8},{20,12},{24,16},{28,20},{1,25},{... | collective-permute-start | bytes 1572872 | tf_op jit(solution)/shard_map/ppermute | solution.py:17
  136.7 1.1 collective-permute-start.30
  137.9 1.5 collective-permute-start.31
  139.3 1.0 collective-permute-start.32
  140.5 3.0 %shard_map.158 = bf16[224,4096]{1,0:T(8,128)(2,1)} custom-call(bf16[224,256]{1,0:T(8,128)(2,1)S(1)} %get-tuple-element.155.hidden_ref, bf16[224,256]{1,0:T(8,128)(2,1)S(1)} %slice.38.hidden_x_ref, bf16[256,4096]{1,0:T(8,128)(2,1)S(1)} %copy-done.8, bf16[256,4096]{1,0:T(8,128)(2,1)S(1)} %collective-permute-done.23.rows_x_ref), custom_call_target="tpu_custom_call" | custom-call | flops 1 | bytes 1 | tf_op jit(solution)/shard_map/pallas_call | solution.py:380
  143.5 3.5 %collective-permute-done.30 = bf16[64,1024]{1,0:T(8,128)(2,1)S(1)} collective-permute-done((bf16[64,1024]{1,0:T(8,128)(2,1)S(1)}, bf16[64,1024]{1,0:T(8,128)(2,1)S(1)}, u32[]{:S(2)}, u32[]{:S(2)}) %collective-permute-start.30) | collective-permute-done | bytes 131104 | tf_op jit(solution)/shard_map/ppermute | solution.py:27
  147.8 2.6 %collective-permute-done.28 = bf16[64,4096]{1,0:T(8,128)(2,1)S(1)} collective-permute-done((bf16[64,4096]{1,0:T(8,128)(2,1)S(1)}, bf16[64,4096]{1,0:T(8,128)(2,1)S(1)}, u32[]{:S(2)}, u32[]{:S(2)}) %collective-permute-start.28) | collective-permute-done | bytes 524320 | tf_op jit(solution)/shard_map/ppermute | solution.py:17
  150.5 1.1 collective-permute-start.33
  151.7 1.7 %collective-permute-start.34 = (bf16[64,1024]{1,0:T(8,128)(2,1)S(1)}, bf16[64,1024]{1,0:T(8,128)(2,1)S(1)}, u32[]{:S(2)}, u32[]{:S(2)}) collective-permute-start(bf16[64,1024]{1,0:T(8,128)(2,1)S(1)} %get-tuple-element.180), channel_id=1, source_target_pairs={{0,2},{1,3},{2,0},{3,1},{4,6},{5,7},{6,4},{7,5},{8,10},{9,11},{10,... | collective-permute-start | bytes 393224 | tf_op jit(solution)/shard_map/ppermute | solution.py:27
  154.1 5.4 %shard_map.159 = (bf16[224,4096]{1,0:T(8,128)(2,1)}, bf16[224,4096]{1,0:T(8,128)(2,1)}) custom-call(bf16[448,256]{1,0:T(8,128)(2,1)S(1)} %get-tuple-element.165.hidden_ref, bf16[448,256]{1,0:T(8,128)(2,1)S(1)} %slice.39.hidden_x_ref, bf16[256,4096]{1,0:T(8,128)(2,1)} %get-tuple-element.143.rows_ref, bf16[256,4096]{1,0:T(8,128)(2,1)} %collective-permute-done.27.rows_x_ref), custom_call_target="tpu_custom_call" | custom-call | flops 1 | bytes 1 | tf_op jit(solution)/shard_map/pallas_call | solution.py:380
  159.5 1.0 fusion
  160.5 1.3 collective-permute-done.33
  161.8 1.0 fusion.1
  (134 shorter events, 16.6 us)
Async XLA Ops:
  0.6 8.6 %copy-start = (bf16[1,2,128,1024]{3,2,1,0:T(8,128)(2,1)S(1)}, bf16[1,2,128,1024]{3,2,1,0:T(8,128)(2,1)}, u32[]{:S(2)}) copy-start(bf16[1,2,128,1024]{3,2,1,0:T(8,128)(2,1)} %param.15) | copy-start | bytes 1572868
  0.6 17.3 %copy-start.23 = (bf16[1,128,1024]{2,1,0:T(8,128)(2,1)S(1)}, bf16[1,128,1024]{2,1,0:T(8,128)(2,1)}, u32[]{:S(2)}) copy-start(bf16[1,128,1024]{2,1,0:T(8,128)(2,1)} %param.19) | copy-start | bytes 786436
  0.7 17.6 %collective-permute-start.3 = (bf16[224,4096]{1,0:T(8,128)(2,1)}, bf16[224,4096]{1,0:T(8,128)(2,1)S(1)}, u32[]{:S(2)}, u32[]{:S(2)}) collective-permute-start(bf16[224,4096]{1,0:T(8,128)(2,1)} %bitcast.38), channel_id=1, source_target_pairs={{0,4},{4,0},{8,12},{12,8},{16,20},{20,16},{24,28},{28,24},{1,5},{5... | collective-permute-start | bytes 5505032 | tf_op jit(solution)/shard_map/ppermute | solution.py:22
  3.7 14.5 %collective-permute-start = (bf16[64,1024]{1,0:T(8,128)(2,1)S(1)}, bf16[64,1024]{1,0:T(8,128)(2,1)S(1)}, u32[]{:S(2)}, u32[]{:S(2)}) collective-permute-start(bf16[64,1024]{1,0:T(8,128)(2,1)S(1)} %convolution_convert_fusion.4), channel_id=1, source_target_pairs={{0,3},{1,2},{2,1},{3,0},{4,7},{5,6},{6,5},{7,4},{8,11},{9,10},{10,... | collective-permute-start | bytes 393224 | tf_op jit(solution)/shard_map/ppermute | solution.py:27
  5.7 12.5 %collective-permute-start.1 = (bf16[64,1024]{1,0:T(8,128)(2,1)S(1)}, bf16[64,1024]{1,0:T(8,128)(2,1)}, u32[]{:S(2)}, u32[]{:S(2)}) collective-permute-start(bf16[64,1024]{1,0:T(8,128)(2,1)S(1)} %convolution_convert_fusion.4), channel_id=1, source_target_pairs={{0,2},{1,3},{2,0},{3,1},{4,6},{5,7},{6,4},{7,5},{8,10},{9,11},{10,... | collective-permute-start | bytes 393224 | tf_op jit(solution)/shard_map/ppermute | solution.py:27
  8.0 10.2 %collective-permute-start.2 = (bf16[64,1024]{1,0:T(8,128)(2,1)S(1)}, bf16[64,1024]{1,0:T(8,128)(2,1)}, u32[]{:S(2)}, u32[]{:S(2)}) collective-permute-start(bf16[64,1024]{1,0:T(8,128)(2,1)S(1)} %convolution_convert_fusion.4), channel_id=1, source_target_pairs={{0,1},{1,0},{2,3},{3,2},{4,5},{5,4},{6,7},{7,6},{8,9},{9,8},{10,11... | collective-permute-start | bytes 393224 | tf_op jit(solution)/shard_map/ppermute | solution.py:27
  9.2 20.6 %collective-permute-start.6 = (bf16[128,1024]{1,0:T(8,128)(2,1)S(1)}, bf16[128,1024]{1,0:T(8,128)(2,1)S(1)}, u32[]{:S(2)}, u32[]{:S(2)}) collective-permute-start(bf16[128,1024]{1,0:T(8,128)(2,1)S(1)} %dynamic-slice_bitcast_fusion), channel_id=1, source_target_pairs={{0,227},{1,226},{2,225},{3,224},{32,195},{33,194},{34,193},{35,192... | collective-permute-start | bytes 786440 | tf_op jit(solution)/shard_map/ppermute | solution.py:33
  19.7 23.6 %copy-start.5 = (bf16[64,4096]{1,0:T(8,128)(2,1)}, bf16[64,4096]{1,0:T(8,128)(2,1)S(1)}, u32[]{:S(2)}) copy-start(bf16[64,4096]{1,0:T(8,128)(2,1)S(1)} %pad_maximum_fusion.6.refs_0_) | copy-start | bytes 1572868
  19.8 21.9 %collective-permute-start.4 = (bf16[64,4096]{1,0:T(8,128)(2,1)S(1)}, bf16[64,4096]{1,0:T(8,128)(2,1)S(1)}, u32[]{:S(2)}, u32[]{:S(2)}) collective-permute-start(bf16[64,4096]{1,0:T(8,128)(2,1)S(1)} %pad_maximum_fusion.6.refs_0_), channel_id=1, source_target_pairs={{0,8},{4,12},{8,16},{12,20},{16,24},{20,28},{24,0},{28,4},{1,9},{5... | collective-permute-start | bytes 1572872 | tf_op jit(solution)/shard_map/ppermute | solution.py:17
  21.4 20.2 %collective-permute-start.5 = (bf16[64,4096]{1,0:T(8,128)(2,1)S(1)}, bf16[64,4096]{1,0:T(8,128)(2,1)S(1)}, u32[]{:S(2)}, u32[]{:S(2)}) collective-permute-start(bf16[64,4096]{1,0:T(8,128)(2,1)S(1)} %pad_maximum_fusion.6.refs_0_), channel_id=1, source_target_pairs={{0,24},{4,28},{8,0},{12,4},{16,8},{20,12},{24,16},{28,20},{1,25},{... | collective-permute-start | bytes 1572872 | tf_op jit(solution)/shard_map/ppermute | solution.py:17
  23.1 9.6 %collective-permute-start.7 = (bf16[64,1024]{1,0:T(8,128)(2,1)S(1)}, bf16[64,1024]{1,0:T(8,128)(2,1)S(1)}, u32[]{:S(2)}, u32[]{:S(2)}) collective-permute-start(bf16[64,1024]{1,0:T(8,128)(2,1)S(1)} %convolution_convert_fusion.3), channel_id=1, source_target_pairs={{0,3},{1,2},{2,1},{3,0},{4,7},{5,6},{6,5},{7,4},{8,11},{9,10},{10,... | collective-permute-start | bytes 393224 | tf_op jit(solution)/shard_map/ppermute | solution.py:27
  30.0 7.4 %collective-permute-start.8 = (bf16[64,1024]{1,0:T(8,128)(2,1)S(1)}, bf16[64,1024]{1,0:T(8,128)(2,1)S(1)}, u32[]{:S(2)}, u32[]{:S(2)}) collective-permute-start(bf16[64,1024]{1,0:T(8,128)(2,1)S(1)} %convolution_convert_fusion.3), channel_id=1, source_target_pairs={{0,2},{1,3},{2,0},{3,1},{4,6},{5,7},{6,4},{7,5},{8,10},{9,11},{10,... | collective-permute-start | bytes 393224 | tf_op jit(solution)/shard_map/ppermute | solution.py:27
  30.1 9.7 %collective-permute-start.9 = (bf16[64,1024]{1,0:T(8,128)(2,1)S(1)}, bf16[64,1024]{1,0:T(8,128)(2,1)S(1)}, u32[]{:S(2)}, u32[]{:S(2)}) collective-permute-start(bf16[64,1024]{1,0:T(8,128)(2,1)S(1)} %convolution_convert_fusion.3), channel_id=1, source_target_pairs={{0,1},{1,0},{2,3},{3,2},{4,5},{5,4},{6,7},{7,6},{8,9},{9,8},{10,11... | collective-permute-start | bytes 393224 | tf_op jit(solution)/shard_map/ppermute | solution.py:27
  32.6 9.0 %collective-permute-start.10 = (bf16[64,1024]{1,0:T(8,128)(2,1)S(1)}, bf16[64,1024]{1,0:T(8,128)(2,1)S(1)}, u32[]{:S(2)}, u32[]{:S(2)}) collective-permute-start(bf16[64,1024]{1,0:T(8,128)(2,1)S(1)} %convolution_convert_fusion.2), channel_id=1, source_target_pairs={{0,1},{1,0},{2,3},{3,2},{4,5},{5,4},{6,7},{7,6},{8,9},{9,8},{10,11... | collective-permute-start | bytes 393224 | tf_op jit(solution)/shard_map/ppermute | solution.py:27
  37.4 13.1 %collective-permute-start.15 = (bf16[224,4096]{1,0:T(8,128)(2,1)}, bf16[224,4096]{1,0:T(8,128)(2,1)}, u32[]{:S(2)}, u32[]{:S(2)}) collective-permute-start(bf16[224,4096]{1,0:T(8,128)(2,1)} %bitcast.8.refs_6_.refs_7_), channel_id=1, source_target_pairs={{0,4},{4,0},{8,12},{12,8},{16,20},{20,16},{24,28},{28,24},{1,5},{5... | collective-permute-start | bytes 5505032 | tf_op jit(solution)/shard_map/ppermute | solution.py:22
  43.4 21.5 %copy-start.1 = (bf16[1,224,4096]{2,1,0:T(8,128)(2,1)S(1)}, bf16[1,224,4096]{2,1,0:T(8,128)(2,1)}, u32[]{:S(2)}) copy-start(bf16[1,224,4096]{2,1,0:T(8,128)(2,1)} %param.23) | copy-start | bytes 5505028
  44.7 20.0 %collective-permute-start.11 = (bf16[96,4096]{1,0:T(8,128)(2,1)}, bf16[96,4096]{1,0:T(8,128)(2,1)S(1)}, u32[]{:S(2)}, u32[]{:S(2)}) collective-permute-start(bf16[96,4096]{1,0:T(8,128)(2,1)} %get-tuple-element.190.refs_0_), channel_id=1, source_target_pairs={{0,8},{4,12},{8,16},{12,20},{16,24},{20,28},{24,0},{28,4},{1,9},{5... | collective-permute-start | bytes 2359304 | tf_op jit(solution)/shard_map/ppermute | solution.py:17
  46.3 18.6 %collective-permute-start.12 = (bf16[96,4096]{1,0:T(8,128)(2,1)}, bf16[96,4096]{1,0:T(8,128)(2,1)}, u32[]{:S(2)}, u32[]{:S(2)}) collective-permute-start(bf16[96,4096]{1,0:T(8,128)(2,1)} %get-tuple-element.189), channel_id=1, source_target_pairs={{0,24},{4,28},{8,0},{12,4},{16,8},{20,12},{24,16},{28,20},{1,25},{... | collective-permute-start | bytes 2359304 | tf_op jit(solution)/shard_map/ppermute | solution.py:17
  47.9 10.3 %collective-permute-start.13 = (bf16[64,1024]{1,0:T(8,128)(2,1)S(1)}, bf16[64,1024]{1,0:T(8,128)(2,1)S(1)}, u32[]{:S(2)}, u32[]{:S(2)}) collective-permute-start(bf16[64,1024]{1,0:T(8,128)(2,1)S(1)} %convolution_convert_fusion.2), channel_id=1, source_target_pairs={{0,3},{1,2},{2,1},{3,0},{4,7},{5,6},{6,5},{7,4},{8,11},{9,10},{10,... | collective-permute-start | bytes 393224 | tf_op jit(solution)/shard_map/ppermute | solution.py:27
  49.0 10.0 %collective-permute-start.14 = (bf16[64,1024]{1,0:T(8,128)(2,1)S(1)}, bf16[64,1024]{1,0:T(8,128)(2,1)}, u32[]{:S(2)}, u32[]{:S(2)}) collective-permute-start(bf16[64,1024]{1,0:T(8,128)(2,1)S(1)} %convolution_convert_fusion.2), channel_id=1, source_target_pairs={{0,2},{1,3},{2,0},{3,1},{4,6},{5,7},{6,4},{7,5},{8,10},{9,11},{10,... | collective-permute-start | bytes 393224 | tf_op jit(solution)/shard_map/ppermute | solution.py:27
  64.9 5.9 %collective-permute-start.18 = (bf16[224,4096]{1,0:T(8,128)(2,1)S(1)}, bf16[224,4096]{1,0:T(8,128)(2,1)S(1)}, u32[]{:S(2)}, u32[]{:S(2)}) collective-permute-start(bf16[224,4096]{1,0:T(8,128)(2,1)S(1)} %bitcast.35), channel_id=1, source_target_pairs={{0,4},{4,0},{8,12},{12,8},{16,20},{20,16},{24,28},{28,24},{1,5},{5... | collective-permute-start | bytes 5505032 | tf_op jit(solution)/shard_map/ppermute | solution.py:22
  64.9 5.9 %copy-start.12 = (bf16[64,4096]{1,0:T(8,128)(2,1)S(1)}, bf16[64,4096]{1,0:T(8,128)(2,1)}, u32[]{:S(2)}) copy-start(bf16[64,4096]{1,0:T(8,128)(2,1)} %copy-done.11) | copy-start | bytes 1572868
  64.9 5.9 %copy-start.10 = (bf16[64,4096]{1,0:T(8,128)(2,1)S(1)}, bf16[64,4096]{1,0:T(8,128)(2,1)}, u32[]{:S(2)}) copy-start(bf16[64,4096]{1,0:T(8,128)(2,1)} %copy-done.9) | copy-start | bytes 1572868
  67.3 21.4 %collective-permute-start.16 = (bf16[96,4096]{1,0:T(8,128)(2,1)S(1)}, bf16[96,4096]{1,0:T(8,128)(2,1)S(1)}, u32[]{:S(2)}, u32[]{:S(2)}) collective-permute-start(bf16[96,4096]{1,0:T(8,128)(2,1)S(1)} %get-tuple-element.186.refs_0_), channel_id=1, source_target_pairs={{0,8},{4,12},{8,16},{12,20},{16,24},{20,28},{24,0},{28,4},{1,9},{5... | collective-permute-start | bytes 2359304 | tf_op jit(solution)/shard_map/ppermute | solution.py:17
  69.1 19.7 %collective-permute-start.17 = (bf16[96,4096]{1,0:T(8,128)(2,1)S(1)}, bf16[96,4096]{1,0:T(8,128)(2,1)S(1)}, u32[]{:S(2)}, u32[]{:S(2)}) collective-permute-start(bf16[96,4096]{1,0:T(8,128)(2,1)S(1)} %get-tuple-element.185), channel_id=1, source_target_pairs={{0,24},{4,28},{8,0},{12,4},{16,8},{20,12},{24,16},{28,20},{1,25},{... | collective-permute-start | bytes 2359304 | tf_op jit(solution)/shard_map/ppermute | solution.py:17
  77.5 14.5 %copy-start.15 = (f32[64,4096]{1,0:T(8,128)}, f32[64,4096]{1,0:T(8,128)S(1)}, u32[]{:S(2)}) copy-start(f32[64,4096]{1,0:T(8,128)S(1)} %get-tuple-element.144) | copy-start | bytes 3145732
  88.9 13.8 %collective-permute-start.20 = (bf16[64,4096]{1,0:T(8,128)(2,1)S(1)}, bf16[64,4096]{1,0:T(8,128)(2,1)S(1)}, u32[]{:S(2)}, u32[]{:S(2)}) collective-permute-start(bf16[64,4096]{1,0:T(8,128)(2,1)S(1)} %pad_maximum_fusion.8), channel_id=1, source_target_pairs={{0,24},{4,28},{8,0},{12,4},{16,8},{20,12},{24,16},{28,20},{1,25},{... | collective-permute-start | bytes 1572872 | tf_op jit(solution)/shard_map/ppermute | solution.py:17
  92.0 14.3 %collective-permute-start.19 = (bf16[64,4096]{1,0:T(8,128)(2,1)S(1)}, bf16[64,4096]{1,0:T(8,128)(2,1)S(1)}, u32[]{:S(2)}, u32[]{:S(2)}) collective-permute-start(bf16[64,4096]{1,0:T(8,128)(2,1)S(1)} %pad_maximum_fusion.7), channel_id=1, source_target_pairs={{0,8},{4,12},{8,16},{12,20},{16,24},{20,28},{24,0},{28,4},{1,9},{5... | collective-permute-start | bytes 1572872 | tf_op jit(solution)/shard_map/ppermute | solution.py:17
  94.6 12.1 %copy-start.7 = (bf16[256,4096]{1,0:T(8,128)(2,1)}, bf16[256,4096]{1,0:T(8,128)(2,1)S(1)}, u32[]{:S(2)}) copy-start(bf16[256,4096]{1,0:T(8,128)(2,1)S(1)} %get-tuple-element.129.rows_ref) | copy-start | bytes 6291460
  106.3 16.2 %collective-permute-start.23 = (bf16[256,4096]{1,0:T(8,128)(2,1)S(1)}, bf16[256,4096]{1,0:T(8,128)(2,1)S(1)}, u32[]{:S(2)}, u32[]{:S(2)}) collective-permute-start(bf16[256,4096]{1,0:T(8,128)(2,1)S(1)} %get-tuple-element.129.rows_ref), channel_id=1, source_target_pairs={{0,4},{4,0},{8,12},{12,8},{16,20},{20,16},{24,28},{28,24},{1,5},{5... | collective-permute-start | bytes 6291464 | tf_op jit(solution)/shard_map/ppermute | solution.py:22
  106.5 15.3 %collective-permute-start.22 = (bf16[64,4096]{1,0:T(8,128)(2,1)S(1)}, bf16[64,4096]{1,0:T(8,128)(2,1)S(1)}, u32[]{:S(2)}, u32[]{:S(2)}) collective-permute-start(bf16[64,4096]{1,0:T(8,128)(2,1)S(1)} %add_convert_fusion.2), channel_id=1, source_target_pairs={{0,24},{4,28},{8,0},{12,4},{16,8},{20,12},{24,16},{28,20},{1,25},{... | collective-permute-start | bytes 1572872 | tf_op jit(solution)/shard_map/ppermute | solution.py:17
  106.8 15.7 %collective-permute-start.21 = (bf16[64,4096]{1,0:T(8,128)(2,1)S(1)}, bf16[64,4096]{1,0:T(8,128)(2,1)S(1)}, u32[]{:S(2)}, u32[]{:S(2)}) collective-permute-start(bf16[64,4096]{1,0:T(8,128)(2,1)S(1)} %add_convert_fusion.3), channel_id=1, source_target_pairs={{0,8},{4,12},{8,16},{12,20},{16,24},{20,28},{24,0},{28,4},{1,9},{5... | collective-permute-start | bytes 1572872 | tf_op jit(solution)/shard_map/ppermute | solution.py:17
  123.3 10.2 %collective-permute-start.27 = (bf16[256,4096]{1,0:T(8,128)(2,1)}, bf16[256,4096]{1,0:T(8,128)(2,1)}, u32[]{:S(2)}, u32[]{:S(2)}) collective-permute-start(bf16[256,4096]{1,0:T(8,128)(2,1)} %get-tuple-element.143.rows_ref), channel_id=1, source_target_pairs={{0,4},{4,0},{8,12},{12,8},{16,20},{20,16},{24,28},{28,24},{1,5},{5... | collective-permute-start | bytes 6291464 | tf_op jit(solution)/shard_map/ppermute | solution.py:22
  123.3 10.1 %collective-permute-start.26 = (bf16[672,256]{1,0:T(8,128)(2,1)}, bf16[672,256]{1,0:T(8,128)(2,1)S(1)}, u32[]{:S(2)}, u32[]{:S(2)}) collective-permute-start(bf16[672,256]{1,0:T(8,128)(2,1)} %copy-done.18), channel_id=1, source_target_pairs={{0,4},{4,0},{8,12},{12,8},{16,20},{20,16},{24,28},{28,24},{1,5},{5... | collective-permute-start | bytes 1032200 | tf_op jit(solution)/shard_map/ppermute | solution.py:22
  123.8 9.6 %collective-permute-start.24 = (bf16[32,4096]{1,0:T(8,128)(2,1)}, bf16[32,4096]{1,0:T(8,128)(2,1)S(1)}, u32[]{:S(2)}, u32[]{:S(2)}) collective-permute-start(bf16[32,4096]{1,0:T(8,128)(2,1)} %copy-done.20), channel_id=1, source_target_pairs={{0,8},{4,12},{8,16},{12,20},{16,24},{20,28},{24,0},{28,4},{1,9},{5... | collective-permute-start | bytes 786440 | tf_op jit(solution)/shard_map/ppermute | solution.py:17
  124.3 9.1 %collective-permute-start.25 = (bf16[32,4096]{1,0:T(8,128)(2,1)}, bf16[32,4096]{1,0:T(8,128)(2,1)S(1)}, u32[]{:S(2)}, u32[]{:S(2)}) collective-permute-start(bf16[32,4096]{1,0:T(8,128)(2,1)} %copy-done.19), channel_id=1, source_target_pairs={{0,24},{4,28},{8,0},{12,4},{16,8},{20,12},{24,16},{28,20},{1,25},{... | collective-permute-start | bytes 786440 | tf_op jit(solution)/shard_map/ppermute | solution.py:17
  128.8 11.5 %copy-start.24 = (s32[1,128,2]{1,2,0:T(2,128)S(1)}, s32[1,128,2]{1,2,0:T(2,128)}, u32[]{:S(2)}) copy-start(s32[1,128,2]{1,2,0:T(2,128)} %param.13) | copy-start | bytes 3076
  128.8 11.5 %copy-start.25 = (f32[1,128,2]{1,2,0:T(2,128)S(1)}, f32[1,128,2]{1,2,0:T(2,128)}, u32[]{:S(2)}) copy-start(f32[1,128,2]{1,2,0:T(2,128)} %param.14) | copy-start | bytes 3076
  128.9 11.6 %copy-start.8 = (bf16[256,4096]{1,0:T(8,128)(2,1)S(1)}, bf16[256,4096]{1,0:T(8,128)(2,1)}, u32[]{:S(2)}) copy-start(bf16[256,4096]{1,0:T(8,128)(2,1)} %copy-done.7) | copy-start | bytes 6291460
  133.6 14.2 %collective-permute-start.29 = (bf16[64,4096]{1,0:T(8,128)(2,1)S(1)}, bf16[64,4096]{1,0:T(8,128)(2,1)S(1)}, u32[]{:S(2)}, u32[]{:S(2)}) collective-permute-start(bf16[64,4096]{1,0:T(8,128)(2,1)S(1)} %add_convert_fusion), channel_id=1, source_target_pairs={{0,24},{4,28},{8,0},{12,4},{16,8},{20,12},{24,16},{28,20},{1,25},{... | collective-permute-start | bytes 1572872 | tf_op jit(solution)/shard_map/ppermute | solution.py:17
  136.6 13.7 %collective-permute-start.28 = (bf16[64,4096]{1,0:T(8,128)(2,1)S(1)}, bf16[64,4096]{1,0:T(8,128)(2,1)S(1)}, u32[]{:S(2)}, u32[]{:S(2)}) collective-permute-start(bf16[64,4096]{1,0:T(8,128)(2,1)S(1)} %add_convert_fusion.1), channel_id=1, source_target_pairs={{0,8},{4,12},{8,16},{12,20},{16,24},{20,28},{24,0},{28,4},{1,9},{5... | collective-permute-start | bytes 1572872 | tf_op jit(solution)/shard_map/ppermute | solution.py:17
  136.7 10.3 %collective-permute-start.30 = (bf16[64,1024]{1,0:T(8,128)(2,1)S(1)}, bf16[64,1024]{1,0:T(8,128)(2,1)S(1)}, u32[]{:S(2)}, u32[]{:S(2)}) collective-permute-start(bf16[64,1024]{1,0:T(8,128)(2,1)S(1)} %get-tuple-element.152), channel_id=1, source_target_pairs={{0,3},{1,2},{2,1},{3,0},{4,7},{5,6},{6,5},{7,4},{8,11},{9,10},{10,... | collective-permute-start | bytes 393224 | tf_op jit(solution)/shard_map/ppermute | solution.py:27
  137.9 9.9 %collective-permute-start.31 = (bf16[64,1024]{1,0:T(8,128)(2,1)S(1)}, bf16[64,1024]{1,0:T(8,128)(2,1)S(1)}, u32[]{:S(2)}, u32[]{:S(2)}) collective-permute-start(bf16[64,1024]{1,0:T(8,128)(2,1)S(1)} %get-tuple-element.153), channel_id=1, source_target_pairs={{0,2},{1,3},{2,0},{3,1},{4,6},{5,7},{6,4},{7,5},{8,10},{9,11},{10,... | collective-permute-start | bytes 393224 | tf_op jit(solution)/shard_map/ppermute | solution.py:27
  139.3 8.4 %collective-permute-start.32 = (bf16[64,1024]{1,0:T(8,128)(2,1)S(1)}, bf16[64,1024]{1,0:T(8,128)(2,1)S(1)}, u32[]{:S(2)}, u32[]{:S(2)}) collective-permute-start(bf16[64,1024]{1,0:T(8,128)(2,1)S(1)} %get-tuple-element.154), channel_id=1, source_target_pairs={{0,1},{1,0},{2,3},{3,2},{4,5},{5,4},{6,7},{7,6},{8,9},{9,8},{10,11... | collective-permute-start | bytes 393224 | tf_op jit(solution)/shard_map/ppermute | solution.py:27
  140.5 9.8 %copy-start.14 = (f32[64,4096]{1,0:T(8,128)S(1)}, f32[64,4096]{1,0:T(8,128)}, u32[]{:S(2)}) copy-start(f32[64,4096]{1,0:T(8,128)} %copy-done.13) | copy-start | bytes 3145732
  150.5 11.3 %collective-permute-start.33 = (bf16[64,1024]{1,0:T(8,128)(2,1)S(1)}, bf16[64,1024]{1,0:T(8,128)(2,1)S(1)}, u32[]{:S(2)}, u32[]{:S(2)}) collective-permute-start(bf16[64,1024]{1,0:T(8,128)(2,1)S(1)} %get-tuple-element.181), channel_id=1, source_target_pairs={{0,3},{1,2},{2,1},{3,0},{4,7},{5,6},{6,5},{7,4},{8,11},{9,10},{10,... | collective-permute-start | bytes 393224 | tf_op jit(solution)/shard_map/ppermute | solution.py:27
  151.7 10.1 %collective-permute-start.34 = (bf16[64,1024]{1,0:T(8,128)(2,1)S(1)}, bf16[64,1024]{1,0:T(8,128)(2,1)S(1)}, u32[]{:S(2)}, u32[]{:S(2)}) collective-permute-start(bf16[64,1024]{1,0:T(8,128)(2,1)S(1)} %get-tuple-element.180), channel_id=1, source_target_pairs={{0,2},{1,3},{2,0},{3,1},{4,6},{5,7},{6,4},{7,5},{8,10},{9,11},{10,... | collective-permute-start | bytes 393224 | tf_op jit(solution)/shard_map/ppermute | solution.py:27
  153.4 8.4 %collective-permute-start.35 = (bf16[64,1024]{1,0:T(8,128)(2,1)S(1)}, bf16[64,1024]{1,0:T(8,128)(2,1)S(1)}, u32[]{:S(2)}, u32[]{:S(2)}) collective-permute-start(bf16[64,1024]{1,0:T(8,128)(2,1)S(1)} %get-tuple-element.179), channel_id=1, source_target_pairs={{0,1},{1,0},{2,3},{3,2},{4,5},{5,4},{6,7},{7,6},{8,9},{9,8},{10,11... | collective-permute-start | bytes 393224 | tf_op jit(solution)/shard_map/ppermute | solution.py:27
  (14 other events, 25.7 us)

commit v6 on v5

--- a/solution.py
+++ b/solution.py
@@ -457,14 +457,23 @@
     fwd_wide = widen(fwd_buf, (three, two, one), place)
     three, two, one = ask_mp(grad_buf)
     back_buf, three = together(pack(back_pick, held_rows), three)
-    fwd_behind, fwd_ahead, three, two, one, back_one, back_buf = together(
-        *both_ways(fwd_wide, fwd_wide), three, two, one, along_mp(back_buf, 1), back_buf
+    fwd_behind, fwd_ahead = both_ways(fwd_wide, fwd_wide)
+    fwd_behind, fwd_ahead, low, high, three, two, one, back_one, back_buf = together(
+        fwd_behind,
+        fwd_ahead,
+        fwd_behind[:half],
+        fwd_ahead[half:],
+        three,
+        two,
+        one,
+        along_mp(back_buf, 1),
+        back_buf,
     )
 
     grad_wide = widen(grad_buf, (three, two, one), place)
-    grad_sent = stacked(fwd_behind[:half], grad_wide)
+    grad_sent = stacked(low, grad_wide)
     cw, ccw, three, two, up_x, down_w = together(
-        *both_ways(grad_sent, stacked(fwd_ahead[half:], grad_wide)),
+        *both_ways(grad_sent, stacked(high, grad_wide)),
         *(along_mp(back_buf, flip) for flip in (3, 2)),
         other_core(up_w),
         down_w,

time: 165 us -> 164 us (level)
    ppermute x15, waiting for transfers between devices: 22.8 us -> 19.4 us  [along_mp(): return lax.ppermute(array, 'mp', [(i, i ^ flip) for i in range(n)])]
    ppermute x14, waiting for transfers between devices: 36.8 us -> 38.6 us  [along_y(): lax.ppermute(array, 'expert', [(i, (i + 2 * step) % n) for i in range(n)])]
  transfers between devices with their start and end apart: 36 -> 36, of which waited for: 18 -> 19; matrix products, arithmetic and copies ran while one was open for 8% -> 8% of each run, Pallas kernels for 16% -> 16%
where the time goes in v6:
time: 164 us; the launch traced here: 161 us
  waiting for transfers between devices  63.8 us (39%)
  starting transfers between devices  47.7 us (29%)
  Pallas kernels  26.5 us (16%)
  other arithmetic  9.16 us (6%)
  local copies, waits for them, and re-layouts  7.99 us (5%)
  matrix products  3.53 us (2%)
  between operations  2.63 us (2%)
    ppermute x14, waiting for transfers between devices, along_y(): lax.ppermute(array, 'expert', [(i, (i + 2 * step) % n) for i in range(n)])  38.6 us
    ppermute x14, starting transfers between devices, along_y(): lax.ppermute(array, 'expert', [(i, (i + 2 * step) % n) for i in range(n)])  21.9 us
    ppermute x15, waiting for transfers between devices, along_mp(): return lax.ppermute(array, 'mp', [(i, i ^ flip) for i in range(n)])  19.4 us
    ppermute x15, starting transfers between devices, along_mp(): return lax.ppermute(array, 'mp', [(i, i ^ flip) for i in range(n)])  18.2 us
    pallas_call x1, Pallas kernels, run_back(): pl.pallas_call(back_kernel, out_shape=block_shapes(width) + (hidden(1), h...  8.84 us
    pallas_call x2, Pallas kernels, run_weights(): pl.pallas_call(weight_kernel, grid=(width // step,), out_shape=(jax.Shape...  8.44 us
    ppermute x1, starting transfers between devices, mirrored(): lax.ppermute(array, ('section', 'mp'), [(i, last - i) for i in range(last...  6.88 us
    pallas_call x1, Pallas kernels, run_fwd(): pl.pallas_call(fwd_kernel, out_shape=block_shapes(width), in_specs=[HBM]...  6.6 us
  transfers between devices with their start and end apart: 36, of which 19 were waited for; matrix products, arithmetic and copies ran while one was open for 8% of the time, Pallas kernels for 16%

profile of v6, /device:TPU:32, one launch (start us, length us, event | category | flops | bytes accessed | tf_op | source)
XLA Modules:
  0.0 161.2 jit_solution(12375326238190791340)
XLA Ops:
  2.6 1.1 convolution_convert_fusion.4
  3.7 2.0 %collective-permute-start = (bf16[64,1024]{1,0:T(8,128)(2,1)S(1)}, bf16[64,1024]{1,0:T(8,128)(2,1)S(1)}, u32[]{:S(2)}, u32[]{:S(2)}) collective-permute-start(bf16[64,1024]{1,0:T(8,128)(2,1)S(1)} %convolution_convert_fusion.4), channel_id=1, source_target_pairs={{0,3},{1,2},{2,1},{3,0},{4,7},{5,6},{6,5},{7,4},{8,11},{9,10},{10,... | collective-permute-start | bytes 393224 | tf_op jit(solution)/shard_map/ppermute | solution.py:27
  5.7 2.3 %collective-permute-start.1 = (bf16[64,1024]{1,0:T(8,128)(2,1)S(1)}, bf16[64,1024]{1,0:T(8,128)(2,1)}, u32[]{:S(2)}, u32[]{:S(2)}) collective-permute-start(bf16[64,1024]{1,0:T(8,128)(2,1)S(1)} %convolution_convert_fusion.4), channel_id=1, source_target_pairs={{0,2},{1,3},{2,0},{3,1},{4,6},{5,7},{6,4},{7,5},{8,10},{9,11},{10,... | collective-permute-start | bytes 393224 | tf_op jit(solution)/shard_map/ppermute | solution.py:27
  9.2 6.9 %collective-permute-start.6 = (bf16[128,1024]{1,0:T(8,128)(2,1)S(1)}, bf16[128,1024]{1,0:T(8,128)(2,1)S(1)}, u32[]{:S(2)}, u32[]{:S(2)}) collective-permute-start(bf16[128,1024]{1,0:T(8,128)(2,1)S(1)} %dynamic-slice_bitcast_fusion), channel_id=1, source_target_pairs={{0,227},{1,226},{2,225},{3,224},{32,195},{33,194},{34,193},{35,192... | collective-permute-start | bytes 786440 | tf_op jit(solution)/shard_map/ppermute | solution.py:33
  18.3 1.3 broadcast_select_fusion.15
  19.8 1.7 %collective-permute-start.4 = (bf16[64,4096]{1,0:T(8,128)(2,1)S(1)}, bf16[64,4096]{1,0:T(8,128)(2,1)S(1)}, u32[]{:S(2)}, u32[]{:S(2)}) collective-permute-start(bf16[64,4096]{1,0:T(8,128)(2,1)S(1)} %pad_maximum_fusion.6.refs_0_), channel_id=1, source_target_pairs={{0,8},{4,12},{8,16},{12,20},{16,24},{20,28},{24,0},{28,4},{1,9},{5... | collective-permute-start | bytes 1572872 | tf_op jit(solution)/shard_map/ppermute | solution.py:17
  21.4 1.7 %collective-permute-start.5 = (bf16[64,4096]{1,0:T(8,128)(2,1)S(1)}, bf16[64,4096]{1,0:T(8,128)(2,1)S(1)}, u32[]{:S(2)}, u32[]{:S(2)}) collective-permute-start(bf16[64,4096]{1,0:T(8,128)(2,1)S(1)} %pad_maximum_fusion.6.refs_0_), channel_id=1, source_target_pairs={{0,24},{4,28},{8,0},{12,4},{16,8},{20,12},{24,16},{28,20},{1,25},{... | collective-permute-start | bytes 1572872 | tf_op jit(solution)/shard_map/ppermute | solution.py:17
  23.1 1.0 collective-permute-start.7
  24.1 5.8 %collective-permute-done.6 = bf16[128,1024]{1,0:T(8,128)(2,1)S(1)} collective-permute-done((bf16[128,1024]{1,0:T(8,128)(2,1)S(1)}, bf16[128,1024]{1,0:T(8,128)(2,1)S(1)}, u32[]{:S(2)}, u32[]{:S(2)}) %collective-permute-start.6) | collective-permute-done | bytes 262176 | tf_op jit(solution)/shard_map/ppermute | solution.py:33
  30.1 2.5 %collective-permute-start.9 = (bf16[64,1024]{1,0:T(8,128)(2,1)S(1)}, bf16[64,1024]{1,0:T(8,128)(2,1)S(1)}, u32[]{:S(2)}, u32[]{:S(2)}) collective-permute-start(bf16[64,1024]{1,0:T(8,128)(2,1)S(1)} %convolution_convert_fusion.3), channel_id=1, source_target_pairs={{0,1},{1,0},{2,3},{3,2},{4,5},{5,4},{6,7},{7,6},{8,9},{9,8},{10,11... | collective-permute-start | bytes 393224 | tf_op jit(solution)/shard_map/ppermute | solution.py:27
  32.7 1.8 %collective-permute-done.4.refs_1_ = bf16[64,4096]{1,0:T(8,128)(2,1)S(1)} collective-permute-done((bf16[64,4096]{1,0:T(8,128)(2,1)S(1)}, bf16[64,4096]{1,0:T(8,128)(2,1)S(1)}, u32[]{:S(2)}, u32[]{:S(2)}) %collective-permute-start.4) | collective-permute-done | bytes 524320 | tf_op jit(solution)/shard_map/ppermute | solution.py:17
  36.1 1.3 collective-permute-done.8
  37.4 2.4 %collective-permute-done.9 = bf16[64,1024]{1,0:T(8,128)(2,1)S(1)} collective-permute-done((bf16[64,1024]{1,0:T(8,128)(2,1)S(1)}, bf16[64,1024]{1,0:T(8,128)(2,1)S(1)}, u32[]{:S(2)}, u32[]{:S(2)}) %collective-permute-start.9) | collective-permute-done | bytes 131104 | tf_op jit(solution)/shard_map/ppermute | solution.py:27
  39.8 1.8 %collective-permute-done.10 = bf16[64,1024]{1,0:T(8,128)(2,1)S(1)} collective-permute-done((bf16[64,1024]{1,0:T(8,128)(2,1)S(1)}, bf16[64,1024]{1,0:T(8,128)(2,1)S(1)}, u32[]{:S(2)}, u32[]{:S(2)}) %collective-permute-start.10) | collective-permute-done | bytes 131104 | tf_op jit(solution)/shard_map/ppermute | solution.py:27
  41.8 1.3 pad_maximum_fusion.2
  43.1 1.6 collective-permute-start.11
  44.7 1.7 %collective-permute-start.12 = (bf16[96,4096]{1,0:T(8,128)(2,1)}, bf16[96,4096]{1,0:T(8,128)(2,1)}, u32[]{:S(2)}, u32[]{:S(2)}) collective-permute-start(bf16[96,4096]{1,0:T(8,128)(2,1)} %get-tuple-element.193), channel_id=1, source_target_pairs={{0,24},{4,28},{8,0},{12,4},{16,8},{20,12},{24,16},{28,20},{1,25},{... | collective-permute-start | bytes 2359304 | tf_op jit(solution)/shard_map/ppermute | solution.py:17
  46.3 1.0 collective-permute-start.13
  47.4 1.6 collective-permute-start.14
  48.9 7.7 %collective-permute-done.13 = bf16[64,1024]{1,0:T(8,128)(2,1)S(1)} collective-permute-done((bf16[64,1024]{1,0:T(8,128)(2,1)S(1)}, bf16[64,1024]{1,0:T(8,128)(2,1)S(1)}, u32[]{:S(2)}, u32[]{:S(2)}) %collective-permute-start.13) | collective-permute-done | bytes 131104 | tf_op jit(solution)/shard_map/ppermute | solution.py:27
  57.3 5.8 %collective-permute-done.11.refs_3_.refs_1_ = bf16[96,4096]{1,0:T(8,128)(2,1)S(1)} collective-permute-done((bf16[96,4096]{1,0:T(8,128)(2,1)}, bf16[96,4096]{1,0:T(8,128)(2,1)S(1)}, u32[]{:S(2)}, u32[]{:S(2)}) %collective-permute-start.11) | collective-permute-done | bytes 786464 | tf_op jit(solution)/shard_map/ppermute | solution.py:17
  63.4 1.0 slice.33
  64.4 1.0 broadcast_select_fusion.9
  65.7 1.8 %collective-permute-start.16 = (bf16[96,4096]{1,0:T(8,128)(2,1)S(1)}, bf16[96,4096]{1,0:T(8,128)(2,1)S(1)}, u32[]{:S(2)}, u32[]{:S(2)}) collective-permute-start(bf16[96,4096]{1,0:T(8,128)(2,1)S(1)} %get-tuple-element.190.refs_0_), channel_id=1, source_target_pairs={{0,8},{4,12},{8,16},{12,20},{16,24},{20,28},{24,0},{28,4},{1,9},{5... | collective-permute-start | bytes 2359304 | tf_op jit(solution)/shard_map/ppermute | solution.py:17
  67.5 1.7 %collective-permute-start.17 = (bf16[96,4096]{1,0:T(8,128)(2,1)S(1)}, bf16[96,4096]{1,0:T(8,128)(2,1)S(1)}, u32[]{:S(2)}, u32[]{:S(2)}) collective-permute-start(bf16[96,4096]{1,0:T(8,128)(2,1)S(1)} %get-tuple-element.189), channel_id=1, source_target_pairs={{0,24},{4,28},{8,0},{12,4},{16,8},{20,12},{24,16},{28,20},{1,25},{... | collective-permute-start | bytes 2359304 | tf_op jit(solution)/shard_map/ppermute | solution.py:17
  69.2 6.6 %shard_map.155 = (f32[64,4096]{1,0:T(8,128)S(1)}, bf16[64,4096]{1,0:T(8,128)(2,1)S(1)}, bf16[64,4096]{1,0:T(8,128)(2,1)S(1)}, bf16[32,4096]{1,0:T(8,128)(2,1)S(1)}, bf16[32,4096]{1,0:T(8,128)(2,1)S(1)}) custom-call(bf16[64,4096]{1,0:T(8,128)(2,1)S(1)} %copy-done.6, bf16[64,4096]{1,0:T(8,128)(2,1)S(1)} %copy-done.10, bf16[64,4096]{1,0:T(8,128)(2,1)S(1)} %copy-done.12, ...), custom_call_target="tpu_custom_call" | custom-call | flops 1 | bytes 1 | tf_op jit(solution)/shard_map/pallas_call | solution.py:320
  75.9 11.3 %collective-permute-done.16.refs_3_.refs_1_ = bf16[96,4096]{1,0:T(8,128)(2,1)S(1)} collective-permute-done((bf16[96,4096]{1,0:T(8,128)(2,1)S(1)}, bf16[96,4096]{1,0:T(8,128)(2,1)S(1)}, u32[]{:S(2)}, u32[]{:S(2)}) %collective-permute-start.16) | collective-permute-done | bytes 786464 | tf_op jit(solution)/shard_map/ppermute | solution.py:17
  87.3 3.0 %collective-permute-start.20 = (bf16[64,4096]{1,0:T(8,128)(2,1)S(1)}, bf16[64,4096]{1,0:T(8,128)(2,1)S(1)}, u32[]{:S(2)}, u32[]{:S(2)}) collective-permute-start(bf16[64,4096]{1,0:T(8,128)(2,1)S(1)} %pad_maximum_fusion.8), channel_id=1, source_target_pairs={{0,24},{4,28},{8,0},{12,4},{16,8},{20,12},{24,16},{28,20},{1,25},{... | collective-permute-start | bytes 1572872 | tf_op jit(solution)/shard_map/ppermute | solution.py:17
  90.5 2.6 %shard_map.156 = (f32[448,256]{1,0:T(8,128)S(1)}, bf16[256,4096]{1,0:T(8,128)(2,1)S(1)}) custom-call(bf16[96,4096]{1,0:T(8,128)(2,1)} %get-tuple-element.194.refs_0_, bf16[96,4096]{1,0:T(8,128)(2,1)S(1)} %collective-permute-done.11.refs_3_.refs_1_, bf16[96,4096]{1,0:T(8,128)(2,1)} %collective-permute-done.12.refs_4_.refs_2_, ...), custom_call_target="tpu_custom_call" | custom-call | flops 1 | bytes 1 | tf_op jit(solution)/shard_map/pallas_call | solution.py:333
  93.1 8.1 %collective-permute-done.20.refs_4_ = bf16[64,4096]{1,0:T(8,128)(2,1)S(1)} collective-permute-done((bf16[64,4096]{1,0:T(8,128)(2,1)S(1)}, bf16[64,4096]{1,0:T(8,128)(2,1)S(1)}, u32[]{:S(2)}, u32[]{:S(2)}) %collective-permute-start.20) | collective-permute-done | bytes 524320 | tf_op jit(solution)/shard_map/ppermute | solution.py:17
  101.1 3.6 %collective-permute-done.19.refs_3_ = bf16[64,4096]{1,0:T(8,128)(2,1)S(1)} collective-permute-done((bf16[64,4096]{1,0:T(8,128)(2,1)S(1)}, bf16[64,4096]{1,0:T(8,128)(2,1)S(1)}, u32[]{:S(2)}, u32[]{:S(2)}) %collective-permute-start.19) | collective-permute-done | bytes 524320 | tf_op jit(solution)/shard_map/ppermute | solution.py:17
  105.2 2.2 %collective-permute-start.21 = (bf16[64,4096]{1,0:T(8,128)(2,1)S(1)}, bf16[64,4096]{1,0:T(8,128)(2,1)S(1)}, u32[]{:S(2)}, u32[]{:S(2)}) collective-permute-start(bf16[64,4096]{1,0:T(8,128)(2,1)S(1)} %add_convert_fusion.3), channel_id=1, source_target_pairs={{0,8},{4,12},{8,16},{12,20},{16,24},{20,28},{24,0},{28,4},{1,9},{5... | collective-permute-start | bytes 1572872 | tf_op jit(solution)/shard_map/ppermute | solution.py:17
  107.4 8.8 %shard_map.157 = (f32[64,4096]{1,0:T(8,128)S(1)}, bf16[64,4096]{1,0:T(8,128)(2,1)S(1)}, bf16[64,4096]{1,0:T(8,128)(2,1)S(1)}, bf16[32,4096]{1,0:T(8,128)(2,1)S(1...) custom-call(bf16[96,4096]{1,0:T(8,128)(2,1)S(1)} %get-tuple-element., ...), custom_call_target="tpu_custom_call" | custom-call | flops 1 | bytes 1 | tf_op jit(solution)/shard_map/pallas_call | solution.py:353
  122.8 2.7 %collective-permute-start.25 = (bf16[32,4096]{1,0:T(8,128)(2,1)}, bf16[32,4096]{1,0:T(8,128)(2,1)S(1)}, u32[]{:S(2)}, u32[]{:S(2)}) collective-permute-start(bf16[32,4096]{1,0:T(8,128)(2,1)} %copy-done.19), channel_id=1, source_target_pairs={{0,24},{4,28},{8,0},{12,4},{16,8},{20,12},{24,16},{28,20},{1,25},{... | collective-permute-start | bytes 786440 | tf_op jit(solution)/shard_map/ppermute | solution.py:17
  125.5 1.7 %fusion.19 = (bf16[64,4096]{1,0:T(8,128)(2,1)S(1)}, f32[64,4096]{1,0:T(8,128)S(1)}) fusion(bf16[64,4096]{1,0:T(8,128)(2,1)} %copy-done.21, f32[64,4096]{1,0:T(8,128)} %copy-done.15, bf16[64,4096]{1,0:T(8,128)(2,1)} %copy-done.22), kind=kLoop, calls=%fused_computation.84 | loop fusion | flops 1310720 | bytes 3670016 | tf_op jit(solution)/shard_map/convert_element_type | solution.py:414
  127.3 4.6 %collective-permute-done.24 = bf16[32,4096]{1,0:T(8,128)(2,1)S(1)} collective-permute-done((bf16[32,4096]{1,0:T(8,128)(2,1)}, bf16[32,4096]{1,0:T(8,128)(2,1)S(1)}, u32[]{:S(2)}, u32[]{:S(2)}) %collective-permute-start.24) | collective-permute-done | bytes 262176 | tf_op jit(solution)/shard_map/ppermute | solution.py:17
  132.0 3.0 %collective-permute-start.29 = (bf16[64,4096]{1,0:T(8,128)(2,1)S(1)}, bf16[64,4096]{1,0:T(8,128)(2,1)S(1)}, u32[]{:S(2)}, u32[]{:S(2)}) collective-permute-start(bf16[64,4096]{1,0:T(8,128)(2,1)S(1)} %add_convert_fusion), channel_id=1, source_target_pairs={{0,24},{4,28},{8,0},{12,4},{16,8},{20,12},{24,16},{28,20},{1,25},{... | collective-permute-start | bytes 1572872 | tf_op jit(solution)/shard_map/ppermute | solution.py:17
  135.1 1.1 collective-permute-start.30
  136.3 1.5 collective-permute-start.31
  138.9 3.0 %shard_map.158 = bf16[224,4096]{1,0:T(8,128)(2,1)} custom-call(bf16[224,256]{1,0:T(8,128)(2,1)S(1)} %get-tuple-element.159.hidden_ref, bf16[224,256]{1,0:T(8,128)(2,1)S(1)} %slice.38.hidden_x_ref, bf16[256,4096]{1,0:T(8,128)(2,1)S(1)} %copy-done.8, bf16[256,4096]{1,0:T(8,128)(2,1)S(1)} %collective-permute-done.23.rows_x_ref), custom_call_target="tpu_custom_call" | custom-call | flops 1 | bytes 1 | tf_op jit(solution)/shard_map/pallas_call | solution.py:380
  141.9 3.5 %collective-permute-done.30 = bf16[64,1024]{1,0:T(8,128)(2,1)S(1)} collective-permute-done((bf16[64,1024]{1,0:T(8,128)(2,1)S(1)}, bf16[64,1024]{1,0:T(8,128)(2,1)S(1)}, u32[]{:S(2)}, u32[]{:S(2)}) %collective-permute-start.30) | collective-permute-done | bytes 131104 | tf_op jit(solution)/shard_map/ppermute | solution.py:27
  146.2 2.6 %collective-permute-done.28 = bf16[64,4096]{1,0:T(8,128)(2,1)S(1)} collective-permute-done((bf16[64,4096]{1,0:T(8,128)(2,1)S(1)}, bf16[64,4096]{1,0:T(8,128)(2,1)S(1)}, u32[]{:S(2)}, u32[]{:S(2)}) %collective-permute-start.28) | collective-permute-done | bytes 524320 | tf_op jit(solution)/shard_map/ppermute | solution.py:17
  148.9 1.1 collective-permute-start.33
  150.1 1.7 %collective-permute-start.34 = (bf16[64,1024]{1,0:T(8,128)(2,1)S(1)}, bf16[64,1024]{1,0:T(8,128)(2,1)S(1)}, u32[]{:S(2)}, u32[]{:S(2)}) collective-permute-start(bf16[64,1024]{1,0:T(8,128)(2,1)S(1)} %get-tuple-element.184), channel_id=1, source_target_pairs={{0,2},{1,3},{2,0},{3,1},{4,6},{5,7},{6,4},{7,5},{8,10},{9,11},{10,... | collective-permute-start | bytes 393224 | tf_op jit(solution)/shard_map/ppermute | solution.py:27
  152.5 5.4 %shard_map.159 = (bf16[224,4096]{1,0:T(8,128)(2,1)}, bf16[224,4096]{1,0:T(8,128)(2,1)}) custom-call(bf16[448,256]{1,0:T(8,128)(2,1)S(1)} %get-tuple-element.169.hidden_ref, bf16[448,256]{1,0:T(8,128)(2,1)S(1)} %slice.39.hidden_x_ref, bf16[256,4096]{1,0:T(8,128)(2,1)} %get-tuple-element.147.rows_ref, bf16[256,4096]{1,0:T(8,128)(2,1)} %collective-permute-done.27.rows_x_ref), custom_call_target="tpu_custom_call" | custom-call | flops 1 | bytes 1 | tf_op jit(solution)/shard_map/pallas_call | solution.py:380
  157.9 1.0 fusion
  158.9 1.3 collective-permute-done.33
  160.2 1.0 fusion.1
  (134 shorter events, 17.6 us)
Async XLA Ops:
  0.6 8.6 %copy-start = (bf16[1,2,128,1024]{3,2,1,0:T(8,128)(2,1)S(1)}, bf16[1,2,128,1024]{3,2,1,0:T(8,128)(2,1)}, u32[]{:S(2)}) copy-start(bf16[1,2,128,1024]{3,2,1,0:T(8,128)(2,1)} %param.15) | copy-start | bytes 1572868
  0.6 17.3 %copy-start.23 = (bf16[1,128,1024]{2,1,0:T(8,128)(2,1)S(1)}, bf16[1,128,1024]{2,1,0:T(8,128)(2,1)}, u32[]{:S(2)}) copy-start(bf16[1,128,1024]{2,1,0:T(8,128)(2,1)} %param.19) | copy-start | bytes 786436
  0.7 17.6 %collective-permute-start.3 = (bf16[224,4096]{1,0:T(8,128)(2,1)}, bf16[224,4096]{1,0:T(8,128)(2,1)S(1)}, u32[]{:S(2)}, u32[]{:S(2)}) collective-permute-start(bf16[224,4096]{1,0:T(8,128)(2,1)} %bitcast.38), channel_id=1, source_target_pairs={{0,4},{4,0},{8,12},{12,8},{16,20},{20,16},{24,28},{28,24},{1,5},{5... | collective-permute-start | bytes 5505032 | tf_op jit(solution)/shard_map/ppermute | solution.py:22
  3.7 14.5 %collective-permute-start = (bf16[64,1024]{1,0:T(8,128)(2,1)S(1)}, bf16[64,1024]{1,0:T(8,128)(2,1)S(1)}, u32[]{:S(2)}, u32[]{:S(2)}) collective-permute-start(bf16[64,1024]{1,0:T(8,128)(2,1)S(1)} %convolution_convert_fusion.4), channel_id=1, source_target_pairs={{0,3},{1,2},{2,1},{3,0},{4,7},{5,6},{6,5},{7,4},{8,11},{9,10},{10,... | collective-permute-start | bytes 393224 | tf_op jit(solution)/shard_map/ppermute | solution.py:27
  5.7 12.5 %collective-permute-start.1 = (bf16[64,1024]{1,0:T(8,128)(2,1)S(1)}, bf16[64,1024]{1,0:T(8,128)(2,1)}, u32[]{:S(2)}, u32[]{:S(2)}) collective-permute-start(bf16[64,1024]{1,0:T(8,128)(2,1)S(1)} %convolution_convert_fusion.4), channel_id=1, source_target_pairs={{0,2},{1,3},{2,0},{3,1},{4,6},{5,7},{6,4},{7,5},{8,10},{9,11},{10,... | collective-permute-start | bytes 393224 | tf_op jit(solution)/shard_map/ppermute | solution.py:27
  8.0 10.2 %collective-permute-start.2 = (bf16[64,1024]{1,0:T(8,128)(2,1)S(1)}, bf16[64,1024]{1,0:T(8,128)(2,1)}, u32[]{:S(2)}, u32[]{:S(2)}) collective-permute-start(bf16[64,1024]{1,0:T(8,128)(2,1)S(1)} %convolution_convert_fusion.4), channel_id=1, source_target_pairs={{0,1},{1,0},{2,3},{3,2},{4,5},{5,4},{6,7},{7,6},{8,9},{9,8},{10,11... | collective-permute-start | bytes 393224 | tf_op jit(solution)/shard_map/ppermute | solution.py:27
  9.2 20.6 %collective-permute-start.6 = (bf16[128,1024]{1,0:T(8,128)(2,1)S(1)}, bf16[128,1024]{1,0:T(8,128)(2,1)S(1)}, u32[]{:S(2)}, u32[]{:S(2)}) collective-permute-start(bf16[128,1024]{1,0:T(8,128)(2,1)S(1)} %dynamic-slice_bitcast_fusion), channel_id=1, source_target_pairs={{0,227},{1,226},{2,225},{3,224},{32,195},{33,194},{34,193},{35,192... | collective-permute-start | bytes 786440 | tf_op jit(solution)/shard_map/ppermute | solution.py:33
  19.7 22.0 %copy-start.5 = (bf16[64,4096]{1,0:T(8,128)(2,1)}, bf16[64,4096]{1,0:T(8,128)(2,1)S(1)}, u32[]{:S(2)}) copy-start(bf16[64,4096]{1,0:T(8,128)(2,1)S(1)} %pad_maximum_fusion.6.refs_0_) | copy-start | bytes 1572868
  19.8 14.7 %collective-permute-start.4 = (bf16[64,4096]{1,0:T(8,128)(2,1)S(1)}, bf16[64,4096]{1,0:T(8,128)(2,1)S(1)}, u32[]{:S(2)}, u32[]{:S(2)}) collective-permute-start(bf16[64,4096]{1,0:T(8,128)(2,1)S(1)} %pad_maximum_fusion.6.refs_0_), channel_id=1, source_target_pairs={{0,8},{4,12},{8,16},{12,20},{16,24},{20,28},{24,0},{28,4},{1,9},{5... | collective-permute-start | bytes 1572872 | tf_op jit(solution)/shard_map/ppermute | solution.py:17
  21.4 13.9 %collective-permute-start.5 = (bf16[64,4096]{1,0:T(8,128)(2,1)S(1)}, bf16[64,4096]{1,0:T(8,128)(2,1)S(1)}, u32[]{:S(2)}, u32[]{:S(2)}) collective-permute-start(bf16[64,4096]{1,0:T(8,128)(2,1)S(1)} %pad_maximum_fusion.6.refs_0_), channel_id=1, source_target_pairs={{0,24},{4,28},{8,0},{12,4},{16,8},{20,12},{24,16},{28,20},{1,25},{... | collective-permute-start | bytes 1572872 | tf_op jit(solution)/shard_map/ppermute | solution.py:17
  23.1 9.6 %collective-permute-start.7 = (bf16[64,1024]{1,0:T(8,128)(2,1)S(1)}, bf16[64,1024]{1,0:T(8,128)(2,1)S(1)}, u32[]{:S(2)}, u32[]{:S(2)}) collective-permute-start(bf16[64,1024]{1,0:T(8,128)(2,1)S(1)} %convolution_convert_fusion.3), channel_id=1, source_target_pairs={{0,3},{1,2},{2,1},{3,0},{4,7},{5,6},{6,5},{7,4},{8,11},{9,10},{10,... | collective-permute-start | bytes 393224 | tf_op jit(solution)/shard_map/ppermute | solution.py:27
  30.0 7.4 %collective-permute-start.8 = (bf16[64,1024]{1,0:T(8,128)(2,1)S(1)}, bf16[64,1024]{1,0:T(8,128)(2,1)S(1)}, u32[]{:S(2)}, u32[]{:S(2)}) collective-permute-start(bf16[64,1024]{1,0:T(8,128)(2,1)S(1)} %convolution_convert_fusion.3), channel_id=1, source_target_pairs={{0,2},{1,3},{2,0},{3,1},{4,6},{5,7},{6,4},{7,5},{8,10},{9,11},{10,... | collective-permute-start | bytes 393224 | tf_op jit(solution)/shard_map/ppermute | solution.py:27
  30.1 9.7 %collective-permute-start.9 = (bf16[64,1024]{1,0:T(8,128)(2,1)S(1)}, bf16[64,1024]{1,0:T(8,128)(2,1)S(1)}, u32[]{:S(2)}, u32[]{:S(2)}) collective-permute-start(bf16[64,1024]{1,0:T(8,128)(2,1)S(1)} %convolution_convert_fusion.3), channel_id=1, source_target_pairs={{0,1},{1,0},{2,3},{3,2},{4,5},{5,4},{6,7},{7,6},{8,9},{9,8},{10,11... | collective-permute-start | bytes 393224 | tf_op jit(solution)/shard_map/ppermute | solution.py:27
  32.6 9.0 %collective-permute-start.10 = (bf16[64,1024]{1,0:T(8,128)(2,1)S(1)}, bf16[64,1024]{1,0:T(8,128)(2,1)S(1)}, u32[]{:S(2)}, u32[]{:S(2)}) collective-permute-start(bf16[64,1024]{1,0:T(8,128)(2,1)S(1)} %convolution_convert_fusion.2), channel_id=1, source_target_pairs={{0,1},{1,0},{2,3},{3,2},{4,5},{5,4},{6,7},{7,6},{8,9},{9,8},{10,11... | collective-permute-start | bytes 393224 | tf_op jit(solution)/shard_map/ppermute | solution.py:27
  34.5 14.5 %collective-permute-start.15 = (bf16[224,4096]{1,0:T(8,128)(2,1)}, bf16[224,4096]{1,0:T(8,128)(2,1)}, u32[]{:S(2)}, u32[]{:S(2)}) collective-permute-start(bf16[224,4096]{1,0:T(8,128)(2,1)} %bitcast.8.refs_6_.refs_7_), channel_id=1, source_target_pairs={{0,4},{4,0},{8,12},{12,8},{16,20},{20,16},{24,28},{28,24},{1,5},{5... | collective-permute-start | bytes 5505032 | tf_op jit(solution)/shard_map/ppermute | solution.py:22
  41.8 21.5 %copy-start.1 = (bf16[1,224,4096]{2,1,0:T(8,128)(2,1)S(1)}, bf16[1,224,4096]{2,1,0:T(8,128)(2,1)}, u32[]{:S(2)}) copy-start(bf16[1,224,4096]{2,1,0:T(8,128)(2,1)} %param.23) | copy-start | bytes 5505028
  43.1 20.0 %collective-permute-start.11 = (bf16[96,4096]{1,0:T(8,128)(2,1)}, bf16[96,4096]{1,0:T(8,128)(2,1)S(1)}, u32[]{:S(2)}, u32[]{:S(2)}) collective-permute-start(bf16[96,4096]{1,0:T(8,128)(2,1)} %get-tuple-element.194.refs_0_), channel_id=1, source_target_pairs={{0,8},{4,12},{8,16},{12,20},{16,24},{20,28},{24,0},{28,4},{1,9},{5... | collective-permute-start | bytes 2359304 | tf_op jit(solution)/shard_map/ppermute | solution.py:17
  44.7 18.6 %collective-permute-start.12 = (bf16[96,4096]{1,0:T(8,128)(2,1)}, bf16[96,4096]{1,0:T(8,128)(2,1)}, u32[]{:S(2)}, u32[]{:S(2)}) collective-permute-start(bf16[96,4096]{1,0:T(8,128)(2,1)} %get-tuple-element.193), channel_id=1, source_target_pairs={{0,24},{4,28},{8,0},{12,4},{16,8},{20,12},{24,16},{28,20},{1,25},{... | collective-permute-start | bytes 2359304 | tf_op jit(solution)/shard_map/ppermute | solution.py:17
  46.3 10.3 %collective-permute-start.13 = (bf16[64,1024]{1,0:T(8,128)(2,1)S(1)}, bf16[64,1024]{1,0:T(8,128)(2,1)S(1)}, u32[]{:S(2)}, u32[]{:S(2)}) collective-permute-start(bf16[64,1024]{1,0:T(8,128)(2,1)S(1)} %convolution_convert_fusion.2), channel_id=1, source_target_pairs={{0,3},{1,2},{2,1},{3,0},{4,7},{5,6},{6,5},{7,4},{8,11},{9,10},{10,... | collective-permute-start | bytes 393224 | tf_op jit(solution)/shard_map/ppermute | solution.py:27
  47.4 10.0 %collective-permute-start.14 = (bf16[64,1024]{1,0:T(8,128)(2,1)S(1)}, bf16[64,1024]{1,0:T(8,128)(2,1)}, u32[]{:S(2)}, u32[]{:S(2)}) collective-permute-start(bf16[64,1024]{1,0:T(8,128)(2,1)S(1)} %convolution_convert_fusion.2), channel_id=1, source_target_pairs={{0,2},{1,3},{2,0},{3,1},{4,6},{5,7},{6,4},{7,5},{8,10},{9,11},{10,... | collective-permute-start | bytes 393224 | tf_op jit(solution)/shard_map/ppermute | solution.py:27
  63.3 5.9 %collective-permute-start.18 = (bf16[224,4096]{1,0:T(8,128)(2,1)S(1)}, bf16[224,4096]{1,0:T(8,128)(2,1)S(1)}, u32[]{:S(2)}, u32[]{:S(2)}) collective-permute-start(bf16[224,4096]{1,0:T(8,128)(2,1)S(1)} %bitcast.35), channel_id=1, source_target_pairs={{0,4},{4,0},{8,12},{12,8},{16,20},{20,16},{24,28},{28,24},{1,5},{5... | collective-permute-start | bytes 5505032 | tf_op jit(solution)/shard_map/ppermute | solution.py:22
  63.3 5.9 %copy-start.12 = (bf16[64,4096]{1,0:T(8,128)(2,1)S(1)}, bf16[64,4096]{1,0:T(8,128)(2,1)}, u32[]{:S(2)}) copy-start(bf16[64,4096]{1,0:T(8,128)(2,1)} %copy-done.11) | copy-start | bytes 1572868
  63.3 5.9 %copy-start.10 = (bf16[64,4096]{1,0:T(8,128)(2,1)S(1)}, bf16[64,4096]{1,0:T(8,128)(2,1)}, u32[]{:S(2)}) copy-start(bf16[64,4096]{1,0:T(8,128)(2,1)} %copy-done.9) | copy-start | bytes 1572868
  65.7 21.4 %collective-permute-start.16 = (bf16[96,4096]{1,0:T(8,128)(2,1)S(1)}, bf16[96,4096]{1,0:T(8,128)(2,1)S(1)}, u32[]{:S(2)}, u32[]{:S(2)}) collective-permute-start(bf16[96,4096]{1,0:T(8,128)(2,1)S(1)} %get-tuple-element.190.refs_0_), channel_id=1, source_target_pairs={{0,8},{4,12},{8,16},{12,20},{16,24},{20,28},{24,0},{28,4},{1,9},{5... | collective-permute-start | bytes 2359304 | tf_op jit(solution)/shard_map/ppermute | solution.py:17
  67.5 19.7 %collective-permute-start.17 = (bf16[96,4096]{1,0:T(8,128)(2,1)S(1)}, bf16[96,4096]{1,0:T(8,128)(2,1)S(1)}, u32[]{:S(2)}, u32[]{:S(2)}) collective-permute-start(bf16[96,4096]{1,0:T(8,128)(2,1)S(1)} %get-tuple-element.189), channel_id=1, source_target_pairs={{0,24},{4,28},{8,0},{12,4},{16,8},{20,12},{24,16},{28,20},{1,25},{... | collective-permute-start | bytes 2359304 | tf_op jit(solution)/shard_map/ppermute | solution.py:17
  75.9 14.5 %copy-start.15 = (f32[64,4096]{1,0:T(8,128)}, f32[64,4096]{1,0:T(8,128)S(1)}, u32[]{:S(2)}) copy-start(f32[64,4096]{1,0:T(8,128)S(1)} %get-tuple-element.148) | copy-start | bytes 3145732
  87.3 13.8 %collective-permute-start.20 = (bf16[64,4096]{1,0:T(8,128)(2,1)S(1)}, bf16[64,4096]{1,0:T(8,128)(2,1)S(1)}, u32[]{:S(2)}, u32[]{:S(2)}) collective-permute-start(bf16[64,4096]{1,0:T(8,128)(2,1)S(1)} %pad_maximum_fusion.8), channel_id=1, source_target_pairs={{0,24},{4,28},{8,0},{12,4},{16,8},{20,12},{24,16},{28,20},{1,25},{... | collective-permute-start | bytes 1572872 | tf_op jit(solution)/shard_map/ppermute | solution.py:17
  90.4 14.3 %collective-permute-start.19 = (bf16[64,4096]{1,0:T(8,128)(2,1)S(1)}, bf16[64,4096]{1,0:T(8,128)(2,1)S(1)}, u32[]{:S(2)}, u32[]{:S(2)}) collective-permute-start(bf16[64,4096]{1,0:T(8,128)(2,1)S(1)} %pad_maximum_fusion.7), channel_id=1, source_target_pairs={{0,8},{4,12},{8,16},{12,20},{16,24},{20,28},{24,0},{28,4},{1,9},{5... | collective-permute-start | bytes 1572872 | tf_op jit(solution)/shard_map/ppermute | solution.py:17
  93.1 12.1 %copy-start.7 = (bf16[256,4096]{1,0:T(8,128)(2,1)}, bf16[256,4096]{1,0:T(8,128)(2,1)S(1)}, u32[]{:S(2)}) copy-start(bf16[256,4096]{1,0:T(8,128)(2,1)S(1)} %get-tuple-element.133.rows_ref) | copy-start | bytes 6291460
  104.7 16.2 %collective-permute-start.23 = (bf16[256,4096]{1,0:T(8,128)(2,1)S(1)}, bf16[256,4096]{1,0:T(8,128)(2,1)S(1)}, u32[]{:S(2)}, u32[]{:S(2)}) collective-permute-start(bf16[256,4096]{1,0:T(8,128)(2,1)S(1)} %get-tuple-element.133.rows_ref), channel_id=1, source_target_pairs={{0,4},{4,0},{8,12},{12,8},{16,20},{20,16},{24,28},{28,24},{1,5},{5... | collective-permute-start | bytes 6291464 | tf_op jit(solution)/shard_map/ppermute | solution.py:22
  104.9 15.3 %collective-permute-start.22 = (bf16[64,4096]{1,0:T(8,128)(2,1)S(1)}, bf16[64,4096]{1,0:T(8,128)(2,1)S(1)}, u32[]{:S(2)}, u32[]{:S(2)}) collective-permute-start(bf16[64,4096]{1,0:T(8,128)(2,1)S(1)} %add_convert_fusion.2), channel_id=1, source_target_pairs={{0,24},{4,28},{8,0},{12,4},{16,8},{20,12},{24,16},{28,20},{1,25},{... | collective-permute-start | bytes 1572872 | tf_op jit(solution)/shard_map/ppermute | solution.py:17
  105.2 15.7 %collective-permute-start.21 = (bf16[64,4096]{1,0:T(8,128)(2,1)S(1)}, bf16[64,4096]{1,0:T(8,128)(2,1)S(1)}, u32[]{:S(2)}, u32[]{:S(2)}) collective-permute-start(bf16[64,4096]{1,0:T(8,128)(2,1)S(1)} %add_convert_fusion.3), channel_id=1, source_target_pairs={{0,8},{4,12},{8,16},{12,20},{16,24},{20,28},{24,0},{28,4},{1,9},{5... | collective-permute-start | bytes 1572872 | tf_op jit(solution)/shard_map/ppermute | solution.py:17
  121.7 10.2 %collective-permute-start.27 = (bf16[256,4096]{1,0:T(8,128)(2,1)}, bf16[256,4096]{1,0:T(8,128)(2,1)}, u32[]{:S(2)}, u32[]{:S(2)}) collective-permute-start(bf16[256,4096]{1,0:T(8,128)(2,1)} %get-tuple-element.147.rows_ref), channel_id=1, source_target_pairs={{0,4},{4,0},{8,12},{12,8},{16,20},{20,16},{24,28},{28,24},{1,5},{5... | collective-permute-start | bytes 6291464 | tf_op jit(solution)/shard_map/ppermute | solution.py:22
  121.7 10.1 %collective-permute-start.26 = (bf16[672,256]{1,0:T(8,128)(2,1)}, bf16[672,256]{1,0:T(8,128)(2,1)S(1)}, u32[]{:S(2)}, u32[]{:S(2)}) collective-permute-start(bf16[672,256]{1,0:T(8,128)(2,1)} %copy-done.18), channel_id=1, source_target_pairs={{0,4},{4,0},{8,12},{12,8},{16,20},{20,16},{24,28},{28,24},{1,5},{5... | collective-permute-start | bytes 1032200 | tf_op jit(solution)/shard_map/ppermute | solution.py:22
  122.2 9.6 %collective-permute-start.24 = (bf16[32,4096]{1,0:T(8,128)(2,1)}, bf16[32,4096]{1,0:T(8,128)(2,1)S(1)}, u32[]{:S(2)}, u32[]{:S(2)}) collective-permute-start(bf16[32,4096]{1,0:T(8,128)(2,1)} %copy-done.20), channel_id=1, source_target_pairs={{0,8},{4,12},{8,16},{12,20},{16,24},{20,28},{24,0},{28,4},{1,9},{5... | collective-permute-start | bytes 786440 | tf_op jit(solution)/shard_map/ppermute | solution.py:17
  122.8 9.1 %collective-permute-start.25 = (bf16[32,4096]{1,0:T(8,128)(2,1)}, bf16[32,4096]{1,0:T(8,128)(2,1)S(1)}, u32[]{:S(2)}, u32[]{:S(2)}) collective-permute-start(bf16[32,4096]{1,0:T(8,128)(2,1)} %copy-done.19), channel_id=1, source_target_pairs={{0,24},{4,28},{8,0},{12,4},{16,8},{20,12},{24,16},{28,20},{1,25},{... | collective-permute-start | bytes 786440 | tf_op jit(solution)/shard_map/ppermute | solution.py:17
  127.2 11.5 %copy-start.24 = (s32[1,128,2]{1,2,0:T(2,128)S(1)}, s32[1,128,2]{1,2,0:T(2,128)}, u32[]{:S(2)}) copy-start(s32[1,128,2]{1,2,0:T(2,128)} %param.13) | copy-start | bytes 3076
  127.2 11.5 %copy-start.25 = (f32[1,128,2]{1,2,0:T(2,128)S(1)}, f32[1,128,2]{1,2,0:T(2,128)}, u32[]{:S(2)}) copy-start(f32[1,128,2]{1,2,0:T(2,128)} %param.14) | copy-start | bytes 3076
  127.3 11.6 %copy-start.8 = (bf16[256,4096]{1,0:T(8,128)(2,1)S(1)}, bf16[256,4096]{1,0:T(8,128)(2,1)}, u32[]{:S(2)}) copy-start(bf16[256,4096]{1,0:T(8,128)(2,1)} %copy-done.7) | copy-start | bytes 6291460
  132.0 14.2 %collective-permute-start.29 = (bf16[64,4096]{1,0:T(8,128)(2,1)S(1)}, bf16[64,4096]{1,0:T(8,128)(2,1)S(1)}, u32[]{:S(2)}, u32[]{:S(2)}) collective-permute-start(bf16[64,4096]{1,0:T(8,128)(2,1)S(1)} %add_convert_fusion), channel_id=1, source_target_pairs={{0,24},{4,28},{8,0},{12,4},{16,8},{20,12},{24,16},{28,20},{1,25},{... | collective-permute-start | bytes 1572872 | tf_op jit(solution)/shard_map/ppermute | solution.py:17
  135.1 13.7 %collective-permute-start.28 = (bf16[64,4096]{1,0:T(8,128)(2,1)S(1)}, bf16[64,4096]{1,0:T(8,128)(2,1)S(1)}, u32[]{:S(2)}, u32[]{:S(2)}) collective-permute-start(bf16[64,4096]{1,0:T(8,128)(2,1)S(1)} %add_convert_fusion.1), channel_id=1, source_target_pairs={{0,8},{4,12},{8,16},{12,20},{16,24},{20,28},{24,0},{28,4},{1,9},{5... | collective-permute-start | bytes 1572872 | tf_op jit(solution)/shard_map/ppermute | solution.py:17
  135.1 10.3 %collective-permute-start.30 = (bf16[64,1024]{1,0:T(8,128)(2,1)S(1)}, bf16[64,1024]{1,0:T(8,128)(2,1)S(1)}, u32[]{:S(2)}, u32[]{:S(2)}) collective-permute-start(bf16[64,1024]{1,0:T(8,128)(2,1)S(1)} %get-tuple-element.156), channel_id=1, source_target_pairs={{0,3},{1,2},{2,1},{3,0},{4,7},{5,6},{6,5},{7,4},{8,11},{9,10},{10,... | collective-permute-start | bytes 393224 | tf_op jit(solution)/shard_map/ppermute | solution.py:27
  136.3 9.9 %collective-permute-start.31 = (bf16[64,1024]{1,0:T(8,128)(2,1)S(1)}, bf16[64,1024]{1,0:T(8,128)(2,1)S(1)}, u32[]{:S(2)}, u32[]{:S(2)}) collective-permute-start(bf16[64,1024]{1,0:T(8,128)(2,1)S(1)} %get-tuple-element.157), channel_id=1, source_target_pairs={{0,2},{1,3},{2,0},{3,1},{4,6},{5,7},{6,4},{7,5},{8,10},{9,11},{10,... | collective-permute-start | bytes 393224 | tf_op jit(solution)/shard_map/ppermute | solution.py:27
  137.8 8.4 %collective-permute-start.32 = (bf16[64,1024]{1,0:T(8,128)(2,1)S(1)}, bf16[64,1024]{1,0:T(8,128)(2,1)S(1)}, u32[]{:S(2)}, u32[]{:S(2)}) collective-permute-start(bf16[64,1024]{1,0:T(8,128)(2,1)S(1)} %get-tuple-element.158), channel_id=1, source_target_pairs={{0,1},{1,0},{2,3},{3,2},{4,5},{5,4},{6,7},{7,6},{8,9},{9,8},{10,11... | collective-permute-start | bytes 393224 | tf_op jit(solution)/shard_map/ppermute | solution.py:27
  138.9 9.8 %copy-start.14 = (f32[64,4096]{1,0:T(8,128)S(1)}, f32[64,4096]{1,0:T(8,128)}, u32[]{:S(2)}) copy-start(f32[64,4096]{1,0:T(8,128)} %copy-done.13) | copy-start | bytes 3145732
  148.9 11.3 %collective-permute-start.33 = (bf16[64,1024]{1,0:T(8,128)(2,1)S(1)}, bf16[64,1024]{1,0:T(8,128)(2,1)S(1)}, u32[]{:S(2)}, u32[]{:S(2)}) collective-permute-start(bf16[64,1024]{1,0:T(8,128)(2,1)S(1)} %get-tuple-element.185), channel_id=1, source_target_pairs={{0,3},{1,2},{2,1},{3,0},{4,7},{5,6},{6,5},{7,4},{8,11},{9,10},{10,... | collective-permute-start | bytes 393224 | tf_op jit(solution)/shard_map/ppermute | solution.py:27
  150.1 10.1 %collective-permute-start.34 = (bf16[64,1024]{1,0:T(8,128)(2,1)S(1)}, bf16[64,1024]{1,0:T(8,128)(2,1)S(1)}, u32[]{:S(2)}, u32[]{:S(2)}) collective-permute-start(bf16[64,1024]{1,0:T(8,128)(2,1)S(1)} %get-tuple-element.184), channel_id=1, source_target_pairs={{0,2},{1,3},{2,0},{3,1},{4,6},{5,7},{6,4},{7,5},{8,10},{9,11},{10,... | collective-permute-start | bytes 393224 | tf_op jit(solution)/shard_map/ppermute | solution.py:27
  151.8 8.4 %collective-permute-start.35 = (bf16[64,1024]{1,0:T(8,128)(2,1)S(1)}, bf16[64,1024]{1,0:T(8,128)(2,1)S(1)}, u32[]{:S(2)}, u32[]{:S(2)}) collective-permute-start(bf16[64,1024]{1,0:T(8,128)(2,1)S(1)} %get-tuple-element.183), channel_id=1, source_target_pairs={{0,1},{1,0},{2,3},{3,2},{4,5},{5,4},{6,7},{7,6},{8,9},{9,8},{10,11... | collective-permute-start | bytes 393224 | tf_op jit(solution)/shard_map/ppermute | solution.py:27
  (14 other events, 25.7 us)
